TPU v7x, 256 devices: a whole 4x4x8 slice. The times are simulated.
256 devices in a mesh: orb: 32 (over x, y, core), grid: 8 (over z).
Axes of the slice: x: 4, y: 4, z: 8, core: 2. Of those that a mesh axis runs over, the one named last changes fastest.
Arguments:
- orbitals: bfloat16 [256, 64, 4096], P('orb', 'grid'), may hold values from -6 to 10
- pair_list: int32 [2, 512], P(None, 'orb'), may hold values from -1 to 255, as said below
- box_anchor: int32 [2, 256], replicated, may hold values from 0 to 16
Outputs:
- potentials: bfloat16 [256, 64, 4096], P('orb', 'grid')
- energies: float32 [256], P('orb')
Inputs may be any that keep to these rules, and one draw needn't show every extreme that they name: `pair_list`: columns 16 * d to 16 * (d + 1) - 1 belong to index d of orb: row 0 names an orbital of that index (8 * d to 8 * (d + 1) - 1), row 1 an orbital of another index or -1 for an empty entry. Empty entries stand at the end of an index's columns; every index has at least 12 live entries and some index none empty. At most 2 live entries of one index name orbitals of one other index, and every index has, for at least one other index, exactly 2 live entries naming its orbitals.
All inputs are finite; a program needn't handle non-finite values.
Results may differ from a plain program's by a relative error of at most 0.0047.
Values may be sent and summed in bfloat16 or wider, within the bound.
No kernel may reach another device: no remote copies, remote signals or barrier semaphores. Data moves between devices by JAX's collectives and lax.ppermute only.
A program may use at most 192 MiB of HBM per device.

v0:
```python
import functools

import jax
import jax.numpy as jnp
import ml_dtypes
import numpy as np
from jax import lax
from jax.experimental import pallas as pl
from jax.experimental.pallas import tpu as pltpu
from jax.sharding import PartitionSpec as P

BOX = 64
LANES = 128
TILES = BOX * BOX // LANES
PLANES = 8
ROWS = TILES * PLANES
GRID = 8
PAIRS = GRID // 2
COMBOS = [(p, q) for q in range(PAIRS) for p in range(q)]
UP, DOWN, MIDDLE, CARRY, PAST_UP, PAST_DOWN, INSIDE, ACROSS = 0, 8, 16, 24, 27, 28, 29, 30
CHUNK = 8
ORB_DEV = 8
PAD = 10
MU2 = 0.02
BF16 = jnp.bfloat16
F32 = jnp.float32
VMEM_LIMIT = 40 * 1024 * 1024


def sine64():
    steps = np.arange(1, BOX + 1, dtype=np.float64)
    return np.sqrt(2.0 / (BOX + 1)) * np.sin(np.pi * steps[:, None] * steps[None, :] / (BOX + 1))


def high_low(table):
    high = table.astype(np.float32).astype(ml_dtypes.bfloat16)
    rest = table - high.astype(np.float64)
    return high, rest.astype(np.float32).astype(ml_dtypes.bfloat16)


def sine_factors():
    sine = sine64()
    zero = np.zeros((BOX, BOX))
    high, low = high_low(np.block([[sine, zero], [zero, sine]]))
    y_right = np.concatenate(
        [np.concatenate([high, low], 1), np.concatenate([high, np.zeros_like(high)], 1)], 0
    )
    half = 2 * np.arange(TILES)
    rows = []
    for h in range(2):
        rows.append(np.concatenate([sine[np.ix_(half + h, half + h)], sine[np.ix_(half + h, half + 1 - h)]], 1))
    high, low = high_low(np.concatenate(rows, 0))
    return jnp.asarray(y_right), jnp.asarray(np.concatenate([high, high, low], 1))


def z_factors(grid_index):
    steps = jnp.arange(1, BOX + 1).astype(F32)
    eigen = 2.0 - 2.0 * jnp.cos(jnp.pi * steps / (BOX + 1))
    s = (eigen[:, None] + eigen[None, :] + MU2).reshape(TILES, LANES)[None]
    theta = jnp.log(1.0 + 0.5 * s + jnp.sqrt(s + 0.25 * s * s))

    def number(n):
        return jnp.asarray(n).reshape(-1).astype(F32)[:, None, None]

    def rest(n):
        return 1.0 - jnp.exp(-2.0 * theta * number(n))

    def fall(n):
        return jnp.exp(-theta * number(n))

    z = grid_index * PLANES + jnp.arange(PLANES)
    up = fall(1) * rest(z) / rest(z + 1)
    down = fall(1) * rest(63 - z) / rest(64 - z)
    scale = MU2 / (rest(1) * rest(65))
    middle = scale * fall(1) * rest(z + 1) * rest(64 - z)
    pair = grid_index // 2
    e = jnp.arange(1, PAIRS)
    other = (pair - e) % PAIRS
    below = e <= pair
    away = jnp.where(below, 8 * grid_index - 16 * other - 16, 16 * other - 8 * grid_index - 8)
    first = jnp.where(below, 16 * other + 16, 64 - 16 * other)
    last = jnp.where(below, 8 * grid_index, 56 - 8 * grid_index)
    carry = fall(away) * rest(first) / rest(last)
    edge = 16 * pair + 8
    past_up = fall(8) * rest(edge) / rest(edge + 8)
    past_down = fall(8) * rest(64 - edge) / rest(72 - edge)
    inside = scale * fall(2) * rest(edge) * rest(64 - edge)
    m1 = jnp.stack([(pair - p) % PAIRS for p, _ in COMBOS])
    m2 = jnp.stack([(pair - q) % PAIRS for _, q in COMBOS])
    low, high = jnp.minimum(m1, m2), jnp.maximum(m1, m2)
    across = scale * fall(16 * (high - low) - 14) * rest(16 * low + 16) * rest(64 - 16 * high)
    return jnp.concatenate([up, down, middle, carry, past_up, past_down, inside, across], 0)


def lane_iota(rows):
    return lax.broadcasted_iota(jnp.int32, (rows, LANES), 1)


def split(value):
    high = value.astype(BF16)
    return high, (value - high.astype(F32)).astype(BF16)


def dot(left, right):
    return jnp.dot(left, right, preferred_element_type=F32)


def times_y(value, y_right):
    high, low = split(value)
    both = dot(jnp.concatenate([high, low], axis=1), y_right)
    return both[:, :LANES] + both[:, LANES:]


def times_x(planes, x_left):
    value = jnp.concatenate(planes, axis=1)
    other = jnp.concatenate([pltpu.roll(p, BOX, 1) for p in planes], axis=1)
    high, low = split(jnp.concatenate([value, other], axis=0))
    both = dot(x_left, jnp.concatenate([high, low, high], axis=0))
    first = lane_iota(TILES) < BOX
    out = []
    for z in range(PLANES):
        tile = both[:, LANES * z : LANES * (z + 1)]
        out.append(jnp.where(first, tile[:TILES], tile[TILES:]))
    return out


def shifted(value, step_x, step_y, buffer):
    buffer[PAD * 8 : PAD * 8 + ROWS, :] = value
    flat = step_x * BOX + step_y
    tiles = flat >> 7
    lanes = flat & 127
    start = pl.multiple_of((tiles + PAD) * 8, 8)
    window = buffer[pl.ds(start, ROWS + 8), :]
    window = pltpu.roll(window, (LANES - lanes) & 127, 1)
    lane = lane_iota(ROWS)
    moved = jnp.where(lane < LANES - lanes, window[:ROWS], window[8:])
    y_new = (lane & (BOX - 1)) + step_y
    return jnp.where((y_new >= 0) & (y_new < BOX), moved, 0.0)


def clear_margins(buffer):
    zero = jnp.zeros((PAD * 8, LANES), F32)
    buffer[: PAD * 8, :] = zero
    buffer[PAD * 8 + ROWS :, :] = zero


def column_sums(value):
    return jnp.sum(value, axis=0, keepdims=True)


def forward(rho, tables, held, coeffs, ends, message, energy, n):
    y_right, x_left, z_table = tables
    held[...] = times_y(rho, y_right[...])
    planes = times_x([held[pl.ds(z, TILES, stride=PLANES), :] for z in range(PLANES)], x_left[...])
    for z in range(PLANES):
        coeffs[n, TILES * z : TILES * (z + 1), :] = planes[z]
    above = jnp.zeros((TILES, LANES), F32)
    product = jnp.zeros((TILES, LANES), F32)
    for z in range(PLANES):
        above = z_table[UP + z] * above + planes[z]
        if energy is not None:
            product += z_table[MIDDLE + z] * planes[z] * (2.0 * above - planes[z])
    below = planes[PLANES - 1]
    for z in range(PLANES - 2, -1, -1):
        below = z_table[DOWN + z] * below + planes[z]
    both = jnp.concatenate([above, below], axis=0)
    ends[n] = both
    message[n] = both.astype(BF16)
    if energy is not None:
        energy[n : n + 1, :] = column_sums(product)


def pack_energy(energy, message):
    high = energy.astype(BF16).astype(F32)
    message[CHUNK, :16, :] = jnp.concatenate([high, energy - high], axis=0).astype(BF16)
    message[CHUNK, 16:, :] = jnp.zeros((2 * TILES - 16, LANES), BF16)


def unpack_energy(message):
    both = message[CHUNK, :16, :].astype(F32)
    return both[:8] + both[8:]


def halves(message, n):
    both = message[n].astype(F32)
    return both[:TILES], both[TILES:]


def between_pairs(pair, ends, z_table):
    product = jnp.zeros((TILES, LANES), F32)
    for i, (p, q) in enumerate(COMBOS):
        p_low = ((pair - p) & (PAIRS - 1)) < ((pair - q) & (PAIRS - 1))
        low = jnp.where(p_low, ends[p][0], ends[q][0])
        high = jnp.where(p_low, ends[q][1], ends[p][1])
        product += z_table[ACROSS + i] * low * high
    return 2.0 * column_sums(product)


def inverse(grid, near, sums, coeffs, tables, held, n):
    y_right, x_left, z_table = tables
    near_up, near_down = halves(near, n)
    upper = (grid & 1) == 1
    from_below = jnp.where(upper, near_up, 0.0)
    from_above = jnp.where(upper, 0.0, near_down)
    for e in range(1, PAIRS):
        below = e <= (grid >> 1)
        term = z_table[CARRY + e - 1] * sums[e - 1]
        from_below += jnp.where(below, term, 0.0)
        from_above += jnp.where(below, 0.0, term)
    planes = [coeffs[n, TILES * z : TILES * (z + 1), :] for z in range(PLANES)]
    ups = []
    for z in range(PLANES):
        from_below = z_table[UP + z] * from_below + planes[z]
        ups.append(from_below)
    solved = [None] * PLANES
    for z in range(PLANES - 1, -1, -1):
        carried = z_table[DOWN + z] * from_above
        solved[z] = z_table[MIDDLE + z] * (ups[z] + carried)
        from_above = planes[z] + carried
    full = times_y(jnp.concatenate(times_x(solved, x_left[...]), axis=0), y_right[...])
    for z in range(PLANES):
        held[pl.ds(z, TILES, stride=PLANES), :] = full[TILES * z : TILES * (z + 1)]
    return held[...]


def pair_scalars(perm, pairs, anchor, n):
    entry = perm[n]
    safe = jnp.maximum(entry, 0)
    owner = pairs[0, safe]
    mate = jnp.maximum(pairs[1, safe], 0)
    step_x = anchor[0, owner] - anchor[0, mate]
    step_y = anchor[1, owner] - anchor[1, mate]
    return entry >= 0, owner & (ORB_DEV - 1), mate >> 3, step_x, step_y


def plan_kernel(pairs, ask, perm, count):
    devices = ask.shape[0]
    entries = 2 * CHUNK
    for t in range(devices + 1):
        count[t] = 0
    for p in range(entries):
        perm[p] = -1
    mates = [pairs[1, p] for p in range(entries)]
    targets = [jnp.where(m >= 0, m >> 3, devices) for m in mates]
    for t in targets:
        count[t] = count[t] + 1
    spots = []
    used = [jnp.int32(0), jnp.int32(0)]
    for p in range(entries):
        seen = count[targets[p]]
        live = mates[p] >= 0
        first, second = live & (seen == 2), live & (seen == 3)
        count[targets[p]] = jnp.where(first, 3, seen)
        spots.append(jnp.where(first, used[0], jnp.where(second, CHUNK + used[1], -1)))
        used[0] += first.astype(jnp.int32)
        used[1] += second.astype(jnp.int32)
    row = lax.broadcasted_iota(jnp.int32, (devices, LANES), 0)
    lane = lax.broadcasted_iota(jnp.int32, (devices, LANES), 1)
    asks = jnp.full((devices, LANES), -1, jnp.int32)
    for p in range(entries):
        live = mates[p] >= 0
        single = live & (spots[p] < 0)
        early = single & (used[0] < CHUNK)
        late = single & (used[0] >= CHUNK)
        spot = jnp.where(early, used[0], jnp.where(late, CHUNK + used[1], spots[p]))
        used[0] += early.astype(jnp.int32)
        used[1] += late.astype(jnp.int32)

        @pl.when(live)
        def _():
            perm[spot] = p

        chunk = jnp.where(spot >= CHUNK, 1, 0)
        here = (row == jnp.where(live, targets[p], -1)) & (lane == chunk)
        asks = jnp.where(here, mates[p] & (ORB_DEV - 1), asks)
    ask[:, 0, :] = asks


def rows_kernel(orb, orb_rows):
    for n in range(ORB_DEV):
        wide = orb[n].astype(F32)
        box = jnp.concatenate([wide[:, LANES * t : LANES * (t + 1)] for t in range(TILES)], axis=0)
        orb_rows[n] = box.astype(BF16)


def base_forward_kernel(orb_rows, y_right, x_left, z_table, coeffs, ends, message, *held):
    for n in range(ORB_DEV):
        box = orb_rows[n].astype(F32)
        forward(box * box, (y_right, x_left, z_table), held[n], coeffs, ends, message, None, n)


def outbox_kernel(chunk, asked, orb_rows, out):
    def step(d, carry):
        out[d, :ROWS, :] = orb_rows[jnp.maximum(asked[d, chunk], 0)]
        return carry

    lax.fori_loop(0, out.shape[0], step, 0)


def pair_forward_kernel(whole, perm, pairs, anchor, orb_rows, fetched, y_right, x_left, z_table, *refs):
    moved_out, coeffs, ends, message, *refs = refs
    energy, *refs = refs if whole else (None, *refs)
    buffers, held = refs[:CHUNK], refs[CHUNK:]
    for n in range(CHUNK):
        clear_margins(buffers[n])
    for n in range(CHUNK):
        _, owner, source, step_x, step_y = pair_scalars(perm, pairs, anchor, n)
        moved = shifted(fetched[source].astype(F32), step_x, step_y, buffers[n])
        moved_out[n] = moved.astype(BF16)
        rho = orb_rows[owner].astype(F32) * moved
        forward(rho, (y_right, x_left, z_table), held[n], coeffs, ends, message, energy, n)
    if whole:
        pack_energy(energy[...], message)


def pair_up(upper, ends, near, z_table, n):
    near_up, near_down = halves(near, n)
    mine = ends[n]
    mine_up, mine_down = mine[:TILES], mine[TILES:]
    low_up = jnp.where(upper, near_up, mine_up)
    high_up = jnp.where(upper, mine_up, near_up)
    low_down = jnp.where(upper, near_down, mine_down)
    high_down = jnp.where(upper, mine_down, near_down)
    up = z_table[PAST_UP] * low_up + high_up
    down = low_down + z_table[PAST_DOWN] * high_down
    return up, down, low_up * high_down


def pair_up_kernel(grid, ends, near, z_table, *outs):
    pair = grid[0] >> 1
    for n in range(CHUNK):
        up, down, _ = pair_up((grid[0] & 1) == 1, ends, near, z_table, n)
        up, down = up.astype(BF16), down.astype(BF16)
        for e in range(1, PAIRS):
            outs[e - 1][n] = jnp.where(pair + e < PAIRS, up, down)


def pair_up_whole_kernel(grid, ends, energy, near, z_table, message):
    rows = lax.broadcasted_iota(jnp.int32, (CHUNK, LANES), 0)
    total = energy[...] + unpack_energy(near)
    for n in range(CHUNK):
        up, down, product = pair_up((grid[0] & 1) == 1, ends, near, z_table, n)
        message[n, :TILES, :] = up.astype(BF16)
        message[n, TILES:, :] = down.astype(BF16)
        total += jnp.where(rows == n, 2.0 * column_sums(z_table[INSIDE] * product), 0.0)
    pack_energy(total, message)


def base_inverse_kernel(grid, near, *refs):
    sums, refs = refs[: PAIRS - 1], refs[PAIRS - 1 :]
    coeffs, orb_rows, y_right, x_left, z_table, total, *held = refs
    for n in range(ORB_DEV):
        here = [block[n].astype(F32) for block in sums]
        potential = inverse(grid[0], near, here, coeffs, (y_right, x_left, z_table), held[n], n)
        total[n] = orb_rows[n].astype(F32) * potential


def pair_inverse_kernel(whole, grid, perm, pairs, anchor, near, *refs):
    count = PAIRS if whole else PAIRS - 1
    blocks, refs = refs[:count], refs[count:]
    coeffs, orb_rows, moved, y_right, x_left, z_table, total_in, total, outbox, *refs = refs
    buffers, held, backs = refs[:CHUNK], refs[CHUNK : 2 * CHUNK], refs[2 * CHUNK]
    pair = grid[0] >> 1
    for n in range(CHUNK):
        clear_margins(buffers[n])
    total[...] = total_in[...]
    if whole:
        within = sum(unpack_energy(block) for block in blocks)
        rows = lax.broadcasted_iota(jnp.int32, (16, LANES), 0)
    for n in range(CHUNK):
        _, owner, _, step_x, step_y = pair_scalars(perm, pairs, anchor, n)
        if whole:
            ends = [halves(block, n) for block in blocks]
            here = [jnp.where(e <= pair, ends[e][0], ends[e][1]) for e in range(1, PAIRS)]
        else:
            here = [block[n].astype(F32) for block in blocks]
        potential = inverse(grid[0], near, here, coeffs, (y_right, x_left, z_table), held[n], n)
        back = shifted(orb_rows[owner].astype(F32) * potential, -step_x, -step_y, buffers[n])
        backs[n, :ROWS, :] = back.astype(BF16)
        if whole:
            value = within[n : n + 1] + between_pairs(pair, ends, z_table)
            high = value.astype(BF16).astype(F32)
            tail = jnp.where(rows == 0, high, jnp.where(rows == 1, value - high, 0.0))
            backs[n, ROWS:, :] = tail.astype(BF16)
    for n in range(CHUNK):
        live, owner, source, _, _ = pair_scalars(perm, pairs, anchor, n)

        @pl.when(live)
        def _():
            outbox[source] = backs[n]
            total[owner] += moved[n].astype(F32) * held[n][...]


def each_arrived(chunk, asked, arrived, action):
    def step(d, carry):
        which = asked[d, chunk]

        @pl.when(which >= 0)
        def _():
            action(which, d)

        return carry

    lax.fori_loop(0, arrived.shape[0], step, 0)


def add_kernel(chunk, asked, arrived, orb_rows, total_in, total, energy):
    total[...] = total_in[...]

    def action(which, d):
        total[which] += arrived[d].astype(F32)

    each_arrived(chunk, asked, arrived, action)
    for n in range(ORB_DEV):
        energy[n : n + 1, :] = column_sums(orb_rows[n].astype(F32) * total[n])


def finish_kernel(chunk, asked, arrived, total_in, energy_in, out, energy_out, total, energy):
    total[...] = total_in[...]
    energy[...] = energy_in[...]

    def action(which, d):
        total[which] += arrived[d, :ROWS, :].astype(F32)
        energy[pl.ds(which, 1), :] += column_sums(arrived[d, ROWS:, :].astype(F32))

    each_arrived(chunk, asked, arrived, action)
    for n in range(ORB_DEV):
        box = total[n]
        out[n] = jnp.concatenate([box[8 * t : 8 * t + 8] for t in range(TILES)], axis=1).astype(BF16)
        energy_out[n] = jnp.sum(energy[n : n + 1, :])


VMEM = pl.BlockSpec(memory_space=pltpu.VMEM)
SMEM = pl.BlockSpec(memory_space=pltpu.SMEM)
HELD = [pltpu.VMEM((ROWS, LANES), F32)] * CHUNK
SHIFT_BUFFERS = [pltpu.VMEM(((2 * PAD + TILES) * 8, LANES), F32)] * CHUNK
MESSAGE = jax.ShapeDtypeStruct((CHUNK, 2 * TILES, LANES), BF16)
MESSAGE_WHOLE = jax.ShapeDtypeStruct((CHUNK + 1, 2 * TILES, LANES), BF16)
SUMS = [jax.ShapeDtypeStruct((CHUNK, TILES, LANES), BF16)] * (PAIRS - 1)
ENDS = jax.ShapeDtypeStruct((CHUNK, 2 * TILES, LANES), F32)
BOXES = jax.ShapeDtypeStruct((CHUNK, ROWS, LANES), BF16)
TOTALS = jax.ShapeDtypeStruct((ORB_DEV, ROWS, LANES), F32)
ENERGY = jax.ShapeDtypeStruct((CHUNK, LANES), F32)


def call(kernel, out_shape, in_specs, scratch, name, micros, out_specs=None, aliases=None):
    return pl.pallas_call(
        kernel,
        out_shape=out_shape,
        in_specs=in_specs,
        out_specs=out_specs if out_specs is not None else jax.tree.map(lambda _: VMEM, out_shape),
        scratch_shapes=scratch,
        input_output_aliases=aliases or {},
        name=name,
        cost_estimate=pl.CostEstimate(flops=0, bytes_accessed=int(micros * 3.0e6), transcendentals=0),
        compiler_params=pltpu.CompilerParams(vmem_limit_bytes=VMEM_LIMIT),
    )


def local(orbitals, pair_list, box_anchor):
    devices = lax.axis_size("orb")
    grid_index = lax.axis_index("grid")
    grid = grid_index.astype(jnp.int32).reshape(1)

    ask, perm = call(
        plan_kernel,
        [
            jax.ShapeDtypeStruct((devices, 1, LANES), jnp.int32),
            jax.ShapeDtypeStruct((2 * CHUNK,), jnp.int32),
        ],
        [SMEM],
        [pltpu.SMEM((devices + 1,), jnp.int32)],
        "plan",
        2,
        out_specs=[VMEM, SMEM],
    )(pair_list)
    asked = lax.all_to_all(ask, "orb", split_axis=0, concat_axis=0, tiled=True).reshape(devices, LANES)

    y_right, x_left = sine_factors()
    z_table = z_factors(grid_index)
    tables = (y_right, x_left, z_table)

    def to_pairs(sums):
        out = [None] * (PAIRS - 1)
        for e in range(1, PAIRS):
            out[e - 1] = lax.ppermute(sums[e - 1], "grid", [(i, (i + 2 * e) % GRID) for i in range(GRID)])
        return out

    def from_grid(ends, message, energy=None):
        near = lax.ppermute(message, "grid", [(i, i ^ 1) for i in range(GRID)])
        if energy is None:
            sums = call(pair_up_kernel, SUMS, [SMEM] + [VMEM] * 3, [], "pair_up", 1)(grid, ends, near, z_table)
            return near, *to_pairs(sums)
        here = call(pair_up_whole_kernel, MESSAGE_WHOLE, [SMEM] + [VMEM] * 4, [], "pair_up_whole", 1)(
            grid, ends, energy, near, z_table
        )
        return near, here, *to_pairs([here] * (PAIRS - 1))

    orb_rows = call(rows_kernel, BOXES, [VMEM], [], "rows", 1)(orbitals)

    def outbox(c):
        shape = jax.ShapeDtypeStruct((devices, ROWS, LANES), BF16)
        return call(functools.partial(outbox_kernel, c), shape, [SMEM, VMEM], [], "outbox", 2)(asked, orb_rows)

    box_a, box_b = outbox(0), outbox(1)
    fetched_a = lax.all_to_all(box_a, "orb", split_axis=0, concat_axis=0, tiled=True)
    base_rows, _ = lax.optimization_barrier((orb_rows, box_a))
    coeffs, *ends = call(
        base_forward_kernel, [TOTALS, ENDS, MESSAGE], [VMEM] * 4, HELD, "base_forward", 3
    )(base_rows, *tables)
    total = call(
        base_inverse_kernel, TOTALS, [SMEM] + [VMEM] * (PAIRS + 5), HELD, "base_inverse", 3
    )(grid, *from_grid(*ends), coeffs, orb_rows, *tables)
    fetched_a, box_b, total = lax.optimization_barrier((fetched_a, box_b, total))
    fetched_b = lax.all_to_all(box_b, "orb", split_axis=0, concat_axis=0, tiled=True)

    def pair_terms(c, fetched, total):
        whole = c == 1
        here = perm[CHUNK * c : CHUNK * (c + 1)]
        moved, coeffs, *ends = call(
            functools.partial(pair_forward_kernel, whole),
            [BOXES, TOTALS, ENDS] + ([MESSAGE_WHOLE, ENERGY] if whole else [MESSAGE]),
            [SMEM] * 3 + [VMEM] * 5,
            SHIFT_BUFFERS + HELD,
            "pair_forward",
            4,
        )(here, pair_list, box_anchor, orb_rows, fetched, *tables)
        blocks = from_grid(*ends)
        rows = ROWS + 16 if whole else ROWS
        return call(
            functools.partial(pair_inverse_kernel, whole),
            [TOTALS, jax.ShapeDtypeStruct((devices, rows, LANES), BF16)],
            [SMEM] * 4 + [VMEM] * (len(blocks) + 7),
            SHIFT_BUFFERS + HELD + [pltpu.VMEM((CHUNK, rows, LANES), BF16)],
            "pair_inverse",
            5,
            aliases={len(blocks) + 10: 0},
        )(grid, here, pair_list, box_anchor, *blocks, coeffs, orb_rows, moved, *tables, total)

    total, back = pair_terms(0, fetched_a, total)
    back, fetched_b = lax.optimization_barrier((back, fetched_b))
    arrived_a = lax.all_to_all(back, "orb", split_axis=0, concat_axis=0, tiled=True)
    total, back = pair_terms(1, fetched_b, total)
    back, arrived_a = lax.optimization_barrier((back, arrived_a))
    arrived_b = lax.all_to_all(back, "orb", split_axis=0, concat_axis=0, tiled=True)
    total, energy = call(
        functools.partial(add_kernel, 0), [TOTALS, ENERGY], [SMEM] + [VMEM] * 3, [], "add", 2, aliases={3: 0}
    )(asked, arrived_a, orb_rows, total)
    energy = lax.psum(energy, "grid")
    total, energy, arrived_b = lax.optimization_barrier((total, energy, arrived_b))
    return call(
        functools.partial(finish_kernel, 1),
        [jax.ShapeDtypeStruct(orbitals.shape, BF16), jax.ShapeDtypeStruct((ORB_DEV,), F32)],
        [SMEM, VMEM, VMEM, VMEM],
        [pltpu.VMEM(TOTALS.shape, F32), pltpu.VMEM(ENERGY.shape, F32)],
        "finish",
        3,
        out_specs=[VMEM, SMEM],
    )(asked, arrived_b, total, energy)


def solution(mesh):
    return jax.shard_map(
        local,
        mesh=mesh,
        in_specs=(P("orb", "grid", None), P(None, "orb"), P()),
        out_specs=(P("orb", "grid", None), P("orb")),
        check_vma=False,
    )
```

profile of v0, /device:TPU:1, one launch (start us, length us, event | category | flops | bytes accessed | tf_op | source)
XLA Modules:
  0.0 170.5 jit_solution(15736629184580527102)
XLA Ops:
  0.6 0.7 copy-done.7
  1.3 1.5 plan.1
  2.8 8.6 %all-to-all-start = ((s32[32,1,128]{2,1,0:T(1,128)}), s32[32,1,128]{2,1,0:T(1,128)S(1)}, u32[]{:S(2)}, u32[]{:S(2)}) async-start(s32[32,1,128]{2,1,0:T(1,128)} %get-tuple-element.39), calls=%async_computation | async-start | bytes 32768 | tf_op jit(solution)/shard_map/all_to_all | solution.py:477
  12.3 1.0 copy-done.5
  13.4 4.9 %all-to-all-done = s32[32,1,128]{2,1,0:T(1,128)S(1)} async-done(((s32[32,1,128]{2,1,0:T(1,128)}), s32[32,1,128]{2,1,0:T(1,128)S(1)}, u32[]{:S(2)}, u32[]{:S(2)}) %all-to-all-start) | async-done | bytes 16416 | tf_op jit(solution)/shard_map/all_to_all | solution.py:477
  18.3 2.5 %outbox.2 = bf16[32,256,128]{2,1,0:T(8,128)(2,1)} custom-call(s32[32,128]{1,0:T(8,128)S(1)} %bitcast.6, bf16[8,256,128]{2,1,0:T(8,128)(2,1)S(1)} %rows.1.orb_rows.refs_4_.refs_5_), custom_call_target="tpu_custom_call" | custom-call | bytes 6000000 | tf_op jit(solution)/shard_map/outbox/pallas_call | solution.py:503
  20.8 5.1 %all-to-all-start.1 = ((bf16[32,256,128]{2,1,0:T(8,128)(2,1)}), bf16[32,256,128]{2,1,0:T(8,128)(2,1)}, u32[]{:S(2)}, u32[]{:S(2)}) async-start(bf16[32,256,128]{2,1,0:T(8,128)(2,1)} %outbox.2), calls=%async_computation.1 | async-start | bytes 4194304 | tf_op jit(solution)/shard_map/all_to_all | solution.py:506
  26.1 0.1 divide_dynamic-update-slice_fusion.1
  26.2 0.1 divide_dynamic-update-slice_fusion
  26.3 0.1 multiply_dynamic-update-slice_fusion
  26.7 0.1 multiply_dynamic-update-slice_fusion.1.z_table.refs_7_.refs_8_.refs_9_
  26.9 3.2 %base_forward.1 = (f32[8,256,128]{2,1,0:T(8,128)S(1)}, f32[8,64,128]{2,1,0:T(8,128)S(1)}, bf16[8,64,128]{2,1,0:T(8,128)(2,1)S(1)}) custom-call(bf16[8,256,128]{2,1,0:T(8,128)(2,1)S(1)} %rows.1.orb_rows.refs_4_.refs_5_, bf16[256,256]{1,0:T(8,128)(2,1)S(1)} %copy-done.1, bf16[64,192]{1,0:T(8,128)(2,1)S(1)} %copy-done.4, ...), custom_call_target="tpu_custom_call" | custom-call | bytes 9000000 | tf_op jit(solution)/shard_map/base_forward/pallas_call | solution.py:508
  30.1 1.7 %collective-permute-start = (bf16[8,64,128]{2,1,0:T(8,128)(2,1)S(1)}, bf16[8,64,128]{2,1,0:T(8,128)(2,1)S(1)}, u32[]{:S(2)}, u32[]{:S(2)}) collective-permute-start(bf16[8,64,128]{2,1,0:T(8,128)(2,1)S(1)} %get-tuple-element.42), channel_id=1, source_target_pairs={{0,1},{1,0},{2,3},{3,2},{4,5},{5,4},{6,7},{7,6},{8,9},{9,8},{10,11... | collective-permute-start | bytes 393224 | tf_op jit(solution)/shard_map/ppermute | solution.py:490
  31.8 3.5 %collective-permute-done.near = bf16[8,64,128]{2,1,0:T(8,128)(2,1)S(1)} collective-permute-done((bf16[8,64,128]{2,1,0:T(8,128)(2,1)S(1)}, bf16[8,64,128]{2,1,0:T(8,128)(2,1)S(1)}, u32[]{:S(2)}, u32[]{:S(2)}) %collective-permute-start) | collective-permute-done | bytes 131104 | tf_op jit(solution)/shard_map/ppermute | solution.py:490
  35.4 3.1 %collective-permute-start.1 = (bf16[8,32,128]{2,1,0:T(8,128)(2,1)S(1)}, bf16[8,32,128]{2,1,0:T(8,128)(2,1)S(1)}, u32[]{:S(2)}, u32[]{:S(2)}) collective-permute-start(bf16[8,32,128]{2,1,0:T(8,128)(2,1)S(1)} %get-tuple-element.44), channel_id=1, source_target_pairs={{0,2},{1,3},{2,4},{3,5},{4,6},{5,7},{6,0},{7,1},{8,10},{9,11},{10,... | collective-permute-start | bytes 196616 | tf_op jit(solution)/shard_map/ppermute | solution.py:486
  38.5 4.7 %collective-permute-start.2 = (bf16[8,32,128]{2,1,0:T(8,128)(2,1)S(1)}, bf16[8,32,128]{2,1,0:T(8,128)(2,1)S(1)}, u32[]{:S(2)}, u32[]{:S(2)}) collective-permute-start(bf16[8,32,128]{2,1,0:T(8,128)(2,1)S(1)} %get-tuple-element.45), channel_id=1, source_target_pairs={{0,4},{1,5},{2,6},{3,7},{4,0},{5,1},{6,2},{7,3},{8,12},{9,13},{10,... | collective-permute-start | bytes 196616 | tf_op jit(solution)/shard_map/ppermute | solution.py:486
  43.2 2.4 %collective-permute-start.3 = (bf16[8,32,128]{2,1,0:T(8,128)(2,1)S(1)}, bf16[8,32,128]{2,1,0:T(8,128)(2,1)S(1)}, u32[]{:S(2)}, u32[]{:S(2)}) collective-permute-start(bf16[8,32,128]{2,1,0:T(8,128)(2,1)S(1)} %get-tuple-element.46), channel_id=1, source_target_pairs={{0,6},{1,7},{2,0},{3,1},{4,2},{5,3},{6,4},{7,5},{8,14},{9,15},{10,... | collective-permute-start | bytes 196616 | tf_op jit(solution)/shard_map/ppermute | solution.py:486
  45.6 1.2 outbox.3
  46.8 1.3 copy-done
  48.1 2.5 %collective-permute-done.3.refs_2_ = bf16[8,32,128]{2,1,0:T(8,128)(2,1)S(1)} collective-permute-done((bf16[8,32,128]{2,1,0:T(8,128)(2,1)S(1)}, bf16[8,32,128]{2,1,0:T(8,128)(2,1)S(1)}, u32[]{:S(2)}, u32[]{:S(2)}) %collective-permute-start.3) | collective-permute-done | bytes 65568 | tf_op jit(solution)/shard_map/ppermute | solution.py:486
  50.7 1.6 base_inverse.1.refs_9_
  52.3 2.1 %all-to-all-done.1.fetched = bf16[32,256,128]{2,1,0:T(8,128)(2,1)} async-done(((bf16[32,256,128]{2,1,0:T(8,128)(2,1)}), bf16[32,256,128]{2,1,0:T(8,128)(2,1)}, u32[]{:S(2)}, u32[]{:S(2)}) %all-to-all-start.1) | async-done | bytes 2097184 | tf_op jit(solution)/shard_map/all_to_all | solution.py:506
  54.4 6.0 %all-to-all-start.2 = ((bf16[32,256,128]{2,1,0:T(8,128)(2,1)}), bf16[32,256,128]{2,1,0:T(8,128)(2,1)}, u32[]{:S(2)}, u32[]{:S(2)}) async-start(bf16[32,256,128]{2,1,0:T(8,128)(2,1)} %copy-done), calls=%async_computation.2 | async-start | bytes 4194304 | tf_op jit(solution)/shard_map/all_to_all | solution.py:515
  60.5 4.9 %pair_forward.2 = (bf16[8,256,128]{2,1,0:T(8,128)(2,1)S(1)}, f32[8,256,128]{2,1,0:T(8,128)S(1)}, f32[8,64,128]{2,1,0:T(8,128)S(1)}, bf16[8,64,128]{2,1,0:T(8,128)(2,1)S(1)}) custom-call(s32[8]{0:T(128)S(1)} %get-tuple-element.84.perm, s32[2,16]{1,0:T(2,128)S(1)} %copy-done.8, s32[2,256]{1,0:T(2,128)S(1)} %copy-done.6, ...), custom_call_target="tpu_custom_call" | custom-call | bytes 12000000 | tf_op jit(solution)/shard_map/pair_forward/pallas_call | solution.py:520
  65.4 1.0 collective-permute-start.4
  66.3 4.0 %collective-permute-done.4.near = bf16[8,64,128]{2,1,0:T(8,128)(2,1)S(1)} collective-permute-done((bf16[8,64,128]{2,1,0:T(8,128)(2,1)S(1)}, bf16[8,64,128]{2,1,0:T(8,128)(2,1)S(1)}, u32[]{:S(2)}, u32[]{:S(2)}) %collective-permute-start.4) | collective-permute-done | bytes 131104 | tf_op jit(solution)/shard_map/ppermute | solution.py:490
  70.4 2.7 %collective-permute-start.5 = (bf16[8,32,128]{2,1,0:T(8,128)(2,1)S(1)}, bf16[8,32,128]{2,1,0:T(8,128)(2,1)S(1)}, u32[]{:S(2)}, u32[]{:S(2)}) collective-permute-start(bf16[8,32,128]{2,1,0:T(8,128)(2,1)S(1)} %get-tuple-element.51), channel_id=1, source_target_pairs={{0,2},{1,3},{2,4},{3,5},{4,6},{5,7},{6,0},{7,1},{8,10},{9,11},{10,... | collective-permute-start | bytes 196616 | tf_op jit(solution)/shard_map/ppermute | solution.py:486
  73.1 4.7 %collective-permute-start.6 = (bf16[8,32,128]{2,1,0:T(8,128)(2,1)S(1)}, bf16[8,32,128]{2,1,0:T(8,128)(2,1)S(1)}, u32[]{:S(2)}, u32[]{:S(2)}) collective-permute-start(bf16[8,32,128]{2,1,0:T(8,128)(2,1)S(1)} %get-tuple-element.52), channel_id=1, source_target_pairs={{0,4},{1,5},{2,6},{3,7},{4,0},{5,1},{6,2},{7,3},{8,12},{9,13},{10,... | collective-permute-start | bytes 196616 | tf_op jit(solution)/shard_map/ppermute | solution.py:486
  77.9 2.4 %collective-permute-start.7 = (bf16[8,32,128]{2,1,0:T(8,128)(2,1)S(1)}, bf16[8,32,128]{2,1,0:T(8,128)(2,1)S(1)}, u32[]{:S(2)}, u32[]{:S(2)}) collective-permute-start(bf16[8,32,128]{2,1,0:T(8,128)(2,1)S(1)} %get-tuple-element.53), channel_id=1, source_target_pairs={{0,6},{1,7},{2,0},{3,1},{4,2},{5,3},{6,4},{7,5},{8,14},{9,15},{10,... | collective-permute-start | bytes 196616 | tf_op jit(solution)/shard_map/ppermute | solution.py:486
  80.3 5.0 %collective-permute-done.7.refs_2_ = bf16[8,32,128]{2,1,0:T(8,128)(2,1)S(1)} collective-permute-done((bf16[8,32,128]{2,1,0:T(8,128)(2,1)S(1)}, bf16[8,32,128]{2,1,0:T(8,128)(2,1)S(1)}, u32[]{:S(2)}, u32[]{:S(2)}) %collective-permute-start.7) | collective-permute-done | bytes 65568 | tf_op jit(solution)/shard_map/ppermute | solution.py:486
  85.3 2.7 %pair_inverse.2 = (f32[8,256,128]{2,1,0:T(8,128)S(1)}, bf16[32,256,128]{2,1,0:T(8,128)(2,1)S(1)}) custom-call(s32[1]{0:T(128)} %bitcast.1.grid, s32[8]{0:T(128)S(1)} %get-tuple-element.84.perm, s32[2,16]{1,0:T(2,128)S(1)} %copy-done.8, s32[2,256]{1,0:T(2,128)S(1)} %copy-done.6, ...), custom_call_target="tpu_custom_call", output_to_operand_aliasing={{0}: (14, {})} | custom-call | bytes 15000000 | tf_op jit(solution)/shard_map/pair_inverse/pallas_call | solution.py:530
  88.0 1.4 copy-done.3
  89.4 8.1 %all-to-all-start.3 = ((bf16[32,256,128]{2,1,0:T(8,128)(2,1)}), bf16[32,256,128]{2,1,0:T(8,128)(2,1)}, u32[]{:S(2)}, u32[]{:S(2)}) async-start(bf16[32,256,128]{2,1,0:T(8,128)(2,1)} %copy-done.3), calls=%async_computation.3 | async-start | bytes 4194304 | tf_op jit(solution)/shard_map/all_to_all | solution.py:542
  97.5 4.9 %pair_forward.3 = (bf16[8,256,128]{2,1,0:T(8,128)(2,1)S(1)}, f32[8,256,128]{2,1,0:T(8,128)S(1)}, f32[8,64,128]{2,1,0:T(8,128)S(1)}, bf16[9,64,128]{2,1,0:T(8,128)(2,1)S(1)}, f32[8,128]{1,0:T(8,128)S(1)}) custom-call(s32[8]{0:T(128)S(1)} %get-tuple-element.85.perm, s32[2,16]{1,0:T(2,128)S(1)} %copy-done.8, s32[2,256]{1,0:T(2,128)S(1)} %copy-done.6, ...), custom_call_target="tpu_custom_call" | custom-call | bytes 12000000 | tf_op jit(solution)/shard_map/pair_forward/pallas_call | solution.py:520
  102.5 5.2 %collective-permute-done.8.near = bf16[9,64,128]{2,1,0:T(8,128)(2,1)S(1)} collective-permute-done((bf16[9,64,128]{2,1,0:T(8,128)(2,1)S(1)}, bf16[9,64,128]{2,1,0:T(8,128)(2,1)S(1)}, u32[]{:S(2)}, u32[]{:S(2)}) %collective-permute-start.8) | collective-permute-done | bytes 147488 | tf_op jit(solution)/shard_map/ppermute | solution.py:490
  107.8 3.2 %collective-permute-start.11 = (bf16[9,64,128]{2,1,0:T(8,128)(2,1)S(1)}, bf16[9,64,128]{2,1,0:T(8,128)(2,1)S(1)}, u32[]{:S(2)}, u32[]{:S(2)}) collective-permute-start(bf16[9,64,128]{2,1,0:T(8,128)(2,1)S(1)} %pair_up_whole.1.refs_0_), channel_id=1, source_target_pairs={{0,6},{1,7},{2,0},{3,1},{4,2},{5,3},{6,4},{7,5},{8,14},{9,15},{10,... | collective-permute-start | bytes 442376 | tf_op jit(solution)/shard_map/ppermute | solution.py:486
  111.0 2.1 %collective-permute-start.10 = (bf16[9,64,128]{2,1,0:T(8,128)(2,1)S(1)}, bf16[9,64,128]{2,1,0:T(8,128)(2,1)S(1)}, u32[]{:S(2)}, u32[]{:S(2)}) collective-permute-start(bf16[9,64,128]{2,1,0:T(8,128)(2,1)S(1)} %pair_up_whole.1.refs_0_), channel_id=1, source_target_pairs={{0,4},{1,5},{2,6},{3,7},{4,0},{5,1},{6,2},{7,3},{8,12},{9,13},{10,... | collective-permute-start | bytes 442376 | tf_op jit(solution)/shard_map/ppermute | solution.py:486
  113.1 0.6 collective-permute-start.9
  113.7 7.5 %collective-permute-done.11.refs_3_ = bf16[9,64,128]{2,1,0:T(8,128)(2,1)S(1)} collective-permute-done((bf16[9,64,128]{2,1,0:T(8,128)(2,1)S(1)}, bf16[9,64,128]{2,1,0:T(8,128)(2,1)S(1)}, u32[]{:S(2)}, u32[]{:S(2)}) %collective-permute-start.11) | collective-permute-done | bytes 147488 | tf_op jit(solution)/shard_map/ppermute | solution.py:486
  121.2 2.1 %collective-permute-done.10.refs_2_ = bf16[9,64,128]{2,1,0:T(8,128)(2,1)S(1)} collective-permute-done((bf16[9,64,128]{2,1,0:T(8,128)(2,1)S(1)}, bf16[9,64,128]{2,1,0:T(8,128)(2,1)S(1)}, u32[]{:S(2)}, u32[]{:S(2)}) %collective-permute-start.10) | collective-permute-done | bytes 147488 | tf_op jit(solution)/shard_map/ppermute | solution.py:486
  123.3 1.2 collective-permute-done.9.refs_1_
  124.5 2.9 %pair_inverse.3 = (f32[8,256,128]{2,1,0:T(8,128)S(1)}, bf16[32,272,128]{2,1,0:T(8,128)(2,1)S(1)}) custom-call(s32[1]{0:T(128)} %bitcast.1.grid, s32[8]{0:T(128)S(1)} %get-tuple-element.85.perm, s32[2,16]{1,0:T(2,128)S(1)} %copy-done.8, s32[2,256]{1,0:T(2,128)S(1)} %copy-done.6, ...), custom_call_target="tpu_custom_call", output_to_operand_aliasing={{0}: (15, {})} | custom-call | bytes 15000000 | tf_op jit(solution)/shard_map/pair_inverse/pallas_call | solution.py:530
  127.3 1.4 copy-done.2
  128.7 8.8 %all-to-all-start.4 = ((bf16[32,272,128]{2,1,0:T(8,128)(2,1)}), bf16[32,272,128]{2,1,0:T(8,128)(2,1)}, u32[]{:S(2)}, u32[]{:S(2)}) async-start(bf16[32,272,128]{2,1,0:T(8,128)(2,1)} %copy-done.2), calls=%async_computation.4 | async-start | bytes 4456448 | tf_op jit(solution)/shard_map/all_to_all | solution.py:545
  137.5 2.4 %add.1088 = (f32[8,256,128]{2,1,0:T(8,128)S(1)}, f32[8,128]{1,0:T(8,128)S(1)}) custom-call(s32[32,128]{1,0:T(8,128)S(1)} %bitcast.8, bf16[32,256,128]{2,1,0:T(8,128)(2,1)} %all-to-all-done.3.arrived, bf16[8,256,128]{2,1,0:T(8,128)(2,1)S(1)} %rows.1.orb_rows.refs_4_.refs_5_, ...), custom_call_target="tpu_custom_call", output_to_operand_aliasing={{0}: (3, {})} | custom-call | bytes 6000000 | tf_op jit(solution)/shard_map/add/pallas_call | solution.py:546
  139.8 16.4 %psum.7.energy_in = f32[8,128]{1,0:T(8,128)S(1)} all-reduce(f32[8,128]{1,0:T(8,128)S(1)} %get-tuple-element.71), channel_id=1, replica_groups=mesh['orb'=32,'grid'=8] {'grid'}, use_global_device_ids=true, to_apply=%region_0.1 | all-reduce | flops 1024 | bytes 8192 | tf_op jit(solution)/shard_map/psum | solution.py:549
  156.2 11.0 %all-to-all-done.4.arrived = bf16[32,272,128]{2,1,0:T(8,128)(2,1)} async-done(((bf16[32,272,128]{2,1,0:T(8,128)(2,1)}), bf16[32,272,128]{2,1,0:T(8,128)(2,1)}, u32[]{:S(2)}, u32[]{:S(2)}) %all-to-all-start.4) | async-done | bytes 2228256 | tf_op jit(solution)/shard_map/all_to_all | solution.py:545
  167.2 3.1 %finish.1 = (bf16[8,8,4096]{2,1,0:T(8,128)(2,1)}, f32[8]{0:T(128)}) custom-call(s32[32,128]{1,0:T(8,128)S(1)} %bitcast.9, bf16[32,272,128]{2,1,0:T(8,128)(2,1)} %all-to-all-done.4.arrived, f32[8,256,128]{2,1,0:T(8,128)S(1)} %get-tuple-element.74.total_in, f32[8,128]{1,0:T(8,128)S(1)} %psum.7.energy_in), custom_call_target="tpu_custom_call" | custom-call | bytes 9000000 | tf_op jit(solution)/shard_map/finish/pallas_call | solution.py:551
  (45 shorter events, 1.6 us)
Async XLA Ops:
  0.6 0.7 copy-start.7
  2.8 15.5 %all-to-all-start = ((s32[32,1,128]{2,1,0:T(1,128)}), s32[32,1,128]{2,1,0:T(1,128)S(1)}, u32[]{:S(2)}, u32[]{:S(2)}) async-start(s32[32,1,128]{2,1,0:T(1,128)} %get-tuple-element.39), calls=%async_computation | async-start | bytes 32768 | tf_op jit(solution)/shard_map/all_to_all | solution.py:477
  12.3 1.0 copy-start.5
  20.8 6.0 %copy-start.1 = (bf16[256,256]{1,0:T(8,128)(2,1)S(1)}, bf16[256,256]{1,0:T(8,128)(2,1)}, u32[]{:S(2)}) copy-start(bf16[256,256]{1,0:T(8,128)(2,1)} %constant.144.clone.y_right.refs_5_.refs_6_.refs_7_) | copy-start | bytes 393220
  20.8 6.0 %copy-start.4 = (bf16[64,192]{1,0:T(8,128)(2,1)S(1)}, bf16[64,192]{1,0:T(8,128)(2,1)}, u32[]{:S(2)}) copy-start(bf16[64,192]{1,0:T(8,128)(2,1)} %constant.145.clone.x_left.refs_6_.refs_7_.refs_8_) | copy-start | bytes 73732
  20.8 33.6 %all-to-all-start.1 = ((bf16[32,256,128]{2,1,0:T(8,128)(2,1)}), bf16[32,256,128]{2,1,0:T(8,128)(2,1)}, u32[]{:S(2)}, u32[]{:S(2)}) async-start(bf16[32,256,128]{2,1,0:T(8,128)(2,1)} %outbox.2), calls=%async_computation.1 | async-start | bytes 4194304 | tf_op jit(solution)/shard_map/all_to_all | solution.py:506
  30.1 5.2 %collective-permute-start = (bf16[8,64,128]{2,1,0:T(8,128)(2,1)S(1)}, bf16[8,64,128]{2,1,0:T(8,128)(2,1)S(1)}, u32[]{:S(2)}, u32[]{:S(2)}) collective-permute-start(bf16[8,64,128]{2,1,0:T(8,128)(2,1)S(1)} %get-tuple-element.42), channel_id=1, source_target_pairs={{0,1},{1,0},{2,3},{3,2},{4,5},{5,4},{6,7},{7,6},{8,9},{9,8},{10,11... | collective-permute-start | bytes 393224 | tf_op jit(solution)/shard_map/ppermute | solution.py:490
  35.4 12.7 %collective-permute-start.1 = (bf16[8,32,128]{2,1,0:T(8,128)(2,1)S(1)}, bf16[8,32,128]{2,1,0:T(8,128)(2,1)S(1)}, u32[]{:S(2)}, u32[]{:S(2)}) collective-permute-start(bf16[8,32,128]{2,1,0:T(8,128)(2,1)S(1)} %get-tuple-element.44), channel_id=1, source_target_pairs={{0,2},{1,3},{2,4},{3,5},{4,6},{5,7},{6,0},{7,1},{8,10},{9,11},{10,... | collective-permute-start | bytes 196616 | tf_op jit(solution)/shard_map/ppermute | solution.py:486
  38.5 9.6 %collective-permute-start.2 = (bf16[8,32,128]{2,1,0:T(8,128)(2,1)S(1)}, bf16[8,32,128]{2,1,0:T(8,128)(2,1)S(1)}, u32[]{:S(2)}, u32[]{:S(2)}) collective-permute-start(bf16[8,32,128]{2,1,0:T(8,128)(2,1)S(1)} %get-tuple-element.45), channel_id=1, source_target_pairs={{0,4},{1,5},{2,6},{3,7},{4,0},{5,1},{6,2},{7,3},{8,12},{9,13},{10,... | collective-permute-start | bytes 196616 | tf_op jit(solution)/shard_map/ppermute | solution.py:486
  43.2 7.4 %collective-permute-start.3 = (bf16[8,32,128]{2,1,0:T(8,128)(2,1)S(1)}, bf16[8,32,128]{2,1,0:T(8,128)(2,1)S(1)}, u32[]{:S(2)}, u32[]{:S(2)}) collective-permute-start(bf16[8,32,128]{2,1,0:T(8,128)(2,1)S(1)} %get-tuple-element.46), channel_id=1, source_target_pairs={{0,6},{1,7},{2,0},{3,1},{4,2},{5,3},{6,4},{7,5},{8,14},{9,15},{10,... | collective-permute-start | bytes 196616 | tf_op jit(solution)/shard_map/ppermute | solution.py:486
  46.8 1.3 copy-start
  52.2 8.2 %copy-start.6 = (s32[2,256]{1,0:T(2,128)S(1)}, s32[2,256]{1,0:T(2,128)}, u32[]{:S(2)}) copy-start(s32[2,256]{1,0:T(2,128)} %anchor.7) | copy-start | bytes 6148
  52.2 8.2 %copy-start.8 = (s32[2,16]{1,0:T(2,128)S(1)}, s32[2,16]{1,0:T(2,128)}, u32[]{:S(2)}) copy-start(s32[2,16]{1,0:T(2,128)} %pairs.9) | copy-start | bytes 388
  54.4 35.0 %all-to-all-start.2 = ((bf16[32,256,128]{2,1,0:T(8,128)(2,1)}), bf16[32,256,128]{2,1,0:T(8,128)(2,1)}, u32[]{:S(2)}, u32[]{:S(2)}) async-start(bf16[32,256,128]{2,1,0:T(8,128)(2,1)} %copy-done), calls=%async_computation.2 | async-start | bytes 4194304 | tf_op jit(solution)/shard_map/all_to_all | solution.py:515
  65.4 5.0 %collective-permute-start.4 = (bf16[8,64,128]{2,1,0:T(8,128)(2,1)S(1)}, bf16[8,64,128]{2,1,0:T(8,128)(2,1)S(1)}, u32[]{:S(2)}, u32[]{:S(2)}) collective-permute-start(bf16[8,64,128]{2,1,0:T(8,128)(2,1)S(1)} %get-tuple-element.49), channel_id=1, source_target_pairs={{0,1},{1,0},{2,3},{3,2},{4,5},{5,4},{6,7},{7,6},{8,9},{9,8},{10,11... | collective-permute-start | bytes 393224 | tf_op jit(solution)/shard_map/ppermute | solution.py:490
  70.4 9.9 %collective-permute-start.5 = (bf16[8,32,128]{2,1,0:T(8,128)(2,1)S(1)}, bf16[8,32,128]{2,1,0:T(8,128)(2,1)S(1)}, u32[]{:S(2)}, u32[]{:S(2)}) collective-permute-start(bf16[8,32,128]{2,1,0:T(8,128)(2,1)S(1)} %get-tuple-element.51), channel_id=1, source_target_pairs={{0,2},{1,3},{2,4},{3,5},{4,6},{5,7},{6,0},{7,1},{8,10},{9,11},{10,... | collective-permute-start | bytes 196616 | tf_op jit(solution)/shard_map/ppermute | solution.py:486
  73.1 7.2 %collective-permute-start.6 = (bf16[8,32,128]{2,1,0:T(8,128)(2,1)S(1)}, bf16[8,32,128]{2,1,0:T(8,128)(2,1)S(1)}, u32[]{:S(2)}, u32[]{:S(2)}) collective-permute-start(bf16[8,32,128]{2,1,0:T(8,128)(2,1)S(1)} %get-tuple-element.52), channel_id=1, source_target_pairs={{0,4},{1,5},{2,6},{3,7},{4,0},{5,1},{6,2},{7,3},{8,12},{9,13},{10,... | collective-permute-start | bytes 196616 | tf_op jit(solution)/shard_map/ppermute | solution.py:486
  77.9 7.4 %collective-permute-start.7 = (bf16[8,32,128]{2,1,0:T(8,128)(2,1)S(1)}, bf16[8,32,128]{2,1,0:T(8,128)(2,1)S(1)}, u32[]{:S(2)}, u32[]{:S(2)}) collective-permute-start(bf16[8,32,128]{2,1,0:T(8,128)(2,1)S(1)} %get-tuple-element.53), channel_id=1, source_target_pairs={{0,6},{1,7},{2,0},{3,1},{4,2},{5,3},{6,4},{7,5},{8,14},{9,15},{10,... | collective-permute-start | bytes 196616 | tf_op jit(solution)/shard_map/ppermute | solution.py:486
  88.0 1.4 copy-start.3
  89.4 39.3 %all-to-all-start.3 = ((bf16[32,256,128]{2,1,0:T(8,128)(2,1)}), bf16[32,256,128]{2,1,0:T(8,128)(2,1)}, u32[]{:S(2)}, u32[]{:S(2)}) async-start(bf16[32,256,128]{2,1,0:T(8,128)(2,1)} %copy-done.3), calls=%async_computation.3 | async-start | bytes 4194304 | tf_op jit(solution)/shard_map/all_to_all | solution.py:542
  102.4 5.3 %collective-permute-start.8 = (bf16[9,64,128]{2,1,0:T(8,128)(2,1)S(1)}, bf16[9,64,128]{2,1,0:T(8,128)(2,1)S(1)}, u32[]{:S(2)}, u32[]{:S(2)}) collective-permute-start(bf16[9,64,128]{2,1,0:T(8,128)(2,1)S(1)} %get-tuple-element.60), channel_id=1, source_target_pairs={{0,1},{1,0},{2,3},{3,2},{4,5},{5,4},{6,7},{7,6},{8,9},{9,8},{10,11... | collective-permute-start | bytes 442376 | tf_op jit(solution)/shard_map/ppermute | solution.py:490
  107.8 13.4 %collective-permute-start.11 = (bf16[9,64,128]{2,1,0:T(8,128)(2,1)S(1)}, bf16[9,64,128]{2,1,0:T(8,128)(2,1)S(1)}, u32[]{:S(2)}, u32[]{:S(2)}) collective-permute-start(bf16[9,64,128]{2,1,0:T(8,128)(2,1)S(1)} %pair_up_whole.1.refs_0_), channel_id=1, source_target_pairs={{0,6},{1,7},{2,0},{3,1},{4,2},{5,3},{6,4},{7,5},{8,14},{9,15},{10,... | collective-permute-start | bytes 442376 | tf_op jit(solution)/shard_map/ppermute | solution.py:486
  111.0 12.3 %collective-permute-start.10 = (bf16[9,64,128]{2,1,0:T(8,128)(2,1)S(1)}, bf16[9,64,128]{2,1,0:T(8,128)(2,1)S(1)}, u32[]{:S(2)}, u32[]{:S(2)}) collective-permute-start(bf16[9,64,128]{2,1,0:T(8,128)(2,1)S(1)} %pair_up_whole.1.refs_0_), channel_id=1, source_target_pairs={{0,4},{1,5},{2,6},{3,7},{4,0},{5,1},{6,2},{7,3},{8,12},{9,13},{10,... | collective-permute-start | bytes 442376 | tf_op jit(solution)/shard_map/ppermute | solution.py:486
  113.1 11.3 %collective-permute-start.9 = (bf16[9,64,128]{2,1,0:T(8,128)(2,1)S(1)}, bf16[9,64,128]{2,1,0:T(8,128)(2,1)S(1)}, u32[]{:S(2)}, u32[]{:S(2)}) collective-permute-start(bf16[9,64,128]{2,1,0:T(8,128)(2,1)S(1)} %pair_up_whole.1.refs_0_), channel_id=1, source_target_pairs={{0,2},{1,3},{2,4},{3,5},{4,6},{5,7},{6,0},{7,1},{8,10},{9,11},{10,... | collective-permute-start | bytes 442376 | tf_op jit(solution)/shard_map/ppermute | solution.py:486
  127.3 1.4 copy-start.2
  128.7 38.5 %all-to-all-start.4 = ((bf16[32,272,128]{2,1,0:T(8,128)(2,1)}), bf16[32,272,128]{2,1,0:T(8,128)(2,1)}, u32[]{:S(2)}, u32[]{:S(2)}) async-start(bf16[32,272,128]{2,1,0:T(8,128)(2,1)} %copy-done.2), calls=%async_computation.4 | async-start | bytes 4456448 | tf_op jit(solution)/shard_map/all_to_all | solution.py:545
where the time goes:
time: 172 us; the launch traced here: 171 us
  starting transfers between devices  65.3 us (38%)
  waiting for transfers between devices  49.1 us (29%)
  Pallas kernels  31.2 us (18%)
  blocking collectives  16.4 us (10%)
  local copies, waits for them, and re-layouts  6.47 us (4%)
    ppermute x9, starting transfers between devices, to_pairs(): lax.ppermute(sums[e - 1], 'grid', [(i, (i + 2 * e) % GRID) for i in range...  26 us
    ppermute x9, waiting for transfers between devices, to_pairs(): lax.ppermute(sums[e - 1], 'grid', [(i, (i + 2 * e) % GRID) for i in range...  18.3 us
    all_to_all x2, starting transfers between devices, local(): lax.all_to_all(back, 'orb', split_axis=0, concat_axis=0, tiled=True)  16.8 us
    psum x1, blocking collectives, local(): energy = lax.psum(energy, 'grid')  16.4 us
    ppermute x3, waiting for transfers between devices, from_grid(): near = lax.ppermute(message, 'grid', [(i, i ^ 1) for i in range(GRID)])  12.7 us
    all_to_all x2, waiting for transfers between devices, local(): lax.all_to_all(back, 'orb', split_axis=0, concat_axis=0, tiled=True)  11 us
    pallas_call x2, Pallas kernels, pair_terms(): call(functools.partial(pair_forward_kernel, whole), [BOXES, TOTALS, ENDS]...  9.83 us
    all_to_all x1, starting transfers between devices, local(): lax.all_to_all(ask, 'orb', split_axis=0, concat_axis=0, tiled=True)  8.6 us
  transfers between devices with their start and end apart: 17, of which 12 were waited for; matrix products, arithmetic and copies ran while one was open for 1% of the time, Pallas kernels for 14%

commit v1 on v0

--- a/solution.py
+++ b/solution.py
@@ -17,6 +17,7 @@
 GRID = 8
 PAIRS = GRID // 2
 COMBOS = [(p, q) for q in range(PAIRS) for p in range(q)]
+PART_ORDER, WHOLE_ORDER = (2, 1, 3), (1, 2, 3)
 UP, DOWN, MIDDLE, CARRY, PAST_UP, PAST_DOWN, INSIDE, ACROSS = 0, 8, 16, 24, 27, 28, 29, 30
 CHUNK = 8
 ORB_DEV = 8
@@ -111,11 +112,16 @@
     return both[:, :LANES] + both[:, LANES:]
 
 
-def times_x(planes, x_left):
+def times_x(planes, x_left, terms):
     value = jnp.concatenate(planes, axis=1)
     other = jnp.concatenate([pltpu.roll(p, BOX, 1) for p in planes], axis=1)
-    high, low = split(jnp.concatenate([value, other], axis=0))
-    both = dot(x_left, jnp.concatenate([high, low, high], axis=0))
+    data = jnp.concatenate([value, other], axis=0)
+    if terms == 1:
+        high = data.astype(BF16)
+        both = dot(x_left[:, BOX:], jnp.concatenate([high, high], axis=0))
+    else:
+        high, low = split(data)
+        both = dot(x_left, jnp.concatenate([high, low, high], axis=0))
     first = lane_iota(TILES) < BOX
     out = []
     for z in range(PLANES):
@@ -151,7 +157,7 @@
 def forward(rho, tables, held, coeffs, ends, message, energy, n):
     y_right, x_left, z_table = tables
     held[...] = times_y(rho, y_right[...])
-    planes = times_x([held[pl.ds(z, TILES, stride=PLANES), :] for z in range(PLANES)], x_left[...])
+    planes = times_x([held[pl.ds(z, TILES, stride=PLANES), :] for z in range(PLANES)], x_left[...], 1)
     for z in range(PLANES):
         coeffs[n, TILES * z : TILES * (z + 1), :] = planes[z]
     above = jnp.zeros((TILES, LANES), F32)
@@ -165,24 +171,23 @@
         below = z_table[DOWN + z] * below + planes[z]
     both = jnp.concatenate([above, below], axis=0)
     ends[n] = both
-    message[n] = both.astype(BF16)
+    message[2 * TILES * n : 2 * TILES * (n + 1), :] = both.astype(BF16)
     if energy is not None:
         energy[n : n + 1, :] = column_sums(product)
 
 
 def pack_energy(energy, message):
     high = energy.astype(BF16).astype(F32)
-    message[CHUNK, :16, :] = jnp.concatenate([high, energy - high], axis=0).astype(BF16)
-    message[CHUNK, 16:, :] = jnp.zeros((2 * TILES - 16, LANES), BF16)
+    message[2 * TILES * CHUNK :, :] = jnp.concatenate([high, energy - high], axis=0).astype(BF16)
 
 
 def unpack_energy(message):
-    both = message[CHUNK, :16, :].astype(F32)
+    both = message[2 * TILES * CHUNK :, :].astype(F32)
     return both[:8] + both[8:]
 
 
 def halves(message, n):
-    both = message[n].astype(F32)
+    both = message[2 * TILES * n : 2 * TILES * (n + 1), :].astype(F32)
     return both[:TILES], both[TILES:]
 
 
@@ -217,7 +222,7 @@
         carried = z_table[DOWN + z] * from_above
         solved[z] = z_table[MIDDLE + z] * (ups[z] + carried)
         from_above = planes[z] + carried
-    full = times_y(jnp.concatenate(times_x(solved, x_left[...]), axis=0), y_right[...])
+    full = times_y(jnp.concatenate(times_x(solved, x_left[...], 2), axis=0), y_right[...])
     for z in range(PLANES):
         held[pl.ds(z, TILES, stride=PLANES), :] = full[TILES * z : TILES * (z + 1)]
     return held[...]
@@ -340,14 +345,18 @@
     total = energy[...] + unpack_energy(near)
     for n in range(CHUNK):
         up, down, product = pair_up((grid[0] & 1) == 1, ends, near, z_table, n)
-        message[n, :TILES, :] = up.astype(BF16)
-        message[n, TILES:, :] = down.astype(BF16)
+        both = jnp.concatenate([up, down], axis=0)
+        message[2 * TILES * n : 2 * TILES * (n + 1), :] = both.astype(BF16)
         total += jnp.where(rows == n, 2.0 * column_sums(z_table[INSIDE] * product), 0.0)
     pack_energy(total, message)
 
 
+def in_order(refs, order):
+    return [refs[order.index(e)] for e in range(1, PAIRS)]
+
+
 def base_inverse_kernel(grid, near, *refs):
-    sums, refs = refs[: PAIRS - 1], refs[PAIRS - 1 :]
+    sums, refs = in_order(refs[: PAIRS - 1], PART_ORDER), refs[PAIRS - 1 :]
     coeffs, orb_rows, y_right, x_left, z_table, total, *held = refs
     for n in range(ORB_DEV):
         here = [block[n].astype(F32) for block in sums]
@@ -358,6 +367,10 @@
 def pair_inverse_kernel(whole, grid, perm, pairs, anchor, near, *refs):
     count = PAIRS if whole else PAIRS - 1
     blocks, refs = refs[:count], refs[count:]
+    if whole:
+        blocks = [blocks[0], *in_order(blocks[1:], WHOLE_ORDER)]
+    else:
+        blocks = in_order(blocks, PART_ORDER)
     coeffs, orb_rows, moved, y_right, x_left, z_table, total_in, total, outbox, *refs = refs
     buffers, held, backs = refs[:CHUNK], refs[CHUNK : 2 * CHUNK], refs[2 * CHUNK]
     pair = grid[0] >> 1
@@ -391,9 +404,9 @@
             total[owner] += moved[n].astype(F32) * held[n][...]
 
 
-def each_arrived(chunk, asked, arrived, action):
+def each_arrived(asked, arrived, action):
     def step(d, carry):
-        which = asked[d, chunk]
+        which = asked[d]
 
         @pl.when(which >= 0)
         def _():
@@ -404,26 +417,37 @@
     lax.fori_loop(0, arrived.shape[0], step, 0)
 
 
-def add_kernel(chunk, asked, arrived, orb_rows, total_in, total, energy):
+def add_kernel(asked, arrived, orb_rows, total_in, total, energy):
     total[...] = total_in[...]
 
     def action(which, d):
         total[which] += arrived[d].astype(F32)
 
-    each_arrived(chunk, asked, arrived, action)
+    each_arrived(asked, arrived, action)
     for n in range(ORB_DEV):
         energy[n : n + 1, :] = column_sums(orb_rows[n].astype(F32) * total[n])
 
 
-def finish_kernel(chunk, asked, arrived, total_in, energy_in, out, energy_out, total, energy):
+def finish_kernel(asked, arrived, total_in, energy_in, out, energy_out, total, energy, boxes, sems):
+    count = arrived.shape[0]
+    which = [asked[d] for d in range(count)]
+    copies = [pltpu.make_async_copy(arrived.at[d], boxes.at[d], sems.at[d]) for d in range(count)]
+    for d in range(count):
+
+        @pl.when(which[d] >= 0)
+        def _():
+            copies[d].start()
+
     total[...] = total_in[...]
     energy[...] = energy_in[...]
-
-    def action(which, d):
-        total[which] += arrived[d, :ROWS, :].astype(F32)
-        energy[pl.ds(which, 1), :] += column_sums(arrived[d, ROWS:, :].astype(F32))
-
-    each_arrived(chunk, asked, arrived, action)
+    for d in range(count):
+
+        @pl.when(which[d] >= 0)
+        def _():
+            copies[d].wait()
+            total[which[d]] += boxes[d, :ROWS, :].astype(F32)
+            energy[pl.ds(which[d], 1), :] += column_sums(boxes[d, ROWS:, :].astype(F32))
+
     for n in range(ORB_DEV):
         box = total[n]
         out[n] = jnp.concatenate([box[8 * t : 8 * t + 8] for t in range(TILES)], axis=1).astype(BF16)
@@ -432,10 +456,11 @@
 
 VMEM = pl.BlockSpec(memory_space=pltpu.VMEM)
 SMEM = pl.BlockSpec(memory_space=pltpu.SMEM)
+ANY = pl.BlockSpec(memory_space=pl.ANY)
 HELD = [pltpu.VMEM((ROWS, LANES), F32)] * CHUNK
 SHIFT_BUFFERS = [pltpu.VMEM(((2 * PAD + TILES) * 8, LANES), F32)] * CHUNK
-MESSAGE = jax.ShapeDtypeStruct((CHUNK, 2 * TILES, LANES), BF16)
-MESSAGE_WHOLE = jax.ShapeDtypeStruct((CHUNK + 1, 2 * TILES, LANES), BF16)
+MESSAGE = jax.ShapeDtypeStruct((CHUNK * 2 * TILES, LANES), BF16)
+MESSAGE_WHOLE = jax.ShapeDtypeStruct((CHUNK * 2 * TILES + 16, LANES), BF16)
 SUMS = [jax.ShapeDtypeStruct((CHUNK, TILES, LANES), BF16)] * (PAIRS - 1)
 ENDS = jax.ShapeDtypeStruct((CHUNK, 2 * TILES, LANES), F32)
 BOXES = jax.ShapeDtypeStruct((CHUNK, ROWS, LANES), BF16)
@@ -480,21 +505,20 @@
     z_table = z_factors(grid_index)
     tables = (y_right, x_left, z_table)
 
-    def to_pairs(sums):
-        out = [None] * (PAIRS - 1)
-        for e in range(1, PAIRS):
-            out[e - 1] = lax.ppermute(sums[e - 1], "grid", [(i, (i + 2 * e) % GRID) for i in range(GRID)])
-        return out
+    def to_pairs(sums, order):
+        return [
+            lax.ppermute(sums[e - 1], "grid", [(i, (i + 2 * e) % GRID) for i in range(GRID)]) for e in order
+        ]
 
     def from_grid(ends, message, energy=None):
         near = lax.ppermute(message, "grid", [(i, i ^ 1) for i in range(GRID)])
         if energy is None:
             sums = call(pair_up_kernel, SUMS, [SMEM] + [VMEM] * 3, [], "pair_up", 1)(grid, ends, near, z_table)
-            return near, *to_pairs(sums)
+            return near, *to_pairs(sums, PART_ORDER)
         here = call(pair_up_whole_kernel, MESSAGE_WHOLE, [SMEM] + [VMEM] * 4, [], "pair_up_whole", 1)(
             grid, ends, energy, near, z_table
         )
-        return near, here, *to_pairs([here] * (PAIRS - 1))
+        return near, here, *to_pairs([here] * (PAIRS - 1), WHOLE_ORDER)
 
     orb_rows = call(rows_kernel, BOXES, [VMEM], [], "rows", 1)(orbitals)
 
@@ -544,19 +568,24 @@
     back, arrived_a = lax.optimization_barrier((back, arrived_a))
     arrived_b = lax.all_to_all(back, "orb", split_axis=0, concat_axis=0, tiled=True)
     total, energy = call(
-        functools.partial(add_kernel, 0), [TOTALS, ENERGY], [SMEM] + [VMEM] * 3, [], "add", 2, aliases={3: 0}
-    )(asked, arrived_a, orb_rows, total)
+        add_kernel, [TOTALS, ENERGY], [SMEM] + [VMEM] * 3, [], "add", 2, aliases={3: 0}
+    )(asked[:, 0], arrived_a, orb_rows, total)
     energy = lax.psum(energy, "grid")
-    total, energy, arrived_b = lax.optimization_barrier((total, energy, arrived_b))
+    asked_b, total, energy, arrived_b = lax.optimization_barrier((asked[:, 1], total, energy, arrived_b))
     return call(
-        functools.partial(finish_kernel, 1),
+        finish_kernel,
         [jax.ShapeDtypeStruct(orbitals.shape, BF16), jax.ShapeDtypeStruct((ORB_DEV,), F32)],
-        [SMEM, VMEM, VMEM, VMEM],
-        [pltpu.VMEM(TOTALS.shape, F32), pltpu.VMEM(ENERGY.shape, F32)],
+        [SMEM, ANY, VMEM, VMEM],
+        [
+            pltpu.VMEM(TOTALS.shape, F32),
+            pltpu.VMEM(ENERGY.shape, F32),
+            pltpu.VMEM(arrived_b.shape, BF16),
+            pltpu.SemaphoreType.DMA((devices,)),
+        ],
         "finish",
         3,
         out_specs=[VMEM, SMEM],
-    )(asked, arrived_b, total, energy)
+    )(asked_b, arrived_b, total, energy)
 
 
 def solution(mesh):

time: 172 us -> 166 us (0.965)
  Pallas kernels: 31.2 us -> 24.9 us
  starting transfers between devices: 65.3 us -> 68.1 us
  waiting for transfers between devices: 49.1 us -> 47 us
    ppermute x9, waiting for transfers between devices: 18.3 us -> 11.9 us  [to_pairs(): lax.ppermute(sums[e - 1], 'grid', [(i, (i + 2 * e) % GRID) for i in range...]
    all_to_all x1, waiting for transfers between devices: 2.14 us -> 6.25 us  [local(): lax.all_to_all(box_a, 'orb', split_axis=0, concat_axis=0, tiled=True)]
    pallas_call x2, Pallas kernels: 9.83 us -> 5.88 us  [pair_terms(): call(functools.partial(pair_forward_kernel, whole), [BOXES, TOTALS, ENDS]...]
    ppermute x9, starting transfers between devices: 26 us -> 28.9 us  [to_pairs(): lax.ppermute(sums[e - 1], 'grid', [(i, (i + 2 * e) % GRID) for i in range...]
    all_to_all x1, waiting for transfers between devices: 0.01 us -> 2.75 us  [local(): lax.all_to_all(box_b, 'orb', split_axis=0, concat_axis=0, tiled=True)]
    pallas_call x1, Pallas kernels: 3.24 us -> 1.03 us  [local(): call(base_forward_kernel, [TOTALS, ENDS, MESSAGE], [VMEM] * 4, HELD, 'bas...]
    ppermute x3, starting transfers between devices: 2.77 us -> 4.7 us  [from_grid(): near = lax.ppermute(message, 'grid', [(i, i ^ 1) for i in range(GRID)])]
    ppermute x3, waiting for transfers between devices: 12.7 us -> 10.8 us  [from_grid(): near = lax.ppermute(message, 'grid', [(i, i ^ 1) for i in range(GRID)])]
  transfers between devices with their start and end apart: 17 -> 17, of which waited for: 12 -> 13; matrix products, arithmetic and copies ran while one was open for 1% -> 1% of each run, Pallas kernels for 14% -> 11%
where the time goes in v1:
time: 166 us
  starting transfers between devices  68.1 us (41%)
  waiting for transfers between devices  47 us (28%)
  Pallas kernels  24.9 us (15%)
  blocking collectives  16.9 us (10%)
  local copies, waits for them, and re-layouts  6.67 us (4%)
    ppermute x9, starting transfers between devices, to_pairs(): lax.ppermute(sums[e - 1], 'grid', [(i, (i + 2 * e) % GRID) for i in range...  28.9 us
    psum x1, blocking collectives, local(): energy = lax.psum(energy, 'grid')  16.9 us
    all_to_all x2, starting transfers between devices, local(): lax.all_to_all(back, 'orb', split_axis=0, concat_axis=0, tiled=True)  15.6 us
    ppermute x9, waiting for transfers between devices, to_pairs(): lax.ppermute(sums[e - 1], 'grid', [(i, (i + 2 * e) % GRID) for i in range...  11.9 us
    ppermute x3, waiting for transfers between devices, from_grid(): near = lax.ppermute(message, 'grid', [(i, i ^ 1) for i in range(GRID)])  10.8 us
    all_to_all x2, waiting for transfers between devices, local(): lax.all_to_all(back, 'orb', split_axis=0, concat_axis=0, tiled=True)  10.3 us
    all_to_all x1, starting transfers between devices, local(): lax.all_to_all(ask, 'orb', split_axis=0, concat_axis=0, tiled=True)  8.6 us
    all_to_all x1, waiting for transfers between devices, local(): lax.all_to_all(box_a, 'orb', split_axis=0, concat_axis=0, tiled=True)  6.25 us
  transfers between devices with their start and end apart: 17, of which 13 were waited for; matrix products, arithmetic and copies ran while one was open for 1% of the time, Pallas kernels for 11%

profile of v1, /device:TPU:1, one launch (start us, length us, event | category | flops | bytes accessed | tf_op | source)
XLA Modules:
  0.0 165.6 jit_solution(8455724976145596272)
XLA Ops:
  0.6 0.7 copy-done.7
  1.3 1.5 plan.1
  2.8 8.6 %all-to-all-start = ((s32[32,1,128]{2,1,0:T(1,128)}), s32[32,1,128]{2,1,0:T(1,128)S(1)}, u32[]{:S(2)}, u32[]{:S(2)}) async-start(s32[32,1,128]{2,1,0:T(1,128)} %get-tuple-element.40), calls=%async_computation | async-start | bytes 32768 | tf_op jit(solution)/shard_map/all_to_all | solution.py:502
  12.3 1.0 copy-done.5
  13.4 4.9 %all-to-all-done = s32[32,1,128]{2,1,0:T(1,128)S(1)} async-done(((s32[32,1,128]{2,1,0:T(1,128)}), s32[32,1,128]{2,1,0:T(1,128)S(1)}, u32[]{:S(2)}, u32[]{:S(2)}) %all-to-all-start) | async-done | bytes 16416 | tf_op jit(solution)/shard_map/all_to_all | solution.py:502
  18.3 2.5 %outbox.2 = bf16[32,256,128]{2,1,0:T(8,128)(2,1)} custom-call(s32[32,128]{1,0:T(8,128)S(1)} %bitcast.6, bf16[8,256,128]{2,1,0:T(8,128)(2,1)S(1)} %rows.1.orb_rows.refs_4_.refs_5_), custom_call_target="tpu_custom_call" | custom-call | bytes 6000000 | tf_op jit(solution)/shard_map/outbox/pallas_call | solution.py:527
  20.8 5.1 %all-to-all-start.1 = ((bf16[32,256,128]{2,1,0:T(8,128)(2,1)}), bf16[32,256,128]{2,1,0:T(8,128)(2,1)}, u32[]{:S(2)}, u32[]{:S(2)}) async-start(bf16[32,256,128]{2,1,0:T(8,128)(2,1)} %outbox.2), calls=%async_computation.1 | async-start | bytes 4194304 | tf_op jit(solution)/shard_map/all_to_all | solution.py:530
  26.1 0.1 divide_dynamic-update-slice_fusion.1
  26.9 1.0 base_forward.1
  27.9 1.7 %collective-permute-start = (bf16[512,128]{1,0:T(8,128)(2,1)S(1)}, bf16[512,128]{1,0:T(8,128)(2,1)S(1)}, u32[]{:S(2)}, u32[]{:S(2)}) collective-permute-start(bf16[512,128]{1,0:T(8,128)(2,1)S(1)} %get-tuple-element.43), channel_id=1, source_target_pairs={{0,1},{1,0},{2,3},{3,2},{4,5},{5,4},{6,7},{7,6},{8,9},{9,8},{10,11... | collective-permute-start | bytes 393224 | tf_op jit(solution)/shard_map/ppermute | solution.py:514
  29.7 3.5 %collective-permute-done.near = bf16[512,128]{1,0:T(8,128)(2,1)S(1)} collective-permute-done((bf16[512,128]{1,0:T(8,128)(2,1)S(1)}, bf16[512,128]{1,0:T(8,128)(2,1)S(1)}, u32[]{:S(2)}, u32[]{:S(2)}) %collective-permute-start) | collective-permute-done | bytes 131104 | tf_op jit(solution)/shard_map/ppermute | solution.py:514
  33.2 6.6 %collective-permute-start.1 = (bf16[8,32,128]{2,1,0:T(8,128)(2,1)S(1)}, bf16[8,32,128]{2,1,0:T(8,128)(2,1)S(1)}, u32[]{:S(2)}, u32[]{:S(2)}) collective-permute-start(bf16[8,32,128]{2,1,0:T(8,128)(2,1)S(1)} %get-tuple-element.45), channel_id=1, source_target_pairs={{0,4},{1,5},{2,6},{3,7},{4,0},{5,1},{6,2},{7,3},{8,12},{9,13},{10,... | collective-permute-start | bytes 196616 | tf_op jit(solution)/shard_map/ppermute | solution.py:510
  39.8 1.2 collective-permute-start.2
  41.0 2.4 %collective-permute-start.3 = (bf16[8,32,128]{2,1,0:T(8,128)(2,1)S(1)}, bf16[8,32,128]{2,1,0:T(8,128)(2,1)S(1)}, u32[]{:S(2)}, u32[]{:S(2)}) collective-permute-start(bf16[8,32,128]{2,1,0:T(8,128)(2,1)S(1)} %get-tuple-element.47), channel_id=1, source_target_pairs={{0,6},{1,7},{2,0},{3,1},{4,2},{5,3},{6,4},{7,5},{8,14},{9,15},{10,... | collective-permute-start | bytes 196616 | tf_op jit(solution)/shard_map/ppermute | solution.py:510
  43.4 1.2 outbox.3
  44.6 1.3 copy-done
  46.0 0.6 collective-permute-done.3.refs_2_
  46.6 1.6 base_inverse.1.refs_9_
  48.2 6.3 %all-to-all-done.1.fetched = bf16[32,256,128]{2,1,0:T(8,128)(2,1)} async-done(((bf16[32,256,128]{2,1,0:T(8,128)(2,1)}), bf16[32,256,128]{2,1,0:T(8,128)(2,1)}, u32[]{:S(2)}, u32[]{:S(2)}) %all-to-all-start.1) | async-done | bytes 2097184 | tf_op jit(solution)/shard_map/all_to_all | solution.py:530
  54.4 5.2 %all-to-all-start.2 = ((bf16[32,256,128]{2,1,0:T(8,128)(2,1)}), bf16[32,256,128]{2,1,0:T(8,128)(2,1)}, u32[]{:S(2)}, u32[]{:S(2)}) async-start(bf16[32,256,128]{2,1,0:T(8,128)(2,1)} %copy-done), calls=%async_computation.2 | async-start | bytes 4194304 | tf_op jit(solution)/shard_map/all_to_all | solution.py:539
  59.7 2.9 %pair_forward.2 = (bf16[8,256,128]{2,1,0:T(8,128)(2,1)S(1)}, f32[8,256,128]{2,1,0:T(8,128)S(1)}, f32[8,64,128]{2,1,0:T(8,128)S(1)}, bf16[512,128]{1,0:T(8,128)(2,1)S(1)}) custom-call(s32[8]{0:T(128)S(1)} %get-tuple-element.88.perm, s32[2,16]{1,0:T(2,128)S(1)} %copy-done.8, s32[2,256]{1,0:T(2,128)S(1)} %copy-done.6, ...), custom_call_target="tpu_custom_call" | custom-call | bytes 12000000 | tf_op jit(solution)/shard_map/pair_forward/pallas_call | solution.py:544
  62.6 1.7 %collective-permute-start.4 = (bf16[512,128]{1,0:T(8,128)(2,1)S(1)}, bf16[512,128]{1,0:T(8,128)(2,1)S(1)}, u32[]{:S(2)}, u32[]{:S(2)}) collective-permute-start(bf16[512,128]{1,0:T(8,128)(2,1)S(1)} %get-tuple-element.50), channel_id=1, source_target_pairs={{0,1},{1,0},{2,3},{3,2},{4,5},{5,4},{6,7},{7,6},{8,9},{9,8},{10,11... | collective-permute-start | bytes 393224 | tf_op jit(solution)/shard_map/ppermute | solution.py:514
  64.3 3.5 %collective-permute-done.4.near = bf16[512,128]{1,0:T(8,128)(2,1)S(1)} collective-permute-done((bf16[512,128]{1,0:T(8,128)(2,1)S(1)}, bf16[512,128]{1,0:T(8,128)(2,1)S(1)}, u32[]{:S(2)}, u32[]{:S(2)}) %collective-permute-start.4) | collective-permute-done | bytes 131104 | tf_op jit(solution)/shard_map/ppermute | solution.py:514
  67.9 6.6 %collective-permute-start.5 = (bf16[8,32,128]{2,1,0:T(8,128)(2,1)S(1)}, bf16[8,32,128]{2,1,0:T(8,128)(2,1)S(1)}, u32[]{:S(2)}, u32[]{:S(2)}) collective-permute-start(bf16[8,32,128]{2,1,0:T(8,128)(2,1)S(1)} %get-tuple-element.52), channel_id=1, source_target_pairs={{0,4},{1,5},{2,6},{3,7},{4,0},{5,1},{6,2},{7,3},{8,12},{9,13},{10,... | collective-permute-start | bytes 196616 | tf_op jit(solution)/shard_map/ppermute | solution.py:510
  74.5 1.2 collective-permute-start.6
  75.7 2.4 %collective-permute-start.7 = (bf16[8,32,128]{2,1,0:T(8,128)(2,1)S(1)}, bf16[8,32,128]{2,1,0:T(8,128)(2,1)S(1)}, u32[]{:S(2)}, u32[]{:S(2)}) collective-permute-start(bf16[8,32,128]{2,1,0:T(8,128)(2,1)S(1)} %get-tuple-element.54), channel_id=1, source_target_pairs={{0,6},{1,7},{2,0},{3,1},{4,2},{5,3},{6,4},{7,5},{8,14},{9,15},{10,... | collective-permute-start | bytes 196616 | tf_op jit(solution)/shard_map/ppermute | solution.py:510
  78.1 2.6 %collective-permute-done.6.refs_1_ = bf16[8,32,128]{2,1,0:T(8,128)(2,1)S(1)} collective-permute-done((bf16[8,32,128]{2,1,0:T(8,128)(2,1)S(1)}, bf16[8,32,128]{2,1,0:T(8,128)(2,1)S(1)}, u32[]{:S(2)}, u32[]{:S(2)}) %collective-permute-start.6) | collective-permute-done | bytes 65568 | tf_op jit(solution)/shard_map/ppermute | solution.py:510
  80.7 0.6 collective-permute-done.7.refs_2_
  81.2 2.7 %pair_inverse.2 = (f32[8,256,128]{2,1,0:T(8,128)S(1)}, bf16[32,256,128]{2,1,0:T(8,128)(2,1)S(1)}) custom-call(s32[1]{0:T(128)} %bitcast.1.grid, s32[8]{0:T(128)S(1)} %get-tuple-element.88.perm, s32[2,16]{1,0:T(2,128)S(1)} %copy-done.8, s32[2,256]{1,0:T(2,128)S(1)} %copy-done.6, ...), custom_call_target="tpu_custom_call", output_to_operand_aliasing={{0}: (14, {})} | custom-call | bytes 15000000 | tf_op jit(solution)/shard_map/pair_inverse/pallas_call | solution.py:554
  83.9 1.4 copy-done.3
  85.3 2.8 %all-to-all-done.2.fetched = bf16[32,256,128]{2,1,0:T(8,128)(2,1)} async-done(((bf16[32,256,128]{2,1,0:T(8,128)(2,1)}), bf16[32,256,128]{2,1,0:T(8,128)(2,1)}, u32[]{:S(2)}, u32[]{:S(2)}) %all-to-all-start.2) | async-done | bytes 2097184 | tf_op jit(solution)/shard_map/all_to_all | solution.py:539
  88.1 6.0 %all-to-all-start.3 = ((bf16[32,256,128]{2,1,0:T(8,128)(2,1)}), bf16[32,256,128]{2,1,0:T(8,128)(2,1)}, u32[]{:S(2)}, u32[]{:S(2)}) async-start(bf16[32,256,128]{2,1,0:T(8,128)(2,1)} %copy-done.3), calls=%async_computation.3 | async-start | bytes 4194304 | tf_op jit(solution)/shard_map/all_to_all | solution.py:566
  94.0 3.0 %pair_forward.3 = (bf16[8,256,128]{2,1,0:T(8,128)(2,1)S(1)}, f32[8,256,128]{2,1,0:T(8,128)S(1)}, f32[8,64,128]{2,1,0:T(8,128)S(1)}, bf16[528,128]{1,0:T(8,128)(2,1)S(1)}, f32[8,128]{1,0:T(8,128)S(1)}) custom-call(s32[8]{0:T(128)S(1)} %get-tuple-element.89.perm, s32[2,16]{1,0:T(2,128)S(1)} %copy-done.8, s32[2,256]{1,0:T(2,128)S(1)} %copy-done.6, ...), custom_call_target="tpu_custom_call" | custom-call | bytes 12000000 | tf_op jit(solution)/shard_map/pair_forward/pallas_call | solution.py:544
  97.0 1.3 collective-permute-start.8
  98.3 3.8 %collective-permute-done.8.near = bf16[528,128]{1,0:T(8,128)(2,1)S(1)} collective-permute-done((bf16[528,128]{1,0:T(8,128)(2,1)S(1)}, bf16[528,128]{1,0:T(8,128)(2,1)S(1)}, u32[]{:S(2)}, u32[]{:S(2)}) %collective-permute-start.8) | collective-permute-done | bytes 135200 | tf_op jit(solution)/shard_map/ppermute | solution.py:514
  102.2 5.2 %collective-permute-start.11 = (bf16[528,128]{1,0:T(8,128)(2,1)S(1)}, bf16[528,128]{1,0:T(8,128)(2,1)S(1)}, u32[]{:S(2)}, u32[]{:S(2)}) collective-permute-start(bf16[528,128]{1,0:T(8,128)(2,1)S(1)} %pair_up_whole.1.refs_0_), channel_id=1, source_target_pairs={{0,6},{1,7},{2,0},{3,1},{4,2},{5,3},{6,4},{7,5},{8,14},{9,15},{10,... | collective-permute-start | bytes 405512 | tf_op jit(solution)/shard_map/ppermute | solution.py:510
  107.4 1.0 collective-permute-start.10
  108.4 2.3 %collective-permute-start.9 = (bf16[528,128]{1,0:T(8,128)(2,1)S(1)}, bf16[528,128]{1,0:T(8,128)(2,1)S(1)}, u32[]{:S(2)}, u32[]{:S(2)}) collective-permute-start(bf16[528,128]{1,0:T(8,128)(2,1)S(1)} %pair_up_whole.1.refs_0_), channel_id=1, source_target_pairs={{0,2},{1,3},{2,4},{3,5},{4,6},{5,7},{6,0},{7,1},{8,10},{9,11},{10,... | collective-permute-start | bytes 405512 | tf_op jit(solution)/shard_map/ppermute | solution.py:510
  110.7 7.7 %collective-permute-done.10.refs_2_ = bf16[528,128]{1,0:T(8,128)(2,1)S(1)} collective-permute-done((bf16[528,128]{1,0:T(8,128)(2,1)S(1)}, bf16[528,128]{1,0:T(8,128)(2,1)S(1)}, u32[]{:S(2)}, u32[]{:S(2)}) %collective-permute-start.10) | collective-permute-done | bytes 135200 | tf_op jit(solution)/shard_map/ppermute | solution.py:510
  118.3 0.4 collective-permute-done.9.refs_1_
  118.8 2.9 %pair_inverse.3 = (f32[8,256,128]{2,1,0:T(8,128)S(1)}, bf16[32,272,128]{2,1,0:T(8,128)(2,1)S(1)}) custom-call(s32[1]{0:T(128)} %bitcast.1.grid, s32[8]{0:T(128)S(1)} %get-tuple-element.89.perm, s32[2,16]{1,0:T(2,128)S(1)} %copy-done.8, s32[2,256]{1,0:T(2,128)S(1)} %copy-done.6, ...), custom_call_target="tpu_custom_call", output_to_operand_aliasing={{0}: (15, {})} | custom-call | bytes 15000000 | tf_op jit(solution)/shard_map/pair_inverse/pallas_call | solution.py:554
  121.7 1.4 copy-done.2
  123.1 9.7 %all-to-all-start.4 = ((bf16[32,272,128]{2,1,0:T(8,128)(2,1)}), bf16[32,272,128]{2,1,0:T(8,128)(2,1)}, u32[]{:S(2)}, u32[]{:S(2)}) async-start(bf16[32,272,128]{2,1,0:T(8,128)(2,1)} %copy-done.2), calls=%async_computation.4 | async-start | bytes 4456448 | tf_op jit(solution)/shard_map/all_to_all | solution.py:569
  132.8 0.2 slice_reduce_fusion
  133.0 2.4 %add.1090 = (f32[8,256,128]{2,1,0:T(8,128)S(1)}, f32[8,128]{1,0:T(8,128)S(1)}) custom-call(s32[32]{0:T(128)S(1)} %get-tuple-element.78.asked, bf16[32,256,128]{2,1,0:T(8,128)(2,1)} %all-to-all-done.3.arrived, bf16[8,256,128]{2,1,0:T(8,128)(2,1)S(1)} %rows.1.orb_rows.refs_4_.refs_5_, ...), custom_call_target="tpu_custom_call", output_to_operand_aliasing={{0}: (3, {})} | custom-call | bytes 6000000 | tf_op jit(solution)/shard_map/add/pallas_call | solution.py:570
  135.3 16.9 %psum.7.energy_in = f32[8,128]{1,0:T(8,128)S(1)} all-reduce(f32[8,128]{1,0:T(8,128)S(1)} %get-tuple-element.72), channel_id=1, replica_groups=mesh['orb'=32,'grid'=8] {'grid'}, use_global_device_ids=true, to_apply=%region_0.1 | all-reduce | flops 1024 | bytes 8192 | tf_op jit(solution)/shard_map/psum | solution.py:573
  152.2 10.3 %all-to-all-done.4.arrived = bf16[32,272,128]{2,1,0:T(8,128)(2,1)} async-done(((bf16[32,272,128]{2,1,0:T(8,128)(2,1)}), bf16[32,272,128]{2,1,0:T(8,128)(2,1)}, u32[]{:S(2)}, u32[]{:S(2)}) %all-to-all-start.4) | async-done | bytes 2228256 | tf_op jit(solution)/shard_map/all_to_all | solution.py:569
  162.5 2.9 %finish.1 = (bf16[8,8,4096]{2,1,0:T(8,128)(2,1)}, f32[8]{0:T(128)}) custom-call(s32[32]{0:T(128)S(1)} %get-tuple-element.74.asked, bf16[32,272,128]{2,1,0:T(8,128)(2,1)} %all-to-all-done.4.arrived, f32[8,256,128]{2,1,0:T(8,128)S(1)} %get-tuple-element.76.total_in, f32[8,128]{1,0:T(8,128)S(1)} %psum.7.energy_in), custom_call_target="tpu_custom_call" | custom-call | bytes 9000000 | tf_op jit(solution)/shard_map/finish/pallas_call | solution.py:575
  (46 shorter events, 1.9 us)
Async XLA Ops:
  0.6 0.7 copy-start.7
  2.8 15.5 %all-to-all-start = ((s32[32,1,128]{2,1,0:T(1,128)}), s32[32,1,128]{2,1,0:T(1,128)S(1)}, u32[]{:S(2)}, u32[]{:S(2)}) async-start(s32[32,1,128]{2,1,0:T(1,128)} %get-tuple-element.40), calls=%async_computation | async-start | bytes 32768 | tf_op jit(solution)/shard_map/all_to_all | solution.py:502
  12.3 1.0 copy-start.5
  20.8 6.0 %copy-start.1 = (bf16[256,256]{1,0:T(8,128)(2,1)S(1)}, bf16[256,256]{1,0:T(8,128)(2,1)}, u32[]{:S(2)}) copy-start(bf16[256,256]{1,0:T(8,128)(2,1)} %constant.144.clone.y_right.refs_5_.refs_6_.refs_7_) | copy-start | bytes 393220
  20.8 6.1 %copy-start.4 = (bf16[64,192]{1,0:T(8,128)(2,1)S(1)}, bf16[64,192]{1,0:T(8,128)(2,1)}, u32[]{:S(2)}) copy-start(bf16[64,192]{1,0:T(8,128)(2,1)} %constant.145.clone.x_left.refs_6_.refs_7_.refs_8_) | copy-start | bytes 73732
  20.8 33.6 %all-to-all-start.1 = ((bf16[32,256,128]{2,1,0:T(8,128)(2,1)}), bf16[32,256,128]{2,1,0:T(8,128)(2,1)}, u32[]{:S(2)}, u32[]{:S(2)}) async-start(bf16[32,256,128]{2,1,0:T(8,128)(2,1)} %outbox.2), calls=%async_computation.1 | async-start | bytes 4194304 | tf_op jit(solution)/shard_map/all_to_all | solution.py:530
  27.9 5.2 %collective-permute-start = (bf16[512,128]{1,0:T(8,128)(2,1)S(1)}, bf16[512,128]{1,0:T(8,128)(2,1)S(1)}, u32[]{:S(2)}, u32[]{:S(2)}) collective-permute-start(bf16[512,128]{1,0:T(8,128)(2,1)S(1)} %get-tuple-element.43), channel_id=1, source_target_pairs={{0,1},{1,0},{2,3},{3,2},{4,5},{5,4},{6,7},{7,6},{8,9},{9,8},{10,11... | collective-permute-start | bytes 393224 | tf_op jit(solution)/shard_map/ppermute | solution.py:514
  33.2 12.7 %collective-permute-start.1 = (bf16[8,32,128]{2,1,0:T(8,128)(2,1)S(1)}, bf16[8,32,128]{2,1,0:T(8,128)(2,1)S(1)}, u32[]{:S(2)}, u32[]{:S(2)}) collective-permute-start(bf16[8,32,128]{2,1,0:T(8,128)(2,1)S(1)} %get-tuple-element.45), channel_id=1, source_target_pairs={{0,4},{1,5},{2,6},{3,7},{4,0},{5,1},{6,2},{7,3},{8,12},{9,13},{10,... | collective-permute-start | bytes 196616 | tf_op jit(solution)/shard_map/ppermute | solution.py:510
  39.8 6.2 %collective-permute-start.2 = (bf16[8,32,128]{2,1,0:T(8,128)(2,1)S(1)}, bf16[8,32,128]{2,1,0:T(8,128)(2,1)S(1)}, u32[]{:S(2)}, u32[]{:S(2)}) collective-permute-start(bf16[8,32,128]{2,1,0:T(8,128)(2,1)S(1)} %get-tuple-element.46), channel_id=1, source_target_pairs={{0,2},{1,3},{2,4},{3,5},{4,6},{5,7},{6,0},{7,1},{8,10},{9,11},{10,... | collective-permute-start | bytes 196616 | tf_op jit(solution)/shard_map/ppermute | solution.py:510
  41.0 5.5 %collective-permute-start.3 = (bf16[8,32,128]{2,1,0:T(8,128)(2,1)S(1)}, bf16[8,32,128]{2,1,0:T(8,128)(2,1)S(1)}, u32[]{:S(2)}, u32[]{:S(2)}) collective-permute-start(bf16[8,32,128]{2,1,0:T(8,128)(2,1)S(1)} %get-tuple-element.47), channel_id=1, source_target_pairs={{0,6},{1,7},{2,0},{3,1},{4,2},{5,3},{6,4},{7,5},{8,14},{9,15},{10,... | collective-permute-start | bytes 196616 | tf_op jit(solution)/shard_map/ppermute | solution.py:510
  44.6 1.3 copy-start
  48.1 11.6 %copy-start.6 = (s32[2,256]{1,0:T(2,128)S(1)}, s32[2,256]{1,0:T(2,128)}, u32[]{:S(2)}) copy-start(s32[2,256]{1,0:T(2,128)} %anchor.7) | copy-start | bytes 6148
  48.1 11.6 %copy-start.8 = (s32[2,16]{1,0:T(2,128)S(1)}, s32[2,16]{1,0:T(2,128)}, u32[]{:S(2)}) copy-start(s32[2,16]{1,0:T(2,128)} %pairs.9) | copy-start | bytes 388
  54.4 33.7 %all-to-all-start.2 = ((bf16[32,256,128]{2,1,0:T(8,128)(2,1)}), bf16[32,256,128]{2,1,0:T(8,128)(2,1)}, u32[]{:S(2)}, u32[]{:S(2)}) async-start(bf16[32,256,128]{2,1,0:T(8,128)(2,1)} %copy-done), calls=%async_computation.2 | async-start | bytes 4194304 | tf_op jit(solution)/shard_map/all_to_all | solution.py:539
  62.6 5.2 %collective-permute-start.4 = (bf16[512,128]{1,0:T(8,128)(2,1)S(1)}, bf16[512,128]{1,0:T(8,128)(2,1)S(1)}, u32[]{:S(2)}, u32[]{:S(2)}) collective-permute-start(bf16[512,128]{1,0:T(8,128)(2,1)S(1)} %get-tuple-element.50), channel_id=1, source_target_pairs={{0,1},{1,0},{2,3},{3,2},{4,5},{5,4},{6,7},{7,6},{8,9},{9,8},{10,11... | collective-permute-start | bytes 393224 | tf_op jit(solution)/shard_map/ppermute | solution.py:514
  67.9 10.2 %collective-permute-start.5 = (bf16[8,32,128]{2,1,0:T(8,128)(2,1)S(1)}, bf16[8,32,128]{2,1,0:T(8,128)(2,1)S(1)}, u32[]{:S(2)}, u32[]{:S(2)}) collective-permute-start(bf16[8,32,128]{2,1,0:T(8,128)(2,1)S(1)} %get-tuple-element.52), channel_id=1, source_target_pairs={{0,4},{1,5},{2,6},{3,7},{4,0},{5,1},{6,2},{7,3},{8,12},{9,13},{10,... | collective-permute-start | bytes 196616 | tf_op jit(solution)/shard_map/ppermute | solution.py:510
  74.5 6.2 %collective-permute-start.6 = (bf16[8,32,128]{2,1,0:T(8,128)(2,1)S(1)}, bf16[8,32,128]{2,1,0:T(8,128)(2,1)S(1)}, u32[]{:S(2)}, u32[]{:S(2)}) collective-permute-start(bf16[8,32,128]{2,1,0:T(8,128)(2,1)S(1)} %get-tuple-element.53), channel_id=1, source_target_pairs={{0,2},{1,3},{2,4},{3,5},{4,6},{5,7},{6,0},{7,1},{8,10},{9,11},{10,... | collective-permute-start | bytes 196616 | tf_op jit(solution)/shard_map/ppermute | solution.py:510
  75.7 5.5 %collective-permute-start.7 = (bf16[8,32,128]{2,1,0:T(8,128)(2,1)S(1)}, bf16[8,32,128]{2,1,0:T(8,128)(2,1)S(1)}, u32[]{:S(2)}, u32[]{:S(2)}) collective-permute-start(bf16[8,32,128]{2,1,0:T(8,128)(2,1)S(1)} %get-tuple-element.54), channel_id=1, source_target_pairs={{0,6},{1,7},{2,0},{3,1},{4,2},{5,3},{6,4},{7,5},{8,14},{9,15},{10,... | collective-permute-start | bytes 196616 | tf_op jit(solution)/shard_map/ppermute | solution.py:510
  83.9 1.4 copy-start.3
  88.1 35.0 %all-to-all-start.3 = ((bf16[32,256,128]{2,1,0:T(8,128)(2,1)}), bf16[32,256,128]{2,1,0:T(8,128)(2,1)}, u32[]{:S(2)}, u32[]{:S(2)}) async-start(bf16[32,256,128]{2,1,0:T(8,128)(2,1)} %copy-done.3), calls=%async_computation.3 | async-start | bytes 4194304 | tf_op jit(solution)/shard_map/all_to_all | solution.py:566
  97.0 5.1 %collective-permute-start.8 = (bf16[528,128]{1,0:T(8,128)(2,1)S(1)}, bf16[528,128]{1,0:T(8,128)(2,1)S(1)}, u32[]{:S(2)}, u32[]{:S(2)}) collective-permute-start(bf16[528,128]{1,0:T(8,128)(2,1)S(1)} %get-tuple-element.61), channel_id=1, source_target_pairs={{0,1},{1,0},{2,3},{3,2},{4,5},{5,4},{6,7},{7,6},{8,9},{9,8},{10,11... | collective-permute-start | bytes 405512 | tf_op jit(solution)/shard_map/ppermute | solution.py:514
  102.2 8.5 %collective-permute-start.11 = (bf16[528,128]{1,0:T(8,128)(2,1)S(1)}, bf16[528,128]{1,0:T(8,128)(2,1)S(1)}, u32[]{:S(2)}, u32[]{:S(2)}) collective-permute-start(bf16[528,128]{1,0:T(8,128)(2,1)S(1)} %pair_up_whole.1.refs_0_), channel_id=1, source_target_pairs={{0,6},{1,7},{2,0},{3,1},{4,2},{5,3},{6,4},{7,5},{8,14},{9,15},{10,... | collective-permute-start | bytes 405512 | tf_op jit(solution)/shard_map/ppermute | solution.py:510
  107.4 10.9 %collective-permute-start.10 = (bf16[528,128]{1,0:T(8,128)(2,1)S(1)}, bf16[528,128]{1,0:T(8,128)(2,1)S(1)}, u32[]{:S(2)}, u32[]{:S(2)}) collective-permute-start(bf16[528,128]{1,0:T(8,128)(2,1)S(1)} %pair_up_whole.1.refs_0_), channel_id=1, source_target_pairs={{0,4},{1,5},{2,6},{3,7},{4,0},{5,1},{6,2},{7,3},{8,12},{9,13},{10,... | collective-permute-start | bytes 405512 | tf_op jit(solution)/shard_map/ppermute | solution.py:510
  108.4 10.4 %collective-permute-start.9 = (bf16[528,128]{1,0:T(8,128)(2,1)S(1)}, bf16[528,128]{1,0:T(8,128)(2,1)S(1)}, u32[]{:S(2)}, u32[]{:S(2)}) collective-permute-start(bf16[528,128]{1,0:T(8,128)(2,1)S(1)} %pair_up_whole.1.refs_0_), channel_id=1, source_target_pairs={{0,2},{1,3},{2,4},{3,5},{4,6},{5,7},{6,0},{7,1},{8,10},{9,11},{10,... | collective-permute-start | bytes 405512 | tf_op jit(solution)/shard_map/ppermute | solution.py:510
  121.7 1.4 copy-start.2
  123.1 39.4 %all-to-all-start.4 = ((bf16[32,272,128]{2,1,0:T(8,128)(2,1)}), bf16[32,272,128]{2,1,0:T(8,128)(2,1)}, u32[]{:S(2)}, u32[]{:S(2)}) async-start(bf16[32,272,128]{2,1,0:T(8,128)(2,1)} %copy-done.2), calls=%async_computation.4 | async-start | bytes 4456448 | tf_op jit(solution)/shard_map/all_to_all | solution.py:569

commit v2 on v0

v2 whole, which is shorter than its diff:
```python
import functools

import jax
import jax.numpy as jnp
import ml_dtypes
import numpy as np
from jax import lax
from jax.experimental import pallas as pl
from jax.experimental.pallas import tpu as pltpu
from jax.sharding import PartitionSpec as P

BOX = 64
LANES = 128
TILES = BOX * BOX // LANES
PLANES = 8
ROWS = TILES * PLANES
GRID = 8
PAIRS = GRID // 2
ORDER = (2, 1, 3)
UP, DOWN, MIDDLE, CARRY, PAST_UP, PAST_DOWN = 0, 8, 16, 24, 27, 28
ORB_DEV = 8
ENTRIES = 16
PAD = 10
MU2 = 0.02
BF16 = jnp.bfloat16
F32 = jnp.float32
VMEM_LIMIT = 40 * 1024 * 1024


def sine64():
    steps = np.arange(1, BOX + 1, dtype=np.float64)
    return np.sqrt(2.0 / (BOX + 1)) * np.sin(np.pi * steps[:, None] * steps[None, :] / (BOX + 1))


def high_low(table):
    high = table.astype(np.float32).astype(ml_dtypes.bfloat16)
    rest = table - high.astype(np.float64)
    return high, rest.astype(np.float32).astype(ml_dtypes.bfloat16)


def sine_factors():
    sine = sine64()
    zero = np.zeros((BOX, BOX))
    high, low = high_low(np.block([[sine, zero], [zero, sine]]))
    y_right = np.concatenate(
        [np.concatenate([high, low], 1), np.concatenate([high, np.zeros_like(high)], 1)], 0
    )
    half = 2 * np.arange(TILES)
    rows = []
    for h in range(2):
        rows.append(np.concatenate([sine[np.ix_(half + h, half + h)], sine[np.ix_(half + h, half + 1 - h)]], 1))
    high, low = high_low(np.concatenate(rows, 0))
    return jnp.asarray(y_right), jnp.asarray(np.concatenate([high, high, low], 1))


def z_factors(grid_index):
    steps = jnp.arange(1, BOX + 1).astype(F32)
    eigen = 2.0 - 2.0 * jnp.cos(jnp.pi * steps / (BOX + 1))
    s = (eigen[:, None] + eigen[None, :] + MU2).reshape(TILES, LANES)[None]
    theta = jnp.log(1.0 + 0.5 * s + jnp.sqrt(s + 0.25 * s * s))

    def number(n):
        return jnp.asarray(n).reshape(-1).astype(F32)[:, None, None]

    def rest(n):
        return 1.0 - jnp.exp(-2.0 * theta * number(n))

    def fall(n):
        return jnp.exp(-theta * number(n))

    z = grid_index * PLANES + jnp.arange(PLANES)
    up = fall(1) * rest(z) / rest(z + 1)
    down = fall(1) * rest(63 - z) / rest(64 - z)
    scale = MU2 / (rest(1) * rest(65))
    middle = scale * fall(1) * rest(z + 1) * rest(64 - z)
    pair = grid_index // 2
    e = jnp.arange(1, PAIRS)
    other = (pair - e) % PAIRS
    below = e <= pair
    away = jnp.where(below, 8 * grid_index - 16 * other - 16, 16 * other - 8 * grid_index - 8)
    first = jnp.where(below, 16 * other + 16, 64 - 16 * other)
    last = jnp.where(below, 8 * grid_index, 56 - 8 * grid_index)
    carry = fall(away) * rest(first) / rest(last)
    edge = 16 * pair + 8
    past_up = fall(8) * rest(edge) / rest(edge + 8)
    past_down = fall(8) * rest(64 - edge) / rest(72 - edge)
    return jnp.concatenate([up, down, middle, carry, past_up, past_down], 0)


def lane_iota(rows):
    return lax.broadcasted_iota(jnp.int32, (rows, LANES), 1)


def split(value):
    high = value.astype(BF16)
    return high, (value - high.astype(F32)).astype(BF16)


def dot(left, right):
    return jnp.dot(left, right, preferred_element_type=F32)


def times_y(value, y_right):
    high, low = split(value)
    both = dot(jnp.concatenate([high, low], axis=1), y_right)
    return both[:, :LANES] + both[:, LANES:]


def times_x(planes, x_left, terms):
    value = jnp.concatenate(planes, axis=1)
    other = jnp.concatenate([pltpu.roll(p, BOX, 1) for p in planes], axis=1)
    data = jnp.concatenate([value, other], axis=0)
    if terms == 1:
        high = data.astype(BF16)
        both = dot(x_left[:, BOX:], jnp.concatenate([high, high], axis=0))
    else:
        high, low = split(data)
        both = dot(x_left, jnp.concatenate([high, low, high], axis=0))
    first = lane_iota(TILES) < BOX
    out = []
    for z in range(PLANES):
        tile = both[:, LANES * z : LANES * (z + 1)]
        out.append(jnp.where(first, tile[:TILES], tile[TILES:]))
    return out


def shifted(value, step_x, step_y, buffer):
    buffer[PAD * 8 : PAD * 8 + ROWS, :] = value
    flat = step_x * BOX + step_y
    tiles = flat >> 7
    lanes = flat & 127
    start = pl.multiple_of((tiles + PAD) * 8, 8)
    window = buffer[pl.ds(start, ROWS + 8), :]
    window = pltpu.roll(window, (LANES - lanes) & 127, 1)
    lane = lane_iota(ROWS)
    moved = jnp.where(lane < LANES - lanes, window[:ROWS], window[8:])
    y_new = (lane & (BOX - 1)) + step_y
    return jnp.where((y_new >= 0) & (y_new < BOX), moved, 0.0)


def clear_margins(buffer):
    zero = jnp.zeros((PAD * 8, LANES), F32)
    buffer[: PAD * 8, :] = zero
    buffer[PAD * 8 + ROWS :, :] = zero


def column_sums(value):
    return jnp.sum(value, axis=0, keepdims=True)


def forward(rho, tables, held, coeffs, ends, message, n):
    y_right, x_left, z_table = tables
    held[...] = times_y(rho, y_right[...])
    planes = times_x([held[pl.ds(z, TILES, stride=PLANES), :] for z in range(PLANES)], x_left[...], 1)
    for z in range(PLANES):
        coeffs[n, TILES * z : TILES * (z + 1), :] = planes[z]
    above = planes[0]
    for z in range(1, PLANES):
        above = z_table[UP + z] * above + planes[z]
    below = planes[PLANES - 1]
    for z in range(PLANES - 2, -1, -1):
        below = z_table[DOWN + z] * below + planes[z]
    both = jnp.concatenate([above, below], axis=0)
    ends[n] = both
    message[2 * TILES * n : 2 * TILES * (n + 1), :] = both.astype(BF16)


def halves(message, n):
    both = message[2 * TILES * n : 2 * TILES * (n + 1), :].astype(F32)
    return both[:TILES], both[TILES:]


def inverse(grid, near, sums, coeffs, tables, held, n):
    y_right, x_left, z_table = tables
    near_up, near_down = halves(near, n)
    upper = (grid & 1) == 1
    from_below = jnp.where(upper, near_up, 0.0)
    from_above = jnp.where(upper, 0.0, near_down)
    for e in range(1, PAIRS):
        below = e <= (grid >> 1)
        term = z_table[CARRY + e - 1] * sums[e - 1]
        from_below += jnp.where(below, term, 0.0)
        from_above += jnp.where(below, 0.0, term)
    planes = [coeffs[n, TILES * z : TILES * (z + 1), :] for z in range(PLANES)]
    ups = []
    for z in range(PLANES):
        from_below = z_table[UP + z] * from_below + planes[z]
        ups.append(from_below)
    solved = [None] * PLANES
    product = jnp.zeros((TILES, LANES), F32)
    for z in range(PLANES - 1, -1, -1):
        carried = z_table[DOWN + z] * from_above
        solved[z] = z_table[MIDDLE + z] * (ups[z] + carried)
        from_above = planes[z] + carried
        product += planes[z] * solved[z]
    full = times_y(jnp.concatenate(times_x(solved, x_left[...], 2), axis=0), y_right[...])
    for z in range(PLANES):
        held[pl.ds(z, TILES, stride=PLANES), :] = full[TILES * z : TILES * (z + 1)]
    return held[...], column_sums(product)


def pair_scalars(pairs, anchor, n):
    owner = pairs[0, n]
    mate = jnp.maximum(pairs[1, n], 0)
    step_x = anchor[0, owner] - anchor[0, mate]
    step_y = anchor[1, owner] - anchor[1, mate]
    return pairs[1, n] >= 0, owner & (ORB_DEV - 1), step_x, step_y


def tile(box, t):
    return box[PLANES * t : PLANES * (t + 1)]


def spread_kernel(pairs, orb, orb_rows, out):
    wide = [orb[n].astype(F32) for n in range(ORB_DEV)]
    for n in range(ORB_DEV):
        box = jnp.concatenate([wide[n][:, LANES * t : LANES * (t + 1)] for t in range(TILES)], axis=0)
        orb_rows[n] = box.astype(BF16)
    rows = lax.broadcasted_iota(jnp.int32, (ENTRIES, LANES), 0)
    partners = jnp.zeros((ENTRIES, LANES), F32)
    for n in range(ENTRIES):
        partners = jnp.where(rows == n, pairs[1, n].astype(F32), partners)
    partners = partners.astype(BF16)
    for t in range(TILES):
        piece = jnp.concatenate([w[:, LANES * t : LANES * (t + 1)] for w in wide], axis=0)
        out[t, : ORB_DEV * PLANES, :] = piece.astype(BF16)
        out[t, ORB_DEV * PLANES :, :] = partners


def serve_kernel(partners, held, out, every):
    count = held.shape[0]
    for d in range(count):
        pieces = held[d, : ORB_DEV * PLANES, :].astype(F32)
        for n in range(ORB_DEV):
            every[ORB_DEV * d + n] = tile(pieces, n)

    def step(d, carry):
        pieces = [every[jnp.maximum(partners[ENTRIES * d + n], 0)] for n in range(ENTRIES)]
        out[d] = jnp.concatenate(pieces, axis=0).astype(BF16)
        return carry

    lax.fori_loop(0, count, step, 0)


def base_forward_kernel(orb_rows, y_right, x_left, z_table, coeffs, ends, message, *held):
    for n in range(ORB_DEV):
        box = orb_rows[n].astype(F32)
        forward(box * box, (y_right, x_left, z_table), held[n], coeffs, ends, message, n)


def pair_forward_kernel(pairs, anchor, orb_rows, fetched, y_right, x_left, z_table, moved_out, coeffs, ends, message, *refs):
    buffers, held = refs[:ENTRIES], refs[ENTRIES:]
    for n in range(ENTRIES):
        clear_margins(buffers[n])
    for m in range(0, ENTRIES, 2):
        both = [fetched[t, PLANES * m : PLANES * (m + 2), :].astype(F32) for t in range(TILES)]
        for n in (m, m + 1):
            _, owner, step_x, step_y = pair_scalars(pairs, anchor, n)
            mate = jnp.concatenate([tile(b, n - m) for b in both], axis=0)
            moved = shifted(mate, step_x, step_y, buffers[n])
            moved_out[n] = moved.astype(BF16)
            rho = orb_rows[owner].astype(F32) * moved
            forward(rho, (y_right, x_left, z_table), held[n], coeffs, ends, message, n)


def pair_up_kernel(grid, ends, near, z_table, *outs):
    pair, upper = grid[0] >> 1, (grid[0] & 1) == 1
    for n in range(ends.shape[0]):
        near_up, near_down = halves(near, n)
        mine = ends[n]
        mine_up, mine_down = mine[:TILES], mine[TILES:]
        low_up = jnp.where(upper, near_up, mine_up)
        high_up = jnp.where(upper, mine_up, near_up)
        low_down = jnp.where(upper, near_down, mine_down)
        high_down = jnp.where(upper, mine_down, near_down)
        up = (z_table[PAST_UP] * low_up + high_up).astype(BF16)
        down = (low_down + z_table[PAST_DOWN] * high_down).astype(BF16)
        for e in range(1, PAIRS):
            outs[e - 1][n] = jnp.where(pair + e < PAIRS, up, down)


def in_order(refs, n):
    return [refs[ORDER.index(e)][n].astype(F32) for e in range(1, PAIRS)]


def base_inverse_kernel(grid, near, *refs):
    sums, refs = refs[: PAIRS - 1], refs[PAIRS - 1 :]
    coeffs, orb_rows, y_right, x_left, z_table, total, energy, *held = refs
    tables = (y_right, x_left, z_table)
    for n in range(ORB_DEV):
        potential, value = inverse(grid[0], near, in_order(sums, n), coeffs, tables, held[n], n)
        total[n] = orb_rows[n].astype(F32) * potential
        energy[n : n + 1, :] = value


def pair_inverse_kernel(grid, pairs, anchor, near, *refs):
    sums, refs = refs[: PAIRS - 1], refs[PAIRS - 1 :]
    coeffs, orb_rows, moved, y_right, x_left, z_table, total_in, total, energy, out, *refs = refs
    buffers, held = refs[:ENTRIES], refs[ENTRIES:]
    tables = (y_right, x_left, z_table)
    for n in range(ENTRIES):
        clear_margins(buffers[n])
    total[...] = total_in[...]
    for m in range(0, ENTRIES, 2):
        backs = []
        for n in (m, m + 1):
            _, owner, step_x, step_y = pair_scalars(pairs, anchor, n)
            potential, value = inverse(grid[0], near, in_order(sums, n), coeffs, tables, held[n], n)
            energy[n : n + 1, :] = value
            backs.append(shifted(orb_rows[owner].astype(F32) * potential, -step_x, -step_y, buffers[n]))
        for t in range(TILES):
            piece = jnp.concatenate([tile(back, t) for back in backs], axis=0)
            out[t, PLANES * m : PLANES * (m + 2), :] = piece.astype(BF16)
    for n in range(ENTRIES):
        live, owner, _, _ = pair_scalars(pairs, anchor, n)
        total[owner] += jnp.where(live, moved[n].astype(F32) * held[n][...], 0.0)


def gather_kernel(partners, pairs, arrived, energy, out, energy_here, every_energy, *every):
    count = arrived.shape[0]
    spare = ORB_DEV * count
    for part in every:
        part[...] = jnp.zeros_like(part)

    def step(d, carry):
        for m in range(0, ENTRIES, 2):
            both = arrived[d, PLANES * m : PLANES * (m + 2), :].astype(F32)
            for n in (m, m + 1):
                which = partners[ENTRIES * d + n]
                which = jnp.where(which >= 0, which, spare)
                every[n % len(every)][which] += tile(both, n - m)
        return carry

    lax.fori_loop(0, count, step, 0)
    every_energy[...] = jnp.zeros_like(every_energy)
    first = lane_iota(1) == 0
    for n in range(ORB_DEV):
        energy_here[n : n + 1, :] = jnp.where(first, energy[n], 0.0)
    for n in range(ENTRIES):
        mate = pairs[1, n]
        owner = pairs[0, n] & (ORB_DEV - 1)
        value = jnp.where(first & (mate >= 0), energy[ORB_DEV + n], 0.0)
        every_energy[pl.ds(jnp.where(mate >= 0, mate, spare), 1), :] += value
        energy_here[pl.ds(owner, 1), :] += value
    for d in range(count):
        pieces = [sum(part[ORB_DEV * d + n] for part in every) for n in range(ORB_DEV)]
        out[d, : ORB_DEV * PLANES, :] = jnp.concatenate(pieces, axis=0).astype(BF16)
        value = every_energy[ORB_DEV * d : ORB_DEV * (d + 1), :]
        high = value.astype(BF16).astype(F32)
        out[d, ORB_DEV * PLANES :, :] = jnp.concatenate([high, value - high], axis=0).astype(BF16)


def finish_kernel(arrived, total, energy, out, energy_out):
    sums = energy[...]
    for t in range(TILES):
        pieces = arrived[t, : ORB_DEV * PLANES, :].astype(F32)
        for n in range(ORB_DEV):
            here = total[n, PLANES * t : PLANES * (t + 1), :] + tile(pieces, n)
            out[n, :, LANES * t : LANES * (t + 1)] = here.astype(BF16)
        both = arrived[t, ORB_DEV * PLANES :, :].astype(F32)
        sums += both[:ORB_DEV] + both[ORB_DEV:]
    for n in range(ORB_DEV):
        energy_out[n] = jnp.sum(sums[n : n + 1, :])


VMEM = pl.BlockSpec(memory_space=pltpu.VMEM)
SMEM = pl.BlockSpec(memory_space=pltpu.SMEM)
HELD = pltpu.VMEM((ROWS, LANES), F32)
SHIFT_BUFFER = pltpu.VMEM(((2 * PAD + TILES) * 8, LANES), F32)


def shape(*dims, dtype=BF16):
    return jax.ShapeDtypeStruct(dims, dtype)


def solve_shapes(count):
    return [
        shape(count, ROWS, LANES, dtype=F32),
        shape(count, 2 * TILES, LANES, dtype=F32),
        shape(count * 2 * TILES, LANES),
    ]


def call(kernel, out_shape, in_specs, scratch, name, micros, out_specs=None, aliases=None):
    return pl.pallas_call(
        kernel,
        out_shape=out_shape,
        in_specs=in_specs,
        out_specs=out_specs if out_specs is not None else jax.tree.map(lambda _: VMEM, out_shape),
        scratch_shapes=scratch,
        input_output_aliases=aliases or {},
        name=name,
        cost_estimate=pl.CostEstimate(flops=0, bytes_accessed=int(micros * 3.0e6), transcendentals=0),
        compiler_params=pltpu.CompilerParams(vmem_limit_bytes=VMEM_LIMIT),
    )


def local(orbitals, pair_list, box_anchor):
    devices = lax.axis_size("orb")
    grid_index = lax.axis_index("grid")
    grid = grid_index.astype(jnp.int32).reshape(1)
    y_right, x_left = sine_factors()
    z_table = z_factors(grid_index)
    tables = (y_right, x_left, z_table)
    spread = ORB_DEV * PLANES + ENTRIES
    totals = shape(ORB_DEV, ROWS, LANES, dtype=F32)

    def to_all(blocks):
        return lax.all_to_all(blocks, "orb", split_axis=0, concat_axis=0, tiled=True)

    def to_near(message):
        return lax.ppermute(message, "grid", [(i, i ^ 1) for i in range(GRID)])

    def from_pairs(ends, near):
        outs = [shape(ends.shape[0], TILES, LANES)] * (PAIRS - 1)
        sums = call(pair_up_kernel, outs, [SMEM] + [VMEM] * 3, [], "pair_up", 1)(grid, ends, near, z_table)
        hops = [[(i, (i + 2 * e) % GRID) for i in range(GRID)] for e in ORDER]
        return [lax.ppermute(sums[e - 1], "grid", hop) for e, hop in zip(ORDER, hops)]

    orb_rows, pieces = call(
        spread_kernel,
        [shape(ORB_DEV, ROWS, LANES), shape(devices, spread, LANES)],
        [SMEM, VMEM],
        [],
        "spread",
        2,
    )(pair_list, orbitals)
    pieces = to_all(pieces)
    base_coeffs, base_ends, message = call(
        base_forward_kernel, solve_shapes(ORB_DEV), [VMEM] * 4, [HELD] * ORB_DEV, "base_forward", 2
    )(orb_rows, *tables)
    pieces, base_near = lax.optimization_barrier((pieces, to_near(message)))
    partners = pieces[:, ORB_DEV * PLANES :, 0].astype(jnp.int32).reshape(-1)
    served = call(
        serve_kernel,
        shape(devices, ENTRIES * PLANES, LANES),
        [SMEM, VMEM],
        [pltpu.VMEM((devices * ORB_DEV, PLANES, LANES), F32)],
        "serve",
        2,
    )(partners, pieces)
    fetched = to_all(served)
    total, base_energy = call(
        base_inverse_kernel,
        [totals, shape(ORB_DEV, LANES, dtype=F32)],
        [SMEM] + [VMEM] * (PAIRS + 5),
        [HELD] * ORB_DEV,
        "base_inverse",
        2,
    )(grid, base_near, *from_pairs(base_ends, base_near), base_coeffs, orb_rows, *tables)
    fetched, total = lax.optimization_barrier((fetched, total))

    moved, coeffs, ends, message = call(
        pair_forward_kernel,
        [shape(ENTRIES, ROWS, LANES)] + solve_shapes(ENTRIES),
        [SMEM] * 2 + [VMEM] * 5,
        [SHIFT_BUFFER] * ENTRIES + [HELD] * ENTRIES,
        "pair_forward",
        5,
    )(pair_list, box_anchor, orb_rows, fetched, *tables)
    near = to_near(message)
    total, pair_energy, back = call(
        pair_inverse_kernel,
        [totals, shape(ENTRIES, LANES, dtype=F32), shape(devices, ENTRIES * PLANES, LANES)],
        [SMEM] * 3 + [VMEM] * (PAIRS + 7),
        [SHIFT_BUFFER] * ENTRIES + [HELD] * ENTRIES,
        "pair_inverse",
        5,
        aliases={PAIRS + 9: 0},
    )(grid, pair_list, box_anchor, near, *from_pairs(ends, near), coeffs, orb_rows, moved, *tables, total)

    arrived = to_all(back)
    energy = lax.psum(jnp.sum(jnp.concatenate([base_energy, pair_energy]), axis=1), "grid")
    due, energy = call(
        gather_kernel,
        [shape(devices, spread, LANES), shape(ORB_DEV, LANES, dtype=F32)],
        [SMEM] * 2 + [VMEM, SMEM],
        [pltpu.VMEM((devices * ORB_DEV + 8, LANES), F32)]
        + [pltpu.VMEM((devices * ORB_DEV + 1, PLANES, LANES), F32)] * 4,
        "gather",
        4,
    )(partners, pair_list, arrived, energy)
    return call(
        finish_kernel,
        [shape(*orbitals.shape), shape(ORB_DEV, dtype=F32)],
        [VMEM] * 3,
        [],
        "finish",
        3,
        out_specs=[VMEM, SMEM],
    )(to_all(due), total, energy)


def solution(mesh):
    return jax.shard_map(
        local,
        mesh=mesh,
        in_specs=(P("orb", "grid", None), P(None, "orb"), P()),
        out_specs=(P("orb", "grid", None), P("orb")),
        check_vma=False,
    )
```

time: 172 us -> 131 us (0.76)
  starting transfers between devices: 65.3 us -> 41 us
  waiting for transfers between devices: 49.1 us -> 29.3 us
  blocking collectives: 16.4 us -> 34.7 us
  Pallas kernels: 31.2 us -> 17.7 us
    all_to_all x0 -> x1, blocking collectives: none -> 20.3 us  [to_all(): lax.all_to_all(blocks, 'orb', split_axis=0, concat_axis=0, tiled=True)]
    all_to_all x5 -> x3, starting transfers between devices: 36.5 us -> 16.6 us  [to_all(): lax.all_to_all(blocks, 'orb', split_axis=0, concat_axis=0, tiled=True)]
    pallas_call x15 -> x10, Pallas kernels: 31.2 us -> 17.7 us  [the longest x1 4.72 us: local(): call(pair_inverse_kernel, [totals, shape(ENTRIES, LANES, dtype=F32), shap...]
    all_to_all x5 -> x3, waiting for transfers between devices: 18.1 us -> 7.62 us  [to_all(): lax.all_to_all(blocks, 'orb', split_axis=0, concat_axis=0, tiled=True)]
    ppermute x12 -> x8, waiting for transfers between devices: 31.1 us -> 21.7 us  [the longest x6 12.5 us: from_pairs(): lax.ppermute(sums[e - 1], 'grid', hop)]
    ppermute x12 -> x8, starting transfers between devices: 28.7 us -> 24.3 us  [the longest x6 21.7 us: from_pairs(): lax.ppermute(sums[e - 1], 'grid', hop)]
    psum x1, blocking collectives: 16.4 us -> 14.4 us  [local(): lax.psum(jnp.sum(jnp.concatenate([base_energy, pair_energy]), axis=1), 'g...]
    unnamed x18 -> x22, local copies, waits for them, and re-layouts: 5.78 us -> 4.97 us
  transfers between devices with their start and end apart: 17 -> 11, of which waited for: 12 -> 7; matrix products, arithmetic and copies ran while one was open for 1% -> 1% of each run, Pallas kernels for 14% -> 2%
where the time goes in v2:
time: 131 us
  starting transfers between devices  41 us (31%)
  blocking collectives  34.7 us (26%)
  waiting for transfers between devices  29.3 us (22%)
  Pallas kernels  17.7 us (14%)
  local copies, waits for them, and re-layouts  5.48 us (4%)
  other arithmetic  1.47 us (1%)
    ppermute x6, starting transfers between devices, from_pairs(): lax.ppermute(sums[e - 1], 'grid', hop)  21.7 us
    all_to_all x1, blocking collectives, to_all(): lax.all_to_all(blocks, 'orb', split_axis=0, concat_axis=0, tiled=True)  20.3 us
    all_to_all x3, starting transfers between devices, to_all(): lax.all_to_all(blocks, 'orb', split_axis=0, concat_axis=0, tiled=True)  16.6 us
    psum x1, blocking collectives, local(): lax.psum(jnp.sum(jnp.concatenate([base_energy, pair_energy]), axis=1), 'g...  14.4 us
    ppermute x6, waiting for transfers between devices, from_pairs(): lax.ppermute(sums[e - 1], 'grid', hop)  12.5 us
    ppermute x2, waiting for transfers between devices, to_near(): return lax.ppermute(message, 'grid', [(i, i ^ 1) for i in range(GRID)])  9.22 us
    all_to_all x3, waiting for transfers between devices, to_all(): lax.all_to_all(blocks, 'orb', split_axis=0, concat_axis=0, tiled=True)  7.62 us
    unnamed x22, local copies, waits for them, and re-layouts  4.97 us
  transfers between devices with their start and end apart: 11, of which 7 were waited for; matrix products, arithmetic and copies ran while one was open for 1% of the time, Pallas kernels for 2%

profile of v2, /device:TPU:1, one launch (start us, length us, event | category | flops | bytes accessed | tf_op | source)
XLA Modules:
  0.0 130.8 jit_solution(15582349953442716652)
XLA Ops:
  0.6 0.0 copy-start.4
  0.7 1.1 copy-done.5
  1.7 0.7 copy-done.8
  2.4 1.5 %spread.1 = (bf16[8,256,128]{2,1,0:T(8,128)(2,1)S(1)}, bf16[32,80,128]{2,1,0:T(8,128)(2,1)}) custom-call(s32[2,16]{1,0:T(2,128)S(1)} %copy-done.8, bf16[8,8,4096]{2,1,0:T(8,128)(2,1)S(1)} %copy-done.5), custom_call_target="tpu_custom_call" | custom-call | bytes 6000000 | tf_op jit(solution)/shard_map/spread/pallas_call | solution.py:420
  3.9 8.6 %all-to-all-start = ((bf16[32,80,128]{2,1,0:T(8,128)(2,1)}), bf16[32,80,128]{2,1,0:T(8,128)(2,1)S(1)}, u32[]{:S(2)}, u32[]{:S(2)}) async-start(bf16[32,80,128]{2,1,0:T(8,128)(2,1)} %get-tuple-element.28), calls=%async_computation | async-start | bytes 1310720 | tf_op jit(solution)/shard_map/all_to_all | solution.py:409
  12.7 0.1 add.667
  12.8 0.1 copy.8
  12.9 0.1 add.662
  13.0 0.1 add.663
  13.2 0.1 divide_dynamic-update-slice_fusion.1
  13.3 0.1 divide_dynamic-update-slice_fusion
  13.4 0.1 multiply_dynamic-update-slice_fusion
  13.5 0.1 divide_dynamic-update-slice_fusion.2
  13.7 0.1 add.681
  13.9 1.0 base_forward.1
  14.9 1.7 %collective-permute-start = (bf16[512,128]{1,0:T(8,128)(2,1)S(1)}, bf16[512,128]{1,0:T(8,128)(2,1)S(1)}, u32[]{:S(2)}, u32[]{:S(2)}) collective-permute-start(bf16[512,128]{1,0:T(8,128)(2,1)S(1)} %get-tuple-element.30), channel_id=1, source_target_pairs={{0,1},{1,0},{2,3},{3,2},{4,5},{5,4},{6,7},{7,6},{8,9},{9,8},{10,11... | collective-permute-start | bytes 393224 | tf_op jit(solution)/shard_map/ppermute | solution.py:412
  16.6 3.6 %collective-permute-done.near = bf16[512,128]{1,0:T(8,128)(2,1)S(1)} collective-permute-done((bf16[512,128]{1,0:T(8,128)(2,1)S(1)}, bf16[512,128]{1,0:T(8,128)(2,1)S(1)}, u32[]{:S(2)}, u32[]{:S(2)}) %collective-permute-start) | collective-permute-done | bytes 131104 | tf_op jit(solution)/shard_map/ppermute | solution.py:412
  20.3 5.2 %all-to-all-done.held = bf16[32,80,128]{2,1,0:T(8,128)(2,1)S(1)} async-done(((bf16[32,80,128]{2,1,0:T(8,128)(2,1)}), bf16[32,80,128]{2,1,0:T(8,128)(2,1)S(1)}, u32[]{:S(2)}, u32[]{:S(2)}) %all-to-all-start) | async-done | bytes 655392 | tf_op jit(solution)/shard_map/all_to_all | solution.py:409
  25.5 0.6 convert_reduce_fusion
  26.1 0.1 reshape.540.partners
  26.2 2.6 %serve.1 = bf16[32,128,128]{2,1,0:T(8,128)(2,1)} custom-call(s32[512]{0:T(512)S(1)} %reshape.540.partners, bf16[32,80,128]{2,1,0:T(8,128)(2,1)S(1)} %all-to-all-done.held), custom_call_target="tpu_custom_call" | custom-call | bytes 6000000 | tf_op jit(solution)/shard_map/serve/pallas_call | solution.py:434
  28.8 3.7 %all-to-all-start.1 = ((bf16[32,128,128]{2,1,0:T(8,128)(2,1)}), bf16[32,128,128]{2,1,0:T(8,128)(2,1)S(1)}, u32[]{:S(2)}, u32[]{:S(2)}) async-start(bf16[32,128,128]{2,1,0:T(8,128)(2,1)} %serve.1), calls=%async_computation.1 | async-start | bytes 2097152 | tf_op jit(solution)/shard_map/all_to_all | solution.py:409
  32.6 0.9 copy-done.7
  33.5 0.1 pair_up.2
  33.6 7.0 %collective-permute-start.1 = (bf16[8,32,128]{2,1,0:T(8,128)(2,1)S(1)}, bf16[8,32,128]{2,1,0:T(8,128)(2,1)S(1)}, u32[]{:S(2)}, u32[]{:S(2)}) collective-permute-start(bf16[8,32,128]{2,1,0:T(8,128)(2,1)S(1)} %get-tuple-element.34), channel_id=1, source_target_pairs={{0,4},{1,5},{2,6},{3,7},{4,0},{5,1},{6,2},{7,3},{8,12},{9,13},{10,... | collective-permute-start | bytes 196616 | tf_op jit(solution)/shard_map/ppermute | solution.py:418
  40.6 1.2 collective-permute-start.2
  41.8 2.4 %collective-permute-start.3 = (bf16[8,32,128]{2,1,0:T(8,128)(2,1)S(1)}, bf16[8,32,128]{2,1,0:T(8,128)(2,1)S(1)}, u32[]{:S(2)}, u32[]{:S(2)}) collective-permute-start(bf16[8,32,128]{2,1,0:T(8,128)(2,1)S(1)} %get-tuple-element.36), channel_id=1, source_target_pairs={{0,6},{1,7},{2,0},{3,1},{4,2},{5,3},{6,4},{7,5},{8,14},{9,15},{10,... | collective-permute-start | bytes 196616 | tf_op jit(solution)/shard_map/ppermute | solution.py:418
  44.2 3.1 %collective-permute-done.2.refs_1_ = bf16[8,32,128]{2,1,0:T(8,128)(2,1)S(1)} collective-permute-done((bf16[8,32,128]{2,1,0:T(8,128)(2,1)S(1)}, bf16[8,32,128]{2,1,0:T(8,128)(2,1)S(1)}, u32[]{:S(2)}, u32[]{:S(2)}) %collective-permute-start.2) | collective-permute-done | bytes 65568 | tf_op jit(solution)/shard_map/ppermute | solution.py:418
  47.3 1.2 copy-done.2
  48.5 1.7 %base_inverse.1 = (f32[8,256,128]{2,1,0:T(8,128)S(1)}, f32[8,128]{1,0:T(8,128)S(1)}) custom-call(s32[1]{0:T(128)} %bitcast.grid, bf16[512,128]{1,0:T(8,128)(2,1)S(1)} %collective-permute-done.near, bf16[8,32,128]{2,1,0:T(8,128)(2,1)S(1)} %collective-permute-done.1.refs_0_, bf16[8,32,128]{2,1,0:T(8,128)(2,1)S(1)} %collective-permute-done.2.refs_1_, ...), custom_call_target="tpu_custom_call" | custom-call | bytes 6000000 | tf_op jit(solution)/shard_map/base_inverse/pallas_call | solution.py:443
  50.2 2.9 %pair_forward.1 = (bf16[16,256,128]{2,1,0:T(8,128)(2,1)S(1)}, f32[16,256,128]{2,1,0:T(8,128)S(1)}, f32[16,64,128]{2,1,0:T(8,128)S(1)}, bf16[1024,128]{1,0:T(8,128)(2,1)S(1)}) custom-call(s32[2,16]{1,0:T(2,128)S(1)} %copy-done.9, s32[2,256]{1,0:T(2,128)S(1)} %copy-done.10, bf16[8,256,128]{2,1,0:T(8,128)(2,1)S(1)} %get-tuple-element.29.orb_rows.refs_4_, ...), custom_call_target="tpu_custom_call" | custom-call | bytes 15000000 | tf_op jit(solution)/shard_map/pair_forward/pallas_call | solution.py:453
  53.1 1.0 collective-permute-start.4
  54.0 5.6 %collective-permute-done.4.near = bf16[1024,128]{1,0:T(8,128)(2,1)S(1)} collective-permute-done((bf16[1024,128]{1,0:T(8,128)(2,1)S(1)}, bf16[1024,128]{1,0:T(8,128)(2,1)S(1)}, u32[]{:S(2)}, u32[]{:S(2)}) %collective-permute-start.4) | collective-permute-done | bytes 262176 | tf_op jit(solution)/shard_map/ppermute | solution.py:412
  59.6 0.1 pair_up.3
  59.8 7.5 %collective-permute-start.5 = (bf16[16,32,128]{2,1,0:T(8,128)(2,1)S(1)}, bf16[16,32,128]{2,1,0:T(8,128)(2,1)S(1)}, u32[]{:S(2)}, u32[]{:S(2)}) collective-permute-start(bf16[16,32,128]{2,1,0:T(8,128)(2,1)S(1)} %get-tuple-element.42), channel_id=1, source_target_pairs={{0,4},{1,5},{2,6},{3,7},{4,0},{5,1},{6,2},{7,3},{8,12},{9,13},{10,... | collective-permute-start | bytes 393224 | tf_op jit(solution)/shard_map/ppermute | solution.py:418
  67.3 1.2 collective-permute-start.6
  68.5 2.4 %collective-permute-start.7 = (bf16[16,32,128]{2,1,0:T(8,128)(2,1)S(1)}, bf16[16,32,128]{2,1,0:T(8,128)(2,1)S(1)}, u32[]{:S(2)}, u32[]{:S(2)}) collective-permute-start(bf16[16,32,128]{2,1,0:T(8,128)(2,1)S(1)} %get-tuple-element.44), channel_id=1, source_target_pairs={{0,6},{1,7},{2,0},{3,1},{4,2},{5,3},{6,4},{7,5},{8,14},{9,15},{10,... | collective-permute-start | bytes 393224 | tf_op jit(solution)/shard_map/ppermute | solution.py:418
  70.9 5.7 %collective-permute-done.6.refs_1_ = bf16[16,32,128]{2,1,0:T(8,128)(2,1)S(1)} collective-permute-done((bf16[16,32,128]{2,1,0:T(8,128)(2,1)S(1)}, bf16[16,32,128]{2,1,0:T(8,128)(2,1)S(1)}, u32[]{:S(2)}, u32[]{:S(2)}) %collective-permute-start.6) | collective-permute-done | bytes 131104 | tf_op jit(solution)/shard_map/ppermute | solution.py:418
  76.6 3.6 %collective-permute-done.7.refs_2_ = bf16[16,32,128]{2,1,0:T(8,128)(2,1)S(1)} collective-permute-done((bf16[16,32,128]{2,1,0:T(8,128)(2,1)S(1)}, bf16[16,32,128]{2,1,0:T(8,128)(2,1)S(1)}, u32[]{:S(2)}, u32[]{:S(2)}) %collective-permute-start.7) | collective-permute-done | bytes 131104 | tf_op jit(solution)/shard_map/ppermute | solution.py:418
  80.2 4.7 %pair_inverse.1 = (f32[8,256,128]{2,1,0:T(8,128)S(1)}, f32[16,128]{1,0:T(8,128)S(1)}, bf16[32,128,128]{2,1,0:T(8,128)(2,1)S(1)}) custom-call(s32[1]{0:T(128)} %bitcast.grid, s32[2,16]{1,0:T(2,128)S(1)} %copy-done.9, s32[2,256]{1,0:T(2,128)S(1)} %copy-done.10, bf16[1024,128]{1,0:T(8,128)(2,1)S(1)} %collective-permute-done.4.near, ...), custom_call_target="tpu_custom_call", output_to_operand_aliasing={{0}: (13, {})} | custom-call | bytes 15000000 | tf_op jit(solution)/shard_map/pair_inverse/pallas_call | solution.py:462
  85.0 1.0 copy-done.3
  86.0 4.3 %all-to-all-start.2 = ((bf16[32,128,128]{2,1,0:T(8,128)(2,1)}), bf16[32,128,128]{2,1,0:T(8,128)(2,1)S(1)}, u32[]{:S(2)}, u32[]{:S(2)}) async-start(bf16[32,128,128]{2,1,0:T(8,128)(2,1)} %copy-done.3), calls=%async_computation.2 | async-start | bytes 2097152 | tf_op jit(solution)/shard_map/all_to_all | solution.py:409
  90.3 0.1 maximum_reduce_fusion
  90.4 14.4 %psum.7.energy = f32[24]{0:T(128)S(1)} all-reduce(f32[24]{0:T(128)S(1)} %maximum_reduce_fusion), channel_id=1, replica_groups=mesh['orb'=32,'grid'=8] {'grid'}, use_global_device_ids=true, to_apply=%region_1.2 | all-reduce | flops 24 | bytes 192 | tf_op jit(solution)/shard_map/psum | solution.py:473
  104.8 2.4 %all-to-all-done.2.arrived = bf16[32,128,128]{2,1,0:T(8,128)(2,1)S(1)} async-done(((bf16[32,128,128]{2,1,0:T(8,128)(2,1)}), bf16[32,128,128]{2,1,0:T(8,128)(2,1)S(1)}, u32[]{:S(2)}, u32[]{:S(2)}) %all-to-all-start.2) | async-done | bytes 1048608 | tf_op jit(solution)/shard_map/all_to_all | solution.py:409
  107.2 2.1 %gather.1 = (bf16[32,80,128]{2,1,0:T(8,128)(2,1)S(1)}, f32[8,128]{1,0:T(8,128)S(1)}) custom-call(s32[512]{0:T(512)S(1)} %reshape.540.partners, s32[2,16]{1,0:T(2,128)S(1)} %copy-done.9, bf16[32,128,128]{2,1,0:T(8,128)(2,1)S(1)} %all-to-all-done.2.arrived, f32[24]{0:T(128)S(1)} %psum.7.energy), custom_call_target="tpu_custom_call" | custom-call | bytes 12000000 | tf_op jit(solution)/shard_map/gather/pallas_call | solution.py:474
  109.3 20.3 %all_to_all.20.arrived = bf16[32,80,128]{2,1,0:T(8,128)(2,1)S(1)} all-to-all(bf16[32,80,128]{2,1,0:T(8,128)(2,1)S(1)} %get-tuple-element.51), channel_id=1, replica_groups=mesh['orb'=32,'grid'=8] {'orb'}, dimensions={0} | all-to-all | bytes 1310720 | tf_op jit(solution)/shard_map/all_to_all | solution.py:409
  129.6 1.0 finish.1
  (30 shorter events, 0.3 us)
Async XLA Ops:
  0.6 13.2 %copy-start.4 = (bf16[64,192]{1,0:T(8,128)(2,1)S(1)}, bf16[64,192]{1,0:T(8,128)(2,1)}, u32[]{:S(2)}) copy-start(bf16[64,192]{1,0:T(8,128)(2,1)} %constant.99.clone.x_left.refs_6_.refs_7_) | copy-start | bytes 73732
  0.6 13.2 %copy-start = (bf16[256,256]{1,0:T(8,128)(2,1)S(1)}, bf16[256,256]{1,0:T(8,128)(2,1)}, u32[]{:S(2)}) copy-start(bf16[256,256]{1,0:T(8,128)(2,1)} %constant.98.clone.y_right.refs_5_.refs_6_) | copy-start | bytes 393220
  0.7 1.1 copy-start.5
  1.7 0.7 copy-start.8
  3.9 21.5 %all-to-all-start = ((bf16[32,80,128]{2,1,0:T(8,128)(2,1)}), bf16[32,80,128]{2,1,0:T(8,128)(2,1)S(1)}, u32[]{:S(2)}, u32[]{:S(2)}) async-start(bf16[32,80,128]{2,1,0:T(8,128)(2,1)} %get-tuple-element.28), calls=%async_computation | async-start | bytes 1310720 | tf_op jit(solution)/shard_map/all_to_all | solution.py:409
  14.9 13.9 %copy-start.1 = (f32[8,256,128]{2,1,0:T(8,128)}, f32[8,256,128]{2,1,0:T(8,128)S(1)}, u32[]{:S(2)}) copy-start(f32[8,256,128]{2,1,0:T(8,128)S(1)} %get-tuple-element.37.refs_3_) | copy-start | bytes 3145732
  14.9 13.9 %copy-start.6 = (f32[8,64,128]{2,1,0:T(8,128)}, f32[8,64,128]{2,1,0:T(8,128)S(1)}, u32[]{:S(2)}) copy-start(f32[8,64,128]{2,1,0:T(8,128)S(1)} %get-tuple-element.33.ends) | copy-start | bytes 786436
  14.9 5.3 %collective-permute-start = (bf16[512,128]{1,0:T(8,128)(2,1)S(1)}, bf16[512,128]{1,0:T(8,128)(2,1)S(1)}, u32[]{:S(2)}, u32[]{:S(2)}) collective-permute-start(bf16[512,128]{1,0:T(8,128)(2,1)S(1)} %get-tuple-element.30), channel_id=1, source_target_pairs={{0,1},{1,0},{2,3},{3,2},{4,5},{5,4},{6,7},{7,6},{8,9},{9,8},{10,11... | collective-permute-start | bytes 393224 | tf_op jit(solution)/shard_map/ppermute | solution.py:412
  28.8 21.4 %all-to-all-start.1 = ((bf16[32,128,128]{2,1,0:T(8,128)(2,1)}), bf16[32,128,128]{2,1,0:T(8,128)(2,1)S(1)}, u32[]{:S(2)}, u32[]{:S(2)}) async-start(bf16[32,128,128]{2,1,0:T(8,128)(2,1)} %serve.1), calls=%async_computation.1 | async-start | bytes 2097152 | tf_op jit(solution)/shard_map/all_to_all | solution.py:409
  32.5 17.7 %copy-start.9 = (s32[2,16]{1,0:T(2,128)S(1)}, s32[2,16]{1,0:T(2,128)}, u32[]{:S(2)}) copy-start(s32[2,16]{1,0:T(2,128)} %pairs.7) | copy-start | bytes 388
  32.5 17.7 %copy-start.10 = (s32[2,256]{1,0:T(2,128)S(1)}, s32[2,256]{1,0:T(2,128)}, u32[]{:S(2)}) copy-start(s32[2,256]{1,0:T(2,128)} %anchor.3) | copy-start | bytes 6148
  32.6 1.0 copy-start.7
  33.6 10.6 %collective-permute-start.1 = (bf16[8,32,128]{2,1,0:T(8,128)(2,1)S(1)}, bf16[8,32,128]{2,1,0:T(8,128)(2,1)S(1)}, u32[]{:S(2)}, u32[]{:S(2)}) collective-permute-start(bf16[8,32,128]{2,1,0:T(8,128)(2,1)S(1)} %get-tuple-element.34), channel_id=1, source_target_pairs={{0,4},{1,5},{2,6},{3,7},{4,0},{5,1},{6,2},{7,3},{8,12},{9,13},{10,... | collective-permute-start | bytes 196616 | tf_op jit(solution)/shard_map/ppermute | solution.py:418
  40.6 6.7 %collective-permute-start.2 = (bf16[8,32,128]{2,1,0:T(8,128)(2,1)S(1)}, bf16[8,32,128]{2,1,0:T(8,128)(2,1)S(1)}, u32[]{:S(2)}, u32[]{:S(2)}) collective-permute-start(bf16[8,32,128]{2,1,0:T(8,128)(2,1)S(1)} %get-tuple-element.35), channel_id=1, source_target_pairs={{0,2},{1,3},{2,4},{3,5},{4,6},{5,7},{6,0},{7,1},{8,10},{9,11},{10,... | collective-permute-start | bytes 196616 | tf_op jit(solution)/shard_map/ppermute | solution.py:418
  41.8 5.5 %collective-permute-start.3 = (bf16[8,32,128]{2,1,0:T(8,128)(2,1)S(1)}, bf16[8,32,128]{2,1,0:T(8,128)(2,1)S(1)}, u32[]{:S(2)}, u32[]{:S(2)}) collective-permute-start(bf16[8,32,128]{2,1,0:T(8,128)(2,1)S(1)} %get-tuple-element.36), channel_id=1, source_target_pairs={{0,6},{1,7},{2,0},{3,1},{4,2},{5,3},{6,4},{7,5},{8,14},{9,15},{10,... | collective-permute-start | bytes 196616 | tf_op jit(solution)/shard_map/ppermute | solution.py:418
  47.3 1.2 copy-start.2
  53.1 6.6 %collective-permute-start.4 = (bf16[1024,128]{1,0:T(8,128)(2,1)S(1)}, bf16[1024,128]{1,0:T(8,128)(2,1)S(1)}, u32[]{:S(2)}, u32[]{:S(2)}) collective-permute-start(bf16[1024,128]{1,0:T(8,128)(2,1)S(1)} %get-tuple-element.40), channel_id=1, source_target_pairs={{0,1},{1,0},{2,3},{3,2},{4,5},{5,4},{6,7},{7,6},{8,9},{9,8},{10,11... | collective-permute-start | bytes 786440 | tf_op jit(solution)/shard_map/ppermute | solution.py:412
  59.8 11.1 %collective-permute-start.5 = (bf16[16,32,128]{2,1,0:T(8,128)(2,1)S(1)}, bf16[16,32,128]{2,1,0:T(8,128)(2,1)S(1)}, u32[]{:S(2)}, u32[]{:S(2)}) collective-permute-start(bf16[16,32,128]{2,1,0:T(8,128)(2,1)S(1)} %get-tuple-element.42), channel_id=1, source_target_pairs={{0,4},{1,5},{2,6},{3,7},{4,0},{5,1},{6,2},{7,3},{8,12},{9,13},{10,... | collective-permute-start | bytes 393224 | tf_op jit(solution)/shard_map/ppermute | solution.py:418
  67.3 9.3 %collective-permute-start.6 = (bf16[16,32,128]{2,1,0:T(8,128)(2,1)S(1)}, bf16[16,32,128]{2,1,0:T(8,128)(2,1)S(1)}, u32[]{:S(2)}, u32[]{:S(2)}) collective-permute-start(bf16[16,32,128]{2,1,0:T(8,128)(2,1)S(1)} %get-tuple-element.43), channel_id=1, source_target_pairs={{0,2},{1,3},{2,4},{3,5},{4,6},{5,7},{6,0},{7,1},{8,10},{9,11},{10,... | collective-permute-start | bytes 393224 | tf_op jit(solution)/shard_map/ppermute | solution.py:418
  68.5 11.7 %collective-permute-start.7 = (bf16[16,32,128]{2,1,0:T(8,128)(2,1)S(1)}, bf16[16,32,128]{2,1,0:T(8,128)(2,1)S(1)}, u32[]{:S(2)}, u32[]{:S(2)}) collective-permute-start(bf16[16,32,128]{2,1,0:T(8,128)(2,1)S(1)} %get-tuple-element.44), channel_id=1, source_target_pairs={{0,6},{1,7},{2,0},{3,1},{4,2},{5,3},{6,4},{7,5},{8,14},{9,15},{10,... | collective-permute-start | bytes 393224 | tf_op jit(solution)/shard_map/ppermute | solution.py:418
  85.0 1.0 copy-start.3
  86.0 21.2 %all-to-all-start.2 = ((bf16[32,128,128]{2,1,0:T(8,128)(2,1)}), bf16[32,128,128]{2,1,0:T(8,128)(2,1)S(1)}, u32[]{:S(2)}, u32[]{:S(2)}) async-start(bf16[32,128,128]{2,1,0:T(8,128)(2,1)} %copy-done.3), calls=%async_computation.2 | async-start | bytes 2097152 | tf_op jit(solution)/shard_map/all_to_all | solution.py:409

commit v3 on v2

--- a/solution.py
+++ b/solution.py
@@ -20,6 +20,7 @@
 UP, DOWN, MIDDLE, CARRY, PAST_UP, PAST_DOWN = 0, 8, 16, 24, 27, 28
 ORB_DEV = 8
 ENTRIES = 16
+HALF = ENTRIES // 2
 PAD = 10
 MU2 = 0.02
 BF16 = jnp.bfloat16
@@ -193,7 +194,7 @@
         solved[z] = z_table[MIDDLE + z] * (ups[z] + carried)
         from_above = planes[z] + carried
         product += planes[z] * solved[z]
-    full = times_y(jnp.concatenate(times_x(solved, x_left[...], 2), axis=0), y_right[...])
+    full = times_y(jnp.concatenate(times_x(solved, x_left[...], 1), axis=0), y_right[...])
     for z in range(PLANES):
         held[pl.ds(z, TILES, stride=PLANES), :] = full[TILES * z : TILES * (z + 1)]
     return held[...], column_sums(product)
@@ -211,11 +212,15 @@
     return box[PLANES * t : PLANES * (t + 1)]
 
 
-def spread_kernel(pairs, orb, orb_rows, out):
+def rows_kernel(orb, orb_rows):
+    for n in range(ORB_DEV):
+        wide = orb[n].astype(F32)
+        box = jnp.concatenate([wide[:, LANES * t : LANES * (t + 1)] for t in range(TILES)], axis=0)
+        orb_rows[n] = box.astype(BF16)
+
+
+def spread_kernel(pairs, orb, out):
     wide = [orb[n].astype(F32) for n in range(ORB_DEV)]
-    for n in range(ORB_DEV):
-        box = jnp.concatenate([wide[n][:, LANES * t : LANES * (t + 1)] for t in range(TILES)], axis=0)
-        orb_rows[n] = box.astype(BF16)
     rows = lax.broadcasted_iota(jnp.int32, (ENTRIES, LANES), 0)
     partners = jnp.zeros((ENTRIES, LANES), F32)
     for n in range(ENTRIES):
@@ -234,12 +239,14 @@
         for n in range(ORB_DEV):
             every[ORB_DEV * d + n] = tile(pieces, n)
 
-    def step(d, carry):
-        pieces = [every[jnp.maximum(partners[ENTRIES * d + n], 0)] for n in range(ENTRIES)]
-        out[d] = jnp.concatenate(pieces, axis=0).astype(BF16)
+    def step(i, carry):
+        for d in range(4):
+            d += 4 * i
+            pieces = [every[jnp.maximum(partners[ENTRIES * d + n], 0)] for n in range(ENTRIES)]
+            out[d] = jnp.concatenate(pieces, axis=0).astype(BF16)
         return carry
 
-    lax.fori_loop(0, count, step, 0)
+    lax.fori_loop(0, count // 4, step, 0)
 
 
 def base_forward_kernel(orb_rows, y_right, x_left, z_table, coeffs, ends, message, *held):
@@ -248,14 +255,15 @@
         forward(box * box, (y_right, x_left, z_table), held[n], coeffs, ends, message, n)
 
 
-def pair_forward_kernel(pairs, anchor, orb_rows, fetched, y_right, x_left, z_table, moved_out, coeffs, ends, message, *refs):
-    buffers, held = refs[:ENTRIES], refs[ENTRIES:]
-    for n in range(ENTRIES):
+def pair_forward_kernel(start, pairs, anchor, orb_rows, fetched, y_right, x_left, z_table, moved_out, coeffs, ends, message, *refs):
+    buffers, held = refs[:HALF], refs[HALF:]
+    for n in range(HALF):
         clear_margins(buffers[n])
-    for m in range(0, ENTRIES, 2):
-        both = [fetched[t, PLANES * m : PLANES * (m + 2), :].astype(F32) for t in range(TILES)]
+    for m in range(0, HALF, 2):
+        row = PLANES * (start + m)
+        both = [fetched[t, row : row + 2 * PLANES, :].astype(F32) for t in range(TILES)]
         for n in (m, m + 1):
-            _, owner, step_x, step_y = pair_scalars(pairs, anchor, n)
+            _, owner, step_x, step_y = pair_scalars(pairs, anchor, start + n)
             mate = jnp.concatenate([tile(b, n - m) for b in both], axis=0)
             moved = shifted(mate, step_x, step_y, buffers[n])
             moved_out[n] = moved.astype(BF16)
@@ -293,26 +301,29 @@
         energy[n : n + 1, :] = value
 
 
-def pair_inverse_kernel(grid, pairs, anchor, near, *refs):
+def pair_inverse_kernel(start, grid, pairs, anchor, near, *refs):
     sums, refs = refs[: PAIRS - 1], refs[PAIRS - 1 :]
-    coeffs, orb_rows, moved, y_right, x_left, z_table, total_in, total, energy, out, *refs = refs
-    buffers, held = refs[:ENTRIES], refs[ENTRIES:]
+    coeffs, orb_rows, moved, y_right, x_left, z_table, total_in, out_in, total, out, energy, *refs = refs
+    buffers, held = refs[:HALF], refs[HALF:]
     tables = (y_right, x_left, z_table)
-    for n in range(ENTRIES):
+    for n in range(HALF):
         clear_margins(buffers[n])
     total[...] = total_in[...]
-    for m in range(0, ENTRIES, 2):
+    if start:
+        out[:, : PLANES * start, :] = out_in[:, : PLANES * start, :]
+    for m in range(0, HALF, 2):
         backs = []
         for n in (m, m + 1):
-            _, owner, step_x, step_y = pair_scalars(pairs, anchor, n)
+            _, owner, step_x, step_y = pair_scalars(pairs, anchor, start + n)
             potential, value = inverse(grid[0], near, in_order(sums, n), coeffs, tables, held[n], n)
             energy[n : n + 1, :] = value
             backs.append(shifted(orb_rows[owner].astype(F32) * potential, -step_x, -step_y, buffers[n]))
+        row = PLANES * (start + m)
         for t in range(TILES):
             piece = jnp.concatenate([tile(back, t) for back in backs], axis=0)
-            out[t, PLANES * m : PLANES * (m + 2), :] = piece.astype(BF16)
-    for n in range(ENTRIES):
-        live, owner, _, _ = pair_scalars(pairs, anchor, n)
+            out[t, row : row + 2 * PLANES, :] = piece.astype(BF16)
+    for n in range(HALF):
+        live, owner, _, _ = pair_scalars(pairs, anchor, start + n)
         total[owner] += jnp.where(live, moved[n].astype(F32) * held[n][...], 0.0)
 
 
@@ -322,16 +333,17 @@
     for part in every:
         part[...] = jnp.zeros_like(part)
 
-    def step(d, carry):
-        for m in range(0, ENTRIES, 2):
-            both = arrived[d, PLANES * m : PLANES * (m + 2), :].astype(F32)
-            for n in (m, m + 1):
-                which = partners[ENTRIES * d + n]
-                which = jnp.where(which >= 0, which, spare)
-                every[n % len(every)][which] += tile(both, n - m)
+    def step(i, carry):
+        for d in (2 * i, 2 * i + 1):
+            for m in range(0, ENTRIES, 2):
+                both = arrived[d, PLANES * m : PLANES * (m + 2), :].astype(F32)
+                for n in (m, m + 1):
+                    which = partners[ENTRIES * d + n]
+                    which = jnp.where(which >= 0, which, spare)
+                    every[n % len(every)][which] += tile(both, n - m)
         return carry
 
-    lax.fori_loop(0, count, step, 0)
+    lax.fori_loop(0, count // 2, step, 0)
     every_energy[...] = jnp.zeros_like(every_energy)
     first = lane_iota(1) == 0
     for n in range(ORB_DEV):
@@ -365,6 +377,7 @@
 
 VMEM = pl.BlockSpec(memory_space=pltpu.VMEM)
 SMEM = pl.BlockSpec(memory_space=pltpu.SMEM)
+ANY = pl.BlockSpec(memory_space=pl.ANY)
 HELD = pltpu.VMEM((ROWS, LANES), F32)
 SHIFT_BUFFER = pltpu.VMEM(((2 * PAD + TILES) * 8, LANES), F32)
 
@@ -417,14 +430,11 @@
         hops = [[(i, (i + 2 * e) % GRID) for i in range(GRID)] for e in ORDER]
         return [lax.ppermute(sums[e - 1], "grid", hop) for e, hop in zip(ORDER, hops)]
 
-    orb_rows, pieces = call(
-        spread_kernel,
-        [shape(ORB_DEV, ROWS, LANES), shape(devices, spread, LANES)],
-        [SMEM, VMEM],
-        [],
-        "spread",
-        2,
-    )(pair_list, orbitals)
+    pieces = call(spread_kernel, shape(devices, spread, LANES), [SMEM, VMEM], [], "spread", 1)(
+        pair_list, orbitals
+    )
+    orbitals, _ = lax.optimization_barrier((orbitals, pieces))
+    orb_rows = call(rows_kernel, shape(ORB_DEV, ROWS, LANES), [VMEM], [], "rows", 1)(orbitals)
     pieces = to_all(pieces)
     base_coeffs, base_ends, message = call(
         base_forward_kernel, solve_shapes(ORB_DEV), [VMEM] * 4, [HELD] * ORB_DEV, "base_forward", 2
@@ -440,6 +450,8 @@
         2,
     )(partners, pieces)
     fetched = to_all(served)
+    base_sums = from_pairs(base_ends, base_near)
+    fetched, base_sums = lax.optimization_barrier((fetched, base_sums))
     total, base_energy = call(
         base_inverse_kernel,
         [totals, shape(ORB_DEV, LANES, dtype=F32)],
@@ -447,30 +459,38 @@
         [HELD] * ORB_DEV,
         "base_inverse",
         2,
-    )(grid, base_near, *from_pairs(base_ends, base_near), base_coeffs, orb_rows, *tables)
-    fetched, total = lax.optimization_barrier((fetched, total))
-
-    moved, coeffs, ends, message = call(
-        pair_forward_kernel,
-        [shape(ENTRIES, ROWS, LANES)] + solve_shapes(ENTRIES),
-        [SMEM] * 2 + [VMEM] * 5,
-        [SHIFT_BUFFER] * ENTRIES + [HELD] * ENTRIES,
-        "pair_forward",
-        5,
-    )(pair_list, box_anchor, orb_rows, fetched, *tables)
-    near = to_near(message)
-    total, pair_energy, back = call(
-        pair_inverse_kernel,
-        [totals, shape(ENTRIES, LANES, dtype=F32), shape(devices, ENTRIES * PLANES, LANES)],
-        [SMEM] * 3 + [VMEM] * (PAIRS + 7),
-        [SHIFT_BUFFER] * ENTRIES + [HELD] * ENTRIES,
-        "pair_inverse",
-        5,
-        aliases={PAIRS + 9: 0},
-    )(grid, pair_list, box_anchor, near, *from_pairs(ends, near), coeffs, orb_rows, moved, *tables, total)
+    )(grid, base_near, *base_sums, base_coeffs, orb_rows, *tables)
+
+    parts = []
+    for start in range(0, ENTRIES, HALF):
+        moved, coeffs, ends, message = call(
+            functools.partial(pair_forward_kernel, start),
+            [shape(HALF, ROWS, LANES)] + solve_shapes(HALF),
+            [SMEM] * 2 + [VMEM] * 5,
+            [SHIFT_BUFFER] * HALF + [HELD] * HALF,
+            "pair_forward",
+            2,
+        )(pair_list, box_anchor, orb_rows, fetched, *tables)
+        parts.append((start, moved, coeffs, ends, to_near(message)))
+    start, moved, coeffs, ends, near = parts[0]
+    total, near = lax.optimization_barrier((total, near))
+    parts[0] = (start, moved, coeffs, ends, near)
+    parts = [(*part, from_pairs(part[3], part[4])) for part in parts]
+    back, energy = served, [base_energy]
+    for start, moved, coeffs, ends, near, sums in parts:
+        total, back, value = call(
+            functools.partial(pair_inverse_kernel, start),
+            [totals, shape(devices, ENTRIES * PLANES, LANES), shape(HALF, LANES, dtype=F32)],
+            [SMEM] * 3 + [VMEM] * (PAIRS + 7) + [VMEM if start else ANY],
+            [SHIFT_BUFFER] * HALF + [HELD] * HALF,
+            "pair_inverse",
+            3,
+            aliases={PAIRS + 9: 0, PAIRS + 10: 1} if start else {PAIRS + 9: 0},
+        )(grid, pair_list, box_anchor, near, *sums, coeffs, orb_rows, moved, *tables, total, back)
+        energy.append(value)
 
     arrived = to_all(back)
-    energy = lax.psum(jnp.sum(jnp.concatenate([base_energy, pair_energy]), axis=1), "grid")
+    energy = lax.psum(jnp.sum(jnp.concatenate(energy), axis=1), "grid")
     due, energy = call(
         gather_kernel,
         [shape(devices, spread, LANES), shape(ORB_DEV, LANES, dtype=F32)],

time: 131 us -> 126 us (0.962)
  waiting for transfers between devices: 29.3 us -> 18.4 us
  starting transfers between devices: 41 us -> 47.9 us
    ppermute x6 -> x9, waiting for transfers between devices: 12.5 us -> 5.28 us  [from_pairs(): lax.ppermute(sums[e - 1], 'grid', hop)]
    ppermute x2 -> x3, waiting for transfers between devices: 9.22 us -> 4.1 us  [to_near(): return lax.ppermute(message, 'grid', [(i, i ^ 1) for i in range(GRID)])]
    ppermute x6 -> x9, starting transfers between devices: 21.7 us -> 25.3 us  [from_pairs(): lax.ppermute(sums[e - 1], 'grid', hop)]
    all_to_all x3, starting transfers between devices: 16.6 us -> 19 us  [to_all(): lax.all_to_all(blocks, 'orb', split_axis=0, concat_axis=0, tiled=True)]
    all_to_all x3, waiting for transfers between devices: 7.62 us -> 8.99 us  [to_all(): lax.all_to_all(blocks, 'orb', split_axis=0, concat_axis=0, tiled=True)]
    pallas_call x3 -> x6, Pallas kernels: 9.11 us -> 10 us  [the longest x2 4.73 us: local(): call(functools.partial(pair_inverse_kernel, start), [totals, shape(device...]
    ppermute x2 -> x3, starting transfers between devices: 2.68 us -> 3.55 us  [to_near(): return lax.ppermute(message, 'grid', [(i, i ^ 1) for i in range(GRID)])]
    unnamed x22 -> x24, local copies, waits for them, and re-layouts: 4.97 us -> 5.02 us
  transfers between devices with their start and end apart: 11 -> 15, of which waited for: 7 -> 8; matrix products, arithmetic and copies ran while one was open for 1% -> 1% of each run, Pallas kernels for 2% -> 5%
where the time goes in v3:
time: 126 us
  starting transfers between devices  47.9 us (38%)
  blocking collectives  33.5 us (27%)
  waiting for transfers between devices  18.4 us (15%)
  Pallas kernels  18 us (14%)
  local copies, waits for them, and re-layouts  5.54 us (4%)
  other arithmetic  1.47 us (1%)
    ppermute x9, starting transfers between devices, from_pairs(): lax.ppermute(sums[e - 1], 'grid', hop)  25.3 us
    all_to_all x1, blocking collectives, to_all(): lax.all_to_all(blocks, 'orb', split_axis=0, concat_axis=0, tiled=True)  19.7 us
    all_to_all x3, starting transfers between devices, to_all(): lax.all_to_all(blocks, 'orb', split_axis=0, concat_axis=0, tiled=True)  19 us
    psum x1, blocking collectives, local(): energy = lax.psum(jnp.sum(jnp.concatenate(energy), axis=1), 'grid')  13.8 us
    all_to_all x3, waiting for transfers between devices, to_all(): lax.all_to_all(blocks, 'orb', split_axis=0, concat_axis=0, tiled=True)  8.99 us
    ppermute x9, waiting for transfers between devices, from_pairs(): lax.ppermute(sums[e - 1], 'grid', hop)  5.28 us
    unnamed x24, local copies, waits for them, and re-layouts  5.02 us
    pallas_call x2, Pallas kernels, local(): call(functools.partial(pair_inverse_kernel, start), [totals, shape(device...  4.73 us
  transfers between devices with their start and end apart: 15, of which 8 were waited for; matrix products, arithmetic and copies ran while one was open for 1% of the time, Pallas kernels for 5%

profile of v3, /device:TPU:1, one launch (start us, length us, event | category | flops | bytes accessed | tf_op | source)
XLA Modules:
  0.0 125.9 jit_solution(4382688735184070330)
XLA Ops:
  0.6 1.0 copy-done.2
  1.7 0.7 copy-done.9
  2.4 1.5 %spread.1 = bf16[32,80,128]{2,1,0:T(8,128)(2,1)} custom-call(s32[2,16]{1,0:T(2,128)S(1)} %copy-done.9, bf16[8,8,4096]{2,1,0:T(8,128)(2,1)S(1)} %copy-done.2), custom_call_target="tpu_custom_call" | custom-call | bytes 3000000 | tf_op jit(solution)/shard_map/spread/pallas_call | solution.py:433
  3.8 8.6 %all-to-all-start = ((bf16[32,80,128]{2,1,0:T(8,128)(2,1)}), bf16[32,80,128]{2,1,0:T(8,128)(2,1)S(1)}, u32[]{:S(2)}, u32[]{:S(2)}) async-start(bf16[32,80,128]{2,1,0:T(8,128)(2,1)} %spread.1), calls=%async_computation | async-start | bytes 1310720 | tf_op jit(solution)/shard_map/all_to_all | solution.py:422
  12.9 0.1 add.663
  13.0 0.1 divide_dynamic-update-slice_fusion.1
  13.2 0.1 divide_dynamic-update-slice_fusion
  13.3 0.1 multiply_dynamic-update-slice_fusion
  13.4 0.1 divide_dynamic-update-slice_fusion.2
  13.8 0.7 copy-done
  14.6 1.0 base_forward.1
  15.6 1.7 %collective-permute-start = (bf16[512,128]{1,0:T(8,128)(2,1)S(1)}, bf16[512,128]{1,0:T(8,128)(2,1)S(1)}, u32[]{:S(2)}, u32[]{:S(2)}) collective-permute-start(bf16[512,128]{1,0:T(8,128)(2,1)S(1)} %get-tuple-element.42), channel_id=1, source_target_pairs={{0,1},{1,0},{2,3},{3,2},{4,5},{5,4},{6,7},{7,6},{8,9},{9,8},{10,11... | collective-permute-start | bytes 393224 | tf_op jit(solution)/shard_map/ppermute | solution.py:425
  17.3 3.6 %collective-permute-done.near = bf16[512,128]{1,0:T(8,128)(2,1)S(1)} collective-permute-done((bf16[512,128]{1,0:T(8,128)(2,1)S(1)}, bf16[512,128]{1,0:T(8,128)(2,1)S(1)}, u32[]{:S(2)}, u32[]{:S(2)}) %collective-permute-start) | collective-permute-done | bytes 131104 | tf_op jit(solution)/shard_map/ppermute | solution.py:425
  20.9 4.4 %all-to-all-done.held = bf16[32,80,128]{2,1,0:T(8,128)(2,1)S(1)} async-done(((bf16[32,80,128]{2,1,0:T(8,128)(2,1)}), bf16[32,80,128]{2,1,0:T(8,128)(2,1)S(1)}, u32[]{:S(2)}, u32[]{:S(2)}) %all-to-all-start) | async-done | bytes 655392 | tf_op jit(solution)/shard_map/all_to_all | solution.py:422
  25.4 0.6 convert_reduce_fusion
  26.1 2.5 %serve.1.refs_10_ = bf16[32,128,128]{2,1,0:T(8,128)(2,1)} custom-call(s32[512]{0:T(512)S(1)} %reshape.540.partners, bf16[32,80,128]{2,1,0:T(8,128)(2,1)S(1)} %all-to-all-done.held), custom_call_target="tpu_custom_call" | custom-call | bytes 6000000 | tf_op jit(solution)/shard_map/serve/pallas_call | solution.py:444
  28.5 3.7 %all-to-all-start.1 = ((bf16[32,128,128]{2,1,0:T(8,128)(2,1)}), bf16[32,128,128]{2,1,0:T(8,128)(2,1)S(1)}, u32[]{:S(2)}, u32[]{:S(2)}) async-start(bf16[32,128,128]{2,1,0:T(8,128)(2,1)} %serve.1.refs_10_), calls=%async_computation.1 | async-start | bytes 2097152 | tf_op jit(solution)/shard_map/all_to_all | solution.py:422
  32.3 0.9 copy-done.6
  33.3 7.0 %collective-permute-start.1 = (bf16[8,32,128]{2,1,0:T(8,128)(2,1)S(1)}, bf16[8,32,128]{2,1,0:T(8,128)(2,1)S(1)}, u32[]{:S(2)}, u32[]{:S(2)}) collective-permute-start(bf16[8,32,128]{2,1,0:T(8,128)(2,1)S(1)} %get-tuple-element.46), channel_id=1, source_target_pairs={{0,4},{1,5},{2,6},{3,7},{4,0},{5,1},{6,2},{7,3},{8,12},{9,13},{10,... | collective-permute-start | bytes 196616 | tf_op jit(solution)/shard_map/ppermute | solution.py:431
  40.3 1.2 collective-permute-start.2
  41.5 2.4 %collective-permute-start.3 = (bf16[8,32,128]{2,1,0:T(8,128)(2,1)S(1)}, bf16[8,32,128]{2,1,0:T(8,128)(2,1)S(1)}, u32[]{:S(2)}, u32[]{:S(2)}) collective-permute-start(bf16[8,32,128]{2,1,0:T(8,128)(2,1)S(1)} %get-tuple-element.48), channel_id=1, source_target_pairs={{0,6},{1,7},{2,0},{3,1},{4,2},{5,3},{6,4},{7,5},{8,14},{9,15},{10,... | collective-permute-start | bytes 196616 | tf_op jit(solution)/shard_map/ppermute | solution.py:431
  43.9 3.1 %collective-permute-done.2.refs_1_ = bf16[8,32,128]{2,1,0:T(8,128)(2,1)S(1)} collective-permute-done((bf16[8,32,128]{2,1,0:T(8,128)(2,1)S(1)}, bf16[8,32,128]{2,1,0:T(8,128)(2,1)S(1)}, u32[]{:S(2)}, u32[]{:S(2)}) %collective-permute-start.2) | collective-permute-done | bytes 65568 | tf_op jit(solution)/shard_map/ppermute | solution.py:431
  47.0 0.6 copy-done.7
  47.6 1.6 %all-to-all-done.1.fetched = bf16[32,128,128]{2,1,0:T(8,128)(2,1)S(1)} async-done(((bf16[32,128,128]{2,1,0:T(8,128)(2,1)}), bf16[32,128,128]{2,1,0:T(8,128)(2,1)S(1)}, u32[]{:S(2)}, u32[]{:S(2)}) %all-to-all-start.1) | async-done | bytes 1048608 | tf_op jit(solution)/shard_map/all_to_all | solution.py:422
  49.2 1.9 %pair_forward.3 = (bf16[8,256,128]{2,1,0:T(8,128)(2,1)S(1)}, f32[8,256,128]{2,1,0:T(8,128)S(1)}, f32[8,64,128]{2,1,0:T(8,128)S(1)}, bf16[512,128]{1,0:T(8,128)(2,1)S(1)}) custom-call(s32[2,16]{1,0:T(2,128)S(1)} %copy-done.10, s32[2,256]{1,0:T(2,128)S(1)} %copy-done.11, bf16[8,256,128]{2,1,0:T(8,128)(2,1)S(1)} %rows.1.orb_rows.refs_4_, ...), custom_call_target="tpu_custom_call" | custom-call | bytes 6000000 | tf_op jit(solution)/shard_map/pair_forward/pallas_call | solution.py:466
  51.1 1.7 %collective-permute-start.8 = (bf16[512,128]{1,0:T(8,128)(2,1)S(1)}, bf16[512,128]{1,0:T(8,128)(2,1)S(1)}, u32[]{:S(2)}, u32[]{:S(2)}) collective-permute-start(bf16[512,128]{1,0:T(8,128)(2,1)S(1)} %get-tuple-element.62), channel_id=1, source_target_pairs={{0,1},{1,0},{2,3},{3,2},{4,5},{5,4},{6,7},{7,6},{8,9},{9,8},{10,11... | collective-permute-start | bytes 393224 | tf_op jit(solution)/shard_map/ppermute | solution.py:425
  52.8 1.9 %pair_forward.2 = (bf16[8,256,128]{2,1,0:T(8,128)(2,1)S(1)}, f32[8,256,128]{2,1,0:T(8,128)S(1)}, f32[8,64,128]{2,1,0:T(8,128)S(1)}, bf16[512,128]{1,0:T(8,128)(2,1)S(1)}) custom-call(s32[2,16]{1,0:T(2,128)S(1)} %copy-done.10, s32[2,256]{1,0:T(2,128)S(1)} %copy-done.11, bf16[8,256,128]{2,1,0:T(8,128)(2,1)S(1)} %rows.1.orb_rows.refs_4_, ...), custom_call_target="tpu_custom_call" | custom-call | bytes 6000000 | tf_op jit(solution)/shard_map/pair_forward/pallas_call | solution.py:466
  54.7 0.1 collective-permute-start.4
  54.8 1.2 base_inverse.1
  56.0 0.5 collective-permute-done.8.near
  56.6 6.6 %collective-permute-start.9 = (bf16[8,32,128]{2,1,0:T(8,128)(2,1)S(1)}, bf16[8,32,128]{2,1,0:T(8,128)(2,1)S(1)}, u32[]{:S(2)}, u32[]{:S(2)}) collective-permute-start(bf16[8,32,128]{2,1,0:T(8,128)(2,1)S(1)} %get-tuple-element.65), channel_id=1, source_target_pairs={{0,4},{1,5},{2,6},{3,7},{4,0},{5,1},{6,2},{7,3},{8,12},{9,13},{10,... | collective-permute-start | bytes 196616 | tf_op jit(solution)/shard_map/ppermute | solution.py:431
  63.2 1.2 collective-permute-start.10
  64.4 2.4 %collective-permute-start.11 = (bf16[8,32,128]{2,1,0:T(8,128)(2,1)S(1)}, bf16[8,32,128]{2,1,0:T(8,128)(2,1)S(1)}, u32[]{:S(2)}, u32[]{:S(2)}) collective-permute-start(bf16[8,32,128]{2,1,0:T(8,128)(2,1)S(1)} %get-tuple-element.67), channel_id=1, source_target_pairs={{0,6},{1,7},{2,0},{3,1},{4,2},{5,3},{6,4},{7,5},{8,14},{9,15},{10,... | collective-permute-start | bytes 196616 | tf_op jit(solution)/shard_map/ppermute | solution.py:431
  66.9 1.0 collective-permute-start.5
  67.9 1.2 collective-permute-start.6
  69.0 2.4 %collective-permute-start.7 = (bf16[8,32,128]{2,1,0:T(8,128)(2,1)S(1)}, bf16[8,32,128]{2,1,0:T(8,128)(2,1)S(1)}, u32[]{:S(2)}, u32[]{:S(2)}) collective-permute-start(bf16[8,32,128]{2,1,0:T(8,128)(2,1)S(1)} %get-tuple-element.54), channel_id=1, source_target_pairs={{0,6},{1,7},{2,0},{3,1},{4,2},{5,3},{6,4},{7,5},{8,14},{9,15},{10,... | collective-permute-start | bytes 196616 | tf_op jit(solution)/shard_map/ppermute | solution.py:431
  71.5 2.3 %pair_inverse.2 = (f32[8,256,128]{2,1,0:T(8,128)S(1)}, bf16[32,128,128]{2,1,0:T(8,128)(2,1)S(1)}, f32[8,128]{1,0:T(8,128)S(1)}) custom-call(s32[1]{0:T(128)} %bitcast.grid, s32[2,16]{1,0:T(2,128)S(1)} %copy-done.10, s32[2,256]{1,0:T(2,128)S(1)} %copy-done.11, bf16[512,128]{1,0:T(8,128)(2,1)S(1)} %collective-permute-done.8.near, ...), custom_call_target="tpu_custom_call", output_to_operand_aliasing={{0}: (13, {})} | custom-call | bytes 9000000 | tf_op jit(solution)/shard_map/pair_inverse/pallas_call | solution.py:481
  73.8 1.1 collective-permute-done.5.refs_0_
  74.9 1.0 collective-permute-done.7.refs_2_
  76.0 2.4 %pair_inverse.3 = (f32[8,256,128]{2,1,0:T(8,128)S(1)}, bf16[32,128,128]{2,1,0:T(8,128)(2,1)S(1)}, f32[8,128]{1,0:T(8,128)S(1)}) custom-call(s32[1]{0:T(128)} %bitcast.grid, s32[2,16]{1,0:T(2,128)S(1)} %copy-done.10, s32[2,256]{1,0:T(2,128)S(1)} %copy-done.11, ...), custom_call_target="tpu_custom_call", output_to_operand_aliasing={{0}: (13, {}), {1}: (14, {})} | custom-call | bytes 9000000 | tf_op jit(solution)/shard_map/pair_inverse/pallas_call | solution.py:481
  78.4 1.0 copy-done.1
  79.3 6.7 %all-to-all-start.2 = ((bf16[32,128,128]{2,1,0:T(8,128)(2,1)}), bf16[32,128,128]{2,1,0:T(8,128)(2,1)S(1)}, u32[]{:S(2)}, u32[]{:S(2)}) async-start(bf16[32,128,128]{2,1,0:T(8,128)(2,1)} %copy-done.1), calls=%async_computation.2 | async-start | bytes 2097152 | tf_op jit(solution)/shard_map/all_to_all | solution.py:422
  86.1 0.1 maximum_reduce_fusion
  86.2 13.8 %psum.7.energy = f32[24]{0:T(128)S(1)} all-reduce(f32[24]{0:T(128)S(1)} %maximum_reduce_fusion), channel_id=1, replica_groups=mesh['orb'=32,'grid'=8] {'grid'}, use_global_device_ids=true, to_apply=%region_1.2 | all-reduce | flops 24 | bytes 192 | tf_op jit(solution)/shard_map/psum | solution.py:493
  100.0 3.0 %all-to-all-done.2.arrived = bf16[32,128,128]{2,1,0:T(8,128)(2,1)S(1)} async-done(((bf16[32,128,128]{2,1,0:T(8,128)(2,1)}), bf16[32,128,128]{2,1,0:T(8,128)(2,1)S(1)}, u32[]{:S(2)}, u32[]{:S(2)}) %all-to-all-start.2) | async-done | bytes 1048608 | tf_op jit(solution)/shard_map/all_to_all | solution.py:422
  103.0 2.0 %gather.1 = (bf16[32,80,128]{2,1,0:T(8,128)(2,1)S(1)}, f32[8,128]{1,0:T(8,128)S(1)}) custom-call(s32[512]{0:T(512)S(1)} %reshape.540.partners, s32[2,16]{1,0:T(2,128)S(1)} %copy-done.10, bf16[32,128,128]{2,1,0:T(8,128)(2,1)S(1)} %all-to-all-done.2.arrived, f32[24]{0:T(128)S(1)} %psum.7.energy), custom_call_target="tpu_custom_call" | custom-call | bytes 12000000 | tf_op jit(solution)/shard_map/gather/pallas_call | solution.py:494
  105.0 19.7 %all_to_all.20.arrived = bf16[32,80,128]{2,1,0:T(8,128)(2,1)S(1)} all-to-all(bf16[32,80,128]{2,1,0:T(8,128)(2,1)S(1)} %get-tuple-element.77), channel_id=1, replica_groups=mesh['orb'=32,'grid'=8] {'orb'}, dimensions={0} | all-to-all | bytes 1310720 | tf_op jit(solution)/shard_map/all_to_all | solution.py:422
  124.7 1.0 finish.1
  (44 shorter events, 1.1 us)
Async XLA Ops:
  0.6 1.0 copy-start.2
  1.7 0.7 copy-start.9
  3.8 21.5 %all-to-all-start = ((bf16[32,80,128]{2,1,0:T(8,128)(2,1)}), bf16[32,80,128]{2,1,0:T(8,128)(2,1)S(1)}, u32[]{:S(2)}, u32[]{:S(2)}) async-start(bf16[32,80,128]{2,1,0:T(8,128)(2,1)} %spread.1), calls=%async_computation | async-start | bytes 1310720 | tf_op jit(solution)/shard_map/all_to_all | solution.py:422
  12.4 1.2 copy-start.3
  13.6 0.9 copy-start
  13.7 0.8 copy-start.4
  15.6 13.0 %copy-start.5 = (f32[8,64,128]{2,1,0:T(8,128)}, f32[8,64,128]{2,1,0:T(8,128)S(1)}, u32[]{:S(2)}) copy-start(f32[8,64,128]{2,1,0:T(8,128)S(1)} %get-tuple-element.44.ends) | copy-start | bytes 786436
  15.6 5.3 %collective-permute-start = (bf16[512,128]{1,0:T(8,128)(2,1)S(1)}, bf16[512,128]{1,0:T(8,128)(2,1)S(1)}, u32[]{:S(2)}, u32[]{:S(2)}) collective-permute-start(bf16[512,128]{1,0:T(8,128)(2,1)S(1)} %get-tuple-element.42), channel_id=1, source_target_pairs={{0,1},{1,0},{2,3},{3,2},{4,5},{5,4},{6,7},{7,6},{8,9},{9,8},{10,11... | collective-permute-start | bytes 393224 | tf_op jit(solution)/shard_map/ppermute | solution.py:425
  28.5 20.6 %all-to-all-start.1 = ((bf16[32,128,128]{2,1,0:T(8,128)(2,1)}), bf16[32,128,128]{2,1,0:T(8,128)(2,1)S(1)}, u32[]{:S(2)}, u32[]{:S(2)}) async-start(bf16[32,128,128]{2,1,0:T(8,128)(2,1)} %serve.1.refs_10_), calls=%async_computation.1 | async-start | bytes 2097152 | tf_op jit(solution)/shard_map/all_to_all | solution.py:422
  32.3 1.0 copy-start.6
  33.3 15.9 %copy-start.11 = (s32[2,256]{1,0:T(2,128)S(1)}, s32[2,256]{1,0:T(2,128)}, u32[]{:S(2)}) copy-start(s32[2,256]{1,0:T(2,128)} %anchor.7) | copy-start | bytes 6148
  33.3 10.6 %collective-permute-start.1 = (bf16[8,32,128]{2,1,0:T(8,128)(2,1)S(1)}, bf16[8,32,128]{2,1,0:T(8,128)(2,1)S(1)}, u32[]{:S(2)}, u32[]{:S(2)}) collective-permute-start(bf16[8,32,128]{2,1,0:T(8,128)(2,1)S(1)} %get-tuple-element.46), channel_id=1, source_target_pairs={{0,4},{1,5},{2,6},{3,7},{4,0},{5,1},{6,2},{7,3},{8,12},{9,13},{10,... | collective-permute-start | bytes 196616 | tf_op jit(solution)/shard_map/ppermute | solution.py:431
  40.3 8.9 %copy-start.10 = (s32[2,16]{1,0:T(2,128)S(1)}, s32[2,16]{1,0:T(2,128)}, u32[]{:S(2)}) copy-start(s32[2,16]{1,0:T(2,128)} %pairs.11) | copy-start | bytes 388
  40.3 6.7 %collective-permute-start.2 = (bf16[8,32,128]{2,1,0:T(8,128)(2,1)S(1)}, bf16[8,32,128]{2,1,0:T(8,128)(2,1)S(1)}, u32[]{:S(2)}, u32[]{:S(2)}) collective-permute-start(bf16[8,32,128]{2,1,0:T(8,128)(2,1)S(1)} %get-tuple-element.47), channel_id=1, source_target_pairs={{0,2},{1,3},{2,4},{3,5},{4,6},{5,7},{6,0},{7,1},{8,10},{9,11},{10,... | collective-permute-start | bytes 196616 | tf_op jit(solution)/shard_map/ppermute | solution.py:431
  41.5 5.5 %collective-permute-start.3 = (bf16[8,32,128]{2,1,0:T(8,128)(2,1)S(1)}, bf16[8,32,128]{2,1,0:T(8,128)(2,1)S(1)}, u32[]{:S(2)}, u32[]{:S(2)}) collective-permute-start(bf16[8,32,128]{2,1,0:T(8,128)(2,1)S(1)} %get-tuple-element.48), channel_id=1, source_target_pairs={{0,6},{1,7},{2,0},{3,1},{4,2},{5,3},{6,4},{7,5},{8,14},{9,15},{10,... | collective-permute-start | bytes 196616 | tf_op jit(solution)/shard_map/ppermute | solution.py:431
  47.0 0.6 copy-start.7
  51.1 3.7 %copy-start.8 = (bf16[8,32,128]{2,1,0:T(8,128)(2,1)S(1)}, bf16[8,32,128]{2,1,0:T(8,128)(2,1)}, u32[]{:S(2)}) copy-start(bf16[8,32,128]{2,1,0:T(8,128)(2,1)} %copy-done.7) | copy-start | bytes 196612
  51.1 5.4 %collective-permute-start.8 = (bf16[512,128]{1,0:T(8,128)(2,1)S(1)}, bf16[512,128]{1,0:T(8,128)(2,1)S(1)}, u32[]{:S(2)}, u32[]{:S(2)}) collective-permute-start(bf16[512,128]{1,0:T(8,128)(2,1)S(1)} %get-tuple-element.62), channel_id=1, source_target_pairs={{0,1},{1,0},{2,3},{3,2},{4,5},{5,4},{6,7},{7,6},{8,9},{9,8},{10,11... | collective-permute-start | bytes 393224 | tf_op jit(solution)/shard_map/ppermute | solution.py:425
  54.7 12.1 %collective-permute-start.4 = (bf16[512,128]{1,0:T(8,128)(2,1)S(1)}, bf16[512,128]{1,0:T(8,128)(2,1)S(1)}, u32[]{:S(2)}, u32[]{:S(2)}) collective-permute-start(bf16[512,128]{1,0:T(8,128)(2,1)S(1)} %get-tuple-element.50), channel_id=1, source_target_pairs={{0,1},{1,0},{2,3},{3,2},{4,5},{5,4},{6,7},{7,6},{8,9},{9,8},{10,11... | collective-permute-start | bytes 393224 | tf_op jit(solution)/shard_map/ppermute | solution.py:425
  56.6 12.4 %collective-permute-start.9 = (bf16[8,32,128]{2,1,0:T(8,128)(2,1)S(1)}, bf16[8,32,128]{2,1,0:T(8,128)(2,1)S(1)}, u32[]{:S(2)}, u32[]{:S(2)}) collective-permute-start(bf16[8,32,128]{2,1,0:T(8,128)(2,1)S(1)} %get-tuple-element.65), channel_id=1, source_target_pairs={{0,4},{1,5},{2,6},{3,7},{4,0},{5,1},{6,2},{7,3},{8,12},{9,13},{10,... | collective-permute-start | bytes 196616 | tf_op jit(solution)/shard_map/ppermute | solution.py:431
  63.2 8.2 %collective-permute-start.10 = (bf16[8,32,128]{2,1,0:T(8,128)(2,1)S(1)}, bf16[8,32,128]{2,1,0:T(8,128)(2,1)S(1)}, u32[]{:S(2)}, u32[]{:S(2)}) collective-permute-start(bf16[8,32,128]{2,1,0:T(8,128)(2,1)S(1)} %get-tuple-element.66), channel_id=1, source_target_pairs={{0,2},{1,3},{2,4},{3,5},{4,6},{5,7},{6,0},{7,1},{8,10},{9,11},{10,... | collective-permute-start | bytes 196616 | tf_op jit(solution)/shard_map/ppermute | solution.py:431
  64.4 7.0 %collective-permute-start.11 = (bf16[8,32,128]{2,1,0:T(8,128)(2,1)S(1)}, bf16[8,32,128]{2,1,0:T(8,128)(2,1)S(1)}, u32[]{:S(2)}, u32[]{:S(2)}) collective-permute-start(bf16[8,32,128]{2,1,0:T(8,128)(2,1)S(1)} %get-tuple-element.67), channel_id=1, source_target_pairs={{0,6},{1,7},{2,0},{3,1},{4,2},{5,3},{6,4},{7,5},{8,14},{9,15},{10,... | collective-permute-start | bytes 196616 | tf_op jit(solution)/shard_map/ppermute | solution.py:431
  66.9 8.1 %collective-permute-start.5 = (bf16[8,32,128]{2,1,0:T(8,128)(2,1)S(1)}, bf16[8,32,128]{2,1,0:T(8,128)(2,1)S(1)}, u32[]{:S(2)}, u32[]{:S(2)}) collective-permute-start(bf16[8,32,128]{2,1,0:T(8,128)(2,1)S(1)} %get-tuple-element.52), channel_id=1, source_target_pairs={{0,4},{1,5},{2,6},{3,7},{4,0},{5,1},{6,2},{7,3},{8,12},{9,13},{10,... | collective-permute-start | bytes 196616 | tf_op jit(solution)/shard_map/ppermute | solution.py:431
  67.9 7.0 %collective-permute-start.6 = (bf16[8,32,128]{2,1,0:T(8,128)(2,1)S(1)}, bf16[8,32,128]{2,1,0:T(8,128)(2,1)S(1)}, u32[]{:S(2)}, u32[]{:S(2)}) collective-permute-start(bf16[8,32,128]{2,1,0:T(8,128)(2,1)S(1)} %get-tuple-element.53), channel_id=1, source_target_pairs={{0,2},{1,3},{2,4},{3,5},{4,6},{5,7},{6,0},{7,1},{8,10},{9,11},{10,... | collective-permute-start | bytes 196616 | tf_op jit(solution)/shard_map/ppermute | solution.py:431
  69.0 6.9 %collective-permute-start.7 = (bf16[8,32,128]{2,1,0:T(8,128)(2,1)S(1)}, bf16[8,32,128]{2,1,0:T(8,128)(2,1)S(1)}, u32[]{:S(2)}, u32[]{:S(2)}) collective-permute-start(bf16[8,32,128]{2,1,0:T(8,128)(2,1)S(1)} %get-tuple-element.54), channel_id=1, source_target_pairs={{0,6},{1,7},{2,0},{3,1},{4,2},{5,3},{6,4},{7,5},{8,14},{9,15},{10,... | collective-permute-start | bytes 196616 | tf_op jit(solution)/shard_map/ppermute | solution.py:431
  78.4 1.0 copy-start.1
  79.3 23.7 %all-to-all-start.2 = ((bf16[32,128,128]{2,1,0:T(8,128)(2,1)}), bf16[32,128,128]{2,1,0:T(8,128)(2,1)S(1)}, u32[]{:S(2)}, u32[]{:S(2)}) async-start(bf16[32,128,128]{2,1,0:T(8,128)(2,1)} %copy-done.1), calls=%async_computation.2 | async-start | bytes 2097152 | tf_op jit(solution)/shard_map/all_to_all | solution.py:422

commit v4 on v3

--- a/solution.py
+++ b/solution.py
@@ -20,6 +20,7 @@
 UP, DOWN, MIDDLE, CARRY, PAST_UP, PAST_DOWN = 0, 8, 16, 24, 27, 28
 ORB_DEV = 8
 ENTRIES = 16
+EXTRA = 8
 HALF = ENTRIES // 2
 PAD = 10
 MU2 = 0.02
@@ -221,10 +222,11 @@
 
 def spread_kernel(pairs, orb, out):
     wide = [orb[n].astype(F32) for n in range(ORB_DEV)]
-    rows = lax.broadcasted_iota(jnp.int32, (ENTRIES, LANES), 0)
-    partners = jnp.zeros((ENTRIES, LANES), F32)
+    place = lax.broadcasted_iota(jnp.int32, (EXTRA, LANES), 0) * 2 + lane_iota(EXTRA)
+    partners = jnp.zeros((EXTRA, LANES), F32)
     for n in range(ENTRIES):
-        partners = jnp.where(rows == n, pairs[1, n].astype(F32), partners)
+        here = (place == n) & (lane_iota(EXTRA) < 2)
+        partners = jnp.where(here, pairs[1, n].astype(F32), partners)
     partners = partners.astype(BF16)
     for t in range(TILES):
         piece = jnp.concatenate([w[:, LANES * t : LANES * (t + 1)] for w in wide], axis=0)
@@ -359,7 +361,8 @@
         out[d, : ORB_DEV * PLANES, :] = jnp.concatenate(pieces, axis=0).astype(BF16)
         value = every_energy[ORB_DEV * d : ORB_DEV * (d + 1), :]
         high = value.astype(BF16).astype(F32)
-        out[d, ORB_DEV * PLANES :, :] = jnp.concatenate([high, value - high], axis=0).astype(BF16)
+        low = pltpu.roll(value - high, 1, 1)
+        out[d, ORB_DEV * PLANES :, :] = jnp.where(lane_iota(ORB_DEV) == 1, low, high).astype(BF16)
 
 
 def finish_kernel(arrived, total, energy, out, energy_out):
@@ -369,8 +372,7 @@
         for n in range(ORB_DEV):
             here = total[n, PLANES * t : PLANES * (t + 1), :] + tile(pieces, n)
             out[n, :, LANES * t : LANES * (t + 1)] = here.astype(BF16)
-        both = arrived[t, ORB_DEV * PLANES :, :].astype(F32)
-        sums += both[:ORB_DEV] + both[ORB_DEV:]
+        sums += arrived[t, ORB_DEV * PLANES :, :].astype(F32)
     for n in range(ORB_DEV):
         energy_out[n] = jnp.sum(sums[n : n + 1, :])
 
@@ -394,7 +396,7 @@
     ]
 
 
-def call(kernel, out_shape, in_specs, scratch, name, micros, out_specs=None, aliases=None):
+def call(kernel, out_shape, in_specs, scratch, name, micros, out_specs=None, aliases=None, limit=VMEM_LIMIT):
     return pl.pallas_call(
         kernel,
         out_shape=out_shape,
@@ -404,7 +406,7 @@
         input_output_aliases=aliases or {},
         name=name,
         cost_estimate=pl.CostEstimate(flops=0, bytes_accessed=int(micros * 3.0e6), transcendentals=0),
-        compiler_params=pltpu.CompilerParams(vmem_limit_bytes=VMEM_LIMIT),
+        compiler_params=pltpu.CompilerParams(vmem_limit_bytes=limit),
     )
 
 
@@ -415,7 +417,7 @@
     y_right, x_left = sine_factors()
     z_table = z_factors(grid_index)
     tables = (y_right, x_left, z_table)
-    spread = ORB_DEV * PLANES + ENTRIES
+    spread = ORB_DEV * PLANES + EXTRA
     totals = shape(ORB_DEV, ROWS, LANES, dtype=F32)
 
     def to_all(blocks):
@@ -430,9 +432,9 @@
         hops = [[(i, (i + 2 * e) % GRID) for i in range(GRID)] for e in ORDER]
         return [lax.ppermute(sums[e - 1], "grid", hop) for e, hop in zip(ORDER, hops)]
 
-    pieces = call(spread_kernel, shape(devices, spread, LANES), [SMEM, VMEM], [], "spread", 1)(
-        pair_list, orbitals
-    )
+    pieces = call(
+        spread_kernel, shape(devices, spread, LANES), [SMEM, VMEM], [], "spread", 1, limit=62 * 1024 * 1024
+    )(pair_list, orbitals)
     orbitals, _ = lax.optimization_barrier((orbitals, pieces))
     orb_rows = call(rows_kernel, shape(ORB_DEV, ROWS, LANES), [VMEM], [], "rows", 1)(orbitals)
     pieces = to_all(pieces)
@@ -440,7 +442,7 @@
         base_forward_kernel, solve_shapes(ORB_DEV), [VMEM] * 4, [HELD] * ORB_DEV, "base_forward", 2
     )(orb_rows, *tables)
     pieces, base_near = lax.optimization_barrier((pieces, to_near(message)))
-    partners = pieces[:, ORB_DEV * PLANES :, 0].astype(jnp.int32).reshape(-1)
+    partners = pieces[:, ORB_DEV * PLANES :, :2].astype(jnp.int32).reshape(-1)
     served = call(
         serve_kernel,
         shape(devices, ENTRIES * PLANES, LANES),

time: 126 us -> 123 us (0.976)
  local copies, waits for them, and re-layouts: 5.54 us -> 3.82 us
    unnamed x24 -> x20, local copies, waits for them, and re-layouts: 5.02 us -> 3.25 us
where the time goes in v4:
time: 123 us
  starting transfers between devices  47.8 us (39%)
  blocking collectives  32.9 us (27%)
  Pallas kernels  18.5 us (15%)
  waiting for transfers between devices  17.9 us (15%)
  local copies, waits for them, and re-layouts  3.82 us (3%)
    ppermute x9, starting transfers between devices, from_pairs(): lax.ppermute(sums[e - 1], 'grid', hop)  25.4 us
    all_to_all x3, starting transfers between devices, to_all(): lax.all_to_all(blocks, 'orb', split_axis=0, concat_axis=0, tiled=True)  19 us
    all_to_all x1, blocking collectives, to_all(): lax.all_to_all(blocks, 'orb', split_axis=0, concat_axis=0, tiled=True)  19 us
    psum x1, blocking collectives, local(): energy = lax.psum(jnp.sum(jnp.concatenate(energy), axis=1), 'grid')  13.9 us
    all_to_all x3, waiting for transfers between devices, to_all(): lax.all_to_all(blocks, 'orb', split_axis=0, concat_axis=0, tiled=True)  8.44 us
    ppermute x9, waiting for transfers between devices, from_pairs(): lax.ppermute(sums[e - 1], 'grid', hop)  5.58 us
    pallas_call x2, Pallas kernels, local(): call(functools.partial(pair_inverse_kernel, start), [totals, shape(device...  4.72 us
    ppermute x3, waiting for transfers between devices, to_near(): return lax.ppermute(message, 'grid', [(i, i ^ 1) for i in range(GRID)])  3.91 us
  transfers between devices with their start and end apart: 15, of which 8 were waited for; matrix products, arithmetic and copies ran while one was open for 1% of the time, Pallas kernels for 5%

profile of v4, /device:TPU:1, one launch (start us, length us, event | category | flops | bytes accessed | tf_op | source)
XLA Modules:
  0.0 122.9 jit_solution(8599983968404191047)
XLA Ops:
  0.6 1.9 %spread.1 = bf16[32,72,128]{2,1,0:T(8,128)(2,1)} custom-call(s32[2,16]{1,0:T(2,128)} %pairs.11, bf16[8,8,4096]{2,1,0:T(8,128)(2,1)} %orb.2), custom_call_target="tpu_custom_call" | custom-call | bytes 3000000 | tf_op jit(solution)/shard_map/spread/pallas_call | solution.py:435
  2.6 8.7 %all-to-all-start = ((bf16[32,72,128]{2,1,0:T(8,128)(2,1)}), bf16[32,72,128]{2,1,0:T(8,128)(2,1)S(1)}, u32[]{:S(2)}, u32[]{:S(2)}) async-start(bf16[32,72,128]{2,1,0:T(8,128)(2,1)} %spread.1), calls=%async_computation | async-start | bytes 1179648 | tf_op jit(solution)/shard_map/all_to_all | solution.py:424
  11.5 0.1 copy.10
  11.7 0.1 add.681
  12.1 0.1 divide_dynamic-update-slice_fusion.1
  12.2 0.1 divide_dynamic-update-slice_fusion
  12.3 0.1 multiply_dynamic-update-slice_fusion
  12.5 0.1 divide_dynamic-update-slice_fusion.2
  12.7 0.6 copy-done
  13.2 0.1 copy-done.3
  13.4 1.0 base_forward.1
  14.4 1.7 %collective-permute-start = (bf16[512,128]{1,0:T(8,128)(2,1)S(1)}, bf16[512,128]{1,0:T(8,128)(2,1)S(1)}, u32[]{:S(2)}, u32[]{:S(2)}) collective-permute-start(bf16[512,128]{1,0:T(8,128)(2,1)S(1)} %get-tuple-element.42), channel_id=1, source_target_pairs={{0,1},{1,0},{2,3},{3,2},{4,5},{5,4},{6,7},{7,6},{8,9},{9,8},{10,11... | collective-permute-start | bytes 393224 | tf_op jit(solution)/shard_map/ppermute | solution.py:427
  16.1 3.6 %collective-permute-done.near = bf16[512,128]{1,0:T(8,128)(2,1)S(1)} collective-permute-done((bf16[512,128]{1,0:T(8,128)(2,1)S(1)}, bf16[512,128]{1,0:T(8,128)(2,1)S(1)}, u32[]{:S(2)}, u32[]{:S(2)}) %collective-permute-start) | collective-permute-done | bytes 131104 | tf_op jit(solution)/shard_map/ppermute | solution.py:427
  19.7 3.9 %all-to-all-done.held = bf16[32,72,128]{2,1,0:T(8,128)(2,1)S(1)} async-done(((bf16[32,72,128]{2,1,0:T(8,128)(2,1)}), bf16[32,72,128]{2,1,0:T(8,128)(2,1)S(1)}, u32[]{:S(2)}, u32[]{:S(2)}) %all-to-all-start) | async-done | bytes 589856 | tf_op jit(solution)/shard_map/all_to_all | solution.py:424
  23.6 0.1 reshape.544.partners
  23.7 2.5 %serve.1.refs_10_ = bf16[32,128,128]{2,1,0:T(8,128)(2,1)} custom-call(s32[512]{0:T(512)S(1)} %reshape.544.partners, bf16[32,72,128]{2,1,0:T(8,128)(2,1)S(1)} %all-to-all-done.held), custom_call_target="tpu_custom_call" | custom-call | bytes 6000000 | tf_op jit(solution)/shard_map/serve/pallas_call | solution.py:446
  26.2 4.0 %all-to-all-start.1 = ((bf16[32,128,128]{2,1,0:T(8,128)(2,1)}), bf16[32,128,128]{2,1,0:T(8,128)(2,1)S(1)}, u32[]{:S(2)}, u32[]{:S(2)}) async-start(bf16[32,128,128]{2,1,0:T(8,128)(2,1)} %serve.1.refs_10_), calls=%async_computation.1 | async-start | bytes 2097152 | tf_op jit(solution)/shard_map/all_to_all | solution.py:424
  30.3 0.9 copy-done.5
  31.3 6.8 %collective-permute-start.1 = (bf16[8,32,128]{2,1,0:T(8,128)(2,1)S(1)}, bf16[8,32,128]{2,1,0:T(8,128)(2,1)S(1)}, u32[]{:S(2)}, u32[]{:S(2)}) collective-permute-start(bf16[8,32,128]{2,1,0:T(8,128)(2,1)S(1)} %get-tuple-element.46), channel_id=1, source_target_pairs={{0,4},{1,5},{2,6},{3,7},{4,0},{5,1},{6,2},{7,3},{8,12},{9,13},{10,... | collective-permute-start | bytes 196616 | tf_op jit(solution)/shard_map/ppermute | solution.py:433
  38.1 1.2 collective-permute-start.2
  39.3 2.4 %collective-permute-start.3 = (bf16[8,32,128]{2,1,0:T(8,128)(2,1)S(1)}, bf16[8,32,128]{2,1,0:T(8,128)(2,1)S(1)}, u32[]{:S(2)}, u32[]{:S(2)}) collective-permute-start(bf16[8,32,128]{2,1,0:T(8,128)(2,1)S(1)} %get-tuple-element.48), channel_id=1, source_target_pairs={{0,6},{1,7},{2,0},{3,1},{4,2},{5,3},{6,4},{7,5},{8,14},{9,15},{10,... | collective-permute-start | bytes 196616 | tf_op jit(solution)/shard_map/ppermute | solution.py:433
  41.7 3.3 %collective-permute-done.2.refs_1_ = bf16[8,32,128]{2,1,0:T(8,128)(2,1)S(1)} collective-permute-done((bf16[8,32,128]{2,1,0:T(8,128)(2,1)S(1)}, bf16[8,32,128]{2,1,0:T(8,128)(2,1)S(1)}, u32[]{:S(2)}, u32[]{:S(2)}) %collective-permute-start.2) | collective-permute-done | bytes 65568 | tf_op jit(solution)/shard_map/ppermute | solution.py:433
  44.9 0.6 copy-done.6
  45.6 1.6 %all-to-all-done.1.fetched = bf16[32,128,128]{2,1,0:T(8,128)(2,1)S(1)} async-done(((bf16[32,128,128]{2,1,0:T(8,128)(2,1)}), bf16[32,128,128]{2,1,0:T(8,128)(2,1)S(1)}, u32[]{:S(2)}, u32[]{:S(2)}) %all-to-all-start.1) | async-done | bytes 1048608 | tf_op jit(solution)/shard_map/all_to_all | solution.py:424
  47.2 1.9 %pair_forward.3 = (bf16[8,256,128]{2,1,0:T(8,128)(2,1)S(1)}, f32[8,256,128]{2,1,0:T(8,128)S(1)}, f32[8,64,128]{2,1,0:T(8,128)S(1)}, bf16[512,128]{1,0:T(8,128)(2,1)S(1)}) custom-call(s32[2,16]{1,0:T(2,128)S(1)} %copy-done.8, s32[2,256]{1,0:T(2,128)S(1)} %copy-done.9, bf16[8,256,128]{2,1,0:T(8,128)(2,1)S(1)} %rows.1.orb_rows.refs_4_, ...), custom_call_target="tpu_custom_call" | custom-call | bytes 6000000 | tf_op jit(solution)/shard_map/pair_forward/pallas_call | solution.py:468
  49.1 1.5 %collective-permute-start.8 = (bf16[512,128]{1,0:T(8,128)(2,1)S(1)}, bf16[512,128]{1,0:T(8,128)(2,1)S(1)}, u32[]{:S(2)}, u32[]{:S(2)}) collective-permute-start(bf16[512,128]{1,0:T(8,128)(2,1)S(1)} %get-tuple-element.62), channel_id=1, source_target_pairs={{0,1},{1,0},{2,3},{3,2},{4,5},{5,4},{6,7},{7,6},{8,9},{9,8},{10,11... | collective-permute-start | bytes 393224 | tf_op jit(solution)/shard_map/ppermute | solution.py:427
  50.6 1.9 %pair_forward.2 = (bf16[8,256,128]{2,1,0:T(8,128)(2,1)S(1)}, f32[8,256,128]{2,1,0:T(8,128)S(1)}, f32[8,64,128]{2,1,0:T(8,128)S(1)}, bf16[512,128]{1,0:T(8,128)(2,1)S(1)}) custom-call(s32[2,16]{1,0:T(2,128)S(1)} %copy-done.8, s32[2,256]{1,0:T(2,128)S(1)} %copy-done.9, bf16[8,256,128]{2,1,0:T(8,128)(2,1)S(1)} %rows.1.orb_rows.refs_4_, ...), custom_call_target="tpu_custom_call" | custom-call | bytes 6000000 | tf_op jit(solution)/shard_map/pair_forward/pallas_call | solution.py:468
  52.5 0.1 collective-permute-start.4
  52.6 1.2 base_inverse.1
  53.8 0.3 collective-permute-done.8.near
  54.2 6.8 %collective-permute-start.9 = (bf16[8,32,128]{2,1,0:T(8,128)(2,1)S(1)}, bf16[8,32,128]{2,1,0:T(8,128)(2,1)S(1)}, u32[]{:S(2)}, u32[]{:S(2)}) collective-permute-start(bf16[8,32,128]{2,1,0:T(8,128)(2,1)S(1)} %get-tuple-element.65), channel_id=1, source_target_pairs={{0,4},{1,5},{2,6},{3,7},{4,0},{5,1},{6,2},{7,3},{8,12},{9,13},{10,... | collective-permute-start | bytes 196616 | tf_op jit(solution)/shard_map/ppermute | solution.py:433
  61.0 1.2 collective-permute-start.10
  62.2 2.4 %collective-permute-start.11 = (bf16[8,32,128]{2,1,0:T(8,128)(2,1)S(1)}, bf16[8,32,128]{2,1,0:T(8,128)(2,1)S(1)}, u32[]{:S(2)}, u32[]{:S(2)}) collective-permute-start(bf16[8,32,128]{2,1,0:T(8,128)(2,1)S(1)} %get-tuple-element.67), channel_id=1, source_target_pairs={{0,6},{1,7},{2,0},{3,1},{4,2},{5,3},{6,4},{7,5},{8,14},{9,15},{10,... | collective-permute-start | bytes 196616 | tf_op jit(solution)/shard_map/ppermute | solution.py:433
  64.7 1.0 collective-permute-start.5
  65.7 1.2 collective-permute-start.6
  66.9 2.4 %collective-permute-start.7 = (bf16[8,32,128]{2,1,0:T(8,128)(2,1)S(1)}, bf16[8,32,128]{2,1,0:T(8,128)(2,1)S(1)}, u32[]{:S(2)}, u32[]{:S(2)}) collective-permute-start(bf16[8,32,128]{2,1,0:T(8,128)(2,1)S(1)} %get-tuple-element.54), channel_id=1, source_target_pairs={{0,6},{1,7},{2,0},{3,1},{4,2},{5,3},{6,4},{7,5},{8,14},{9,15},{10,... | collective-permute-start | bytes 196616 | tf_op jit(solution)/shard_map/ppermute | solution.py:433
  69.3 2.3 %pair_inverse.2 = (f32[8,256,128]{2,1,0:T(8,128)S(1)}, bf16[32,128,128]{2,1,0:T(8,128)(2,1)S(1)}, f32[8,128]{1,0:T(8,128)S(1)}) custom-call(s32[1]{0:T(128)} %bitcast.grid, s32[2,16]{1,0:T(2,128)S(1)} %copy-done.8, s32[2,256]{1,0:T(2,128)S(1)} %copy-done.9, bf16[512,128]{1,0:T(8,128)(2,1)S(1)} %collective-permute-done.8.near, ...), custom_call_target="tpu_custom_call", output_to_operand_aliasing={{0}: (13, {})} | custom-call | bytes 9000000 | tf_op jit(solution)/shard_map/pair_inverse/pallas_call | solution.py:483
  71.6 1.1 collective-permute-done.5.refs_0_
  72.7 1.3 %collective-permute-done.7.refs_2_ = bf16[8,32,128]{2,1,0:T(8,128)(2,1)S(1)} collective-permute-done((bf16[8,32,128]{2,1,0:T(8,128)(2,1)S(1)}, bf16[8,32,128]{2,1,0:T(8,128)(2,1)S(1)}, u32[]{:S(2)}, u32[]{:S(2)}) %collective-permute-start.7) | collective-permute-done | bytes 65568 | tf_op jit(solution)/shard_map/ppermute | solution.py:433
  73.9 2.4 %pair_inverse.3 = (f32[8,256,128]{2,1,0:T(8,128)S(1)}, bf16[32,128,128]{2,1,0:T(8,128)(2,1)S(1)}, f32[8,128]{1,0:T(8,128)S(1)}) custom-call(s32[1]{0:T(128)} %bitcast.grid, s32[2,16]{1,0:T(2,128)S(1)} %copy-done.8, s32[2,256]{1,0:T(2,128)S(1)} %copy-done.9, ...), custom_call_target="tpu_custom_call", output_to_operand_aliasing={{0}: (13, {}), {1}: (14, {})} | custom-call | bytes 9000000 | tf_op jit(solution)/shard_map/pair_inverse/pallas_call | solution.py:483
  76.3 1.0 copy-done.1
  77.3 6.3 %all-to-all-start.2 = ((bf16[32,128,128]{2,1,0:T(8,128)(2,1)}), bf16[32,128,128]{2,1,0:T(8,128)(2,1)S(1)}, u32[]{:S(2)}, u32[]{:S(2)}) async-start(bf16[32,128,128]{2,1,0:T(8,128)(2,1)} %copy-done.1), calls=%async_computation.2 | async-start | bytes 2097152 | tf_op jit(solution)/shard_map/all_to_all | solution.py:424
  83.6 0.1 maximum_reduce_fusion
  83.7 13.9 %psum.7.energy = f32[24]{0:T(128)S(1)} all-reduce(f32[24]{0:T(128)S(1)} %maximum_reduce_fusion), channel_id=1, replica_groups=mesh['orb'=32,'grid'=8] {'grid'}, use_global_device_ids=true, to_apply=%region_1.2 | all-reduce | flops 24 | bytes 192 | tf_op jit(solution)/shard_map/psum | solution.py:495
  97.6 3.0 %all-to-all-done.2.arrived = bf16[32,128,128]{2,1,0:T(8,128)(2,1)S(1)} async-done(((bf16[32,128,128]{2,1,0:T(8,128)(2,1)}), bf16[32,128,128]{2,1,0:T(8,128)(2,1)S(1)}, u32[]{:S(2)}, u32[]{:S(2)}) %all-to-all-start.2) | async-done | bytes 1048608 | tf_op jit(solution)/shard_map/all_to_all | solution.py:424
  100.6 2.1 %gather.1 = (bf16[32,72,128]{2,1,0:T(8,128)(2,1)S(1)}, f32[8,128]{1,0:T(8,128)S(1)}) custom-call(s32[512]{0:T(512)S(1)} %reshape.544.partners, s32[2,16]{1,0:T(2,128)S(1)} %copy-done.8, bf16[32,128,128]{2,1,0:T(8,128)(2,1)S(1)} %all-to-all-done.2.arrived, f32[24]{0:T(128)S(1)} %psum.7.energy), custom_call_target="tpu_custom_call" | custom-call | bytes 12000000 | tf_op jit(solution)/shard_map/gather/pallas_call | solution.py:496
  102.7 19.0 %all_to_all.20.arrived = bf16[32,72,128]{2,1,0:T(8,128)(2,1)S(1)} all-to-all(bf16[32,72,128]{2,1,0:T(8,128)(2,1)S(1)} %get-tuple-element.77), channel_id=1, replica_groups=mesh['orb'=32,'grid'=8] {'orb'}, dimensions={0} | all-to-all | bytes 1179648 | tf_op jit(solution)/shard_map/all_to_all | solution.py:424
  121.7 1.0 finish.1
  (40 shorter events, 0.9 us)
Async XLA Ops:
  2.6 9.4 %copy-start.2 = (bf16[8,8,4096]{2,1,0:T(8,128)(2,1)S(1)}, bf16[8,8,4096]{2,1,0:T(8,128)(2,1)}, u32[]{:S(2)}) copy-start(bf16[8,8,4096]{2,1,0:T(8,128)(2,1)} %orb.2) | copy-start | bytes 1572868
  2.6 21.0 %all-to-all-start = ((bf16[32,72,128]{2,1,0:T(8,128)(2,1)}), bf16[32,72,128]{2,1,0:T(8,128)(2,1)S(1)}, u32[]{:S(2)}, u32[]{:S(2)}) async-start(bf16[32,72,128]{2,1,0:T(8,128)(2,1)} %spread.1), calls=%async_computation | async-start | bytes 1179648 | tf_op jit(solution)/shard_map/all_to_all | solution.py:424
  12.3 0.9 copy-start
  12.6 0.8 copy-start.3
  14.4 11.8 %copy-start.4 = (f32[8,64,128]{2,1,0:T(8,128)}, f32[8,64,128]{2,1,0:T(8,128)S(1)}, u32[]{:S(2)}) copy-start(f32[8,64,128]{2,1,0:T(8,128)S(1)} %get-tuple-element.44.ends) | copy-start | bytes 786436
  14.4 5.3 %collective-permute-start = (bf16[512,128]{1,0:T(8,128)(2,1)S(1)}, bf16[512,128]{1,0:T(8,128)(2,1)S(1)}, u32[]{:S(2)}, u32[]{:S(2)}) collective-permute-start(bf16[512,128]{1,0:T(8,128)(2,1)S(1)} %get-tuple-element.42), channel_id=1, source_target_pairs={{0,1},{1,0},{2,3},{3,2},{4,5},{5,4},{6,7},{7,6},{8,9},{9,8},{10,11... | collective-permute-start | bytes 393224 | tf_op jit(solution)/shard_map/ppermute | solution.py:427
  26.2 20.9 %all-to-all-start.1 = ((bf16[32,128,128]{2,1,0:T(8,128)(2,1)}), bf16[32,128,128]{2,1,0:T(8,128)(2,1)S(1)}, u32[]{:S(2)}, u32[]{:S(2)}) async-start(bf16[32,128,128]{2,1,0:T(8,128)(2,1)} %serve.1.refs_10_), calls=%async_computation.1 | async-start | bytes 2097152 | tf_op jit(solution)/shard_map/all_to_all | solution.py:424
  30.2 1.0 copy-start.5
  31.3 15.9 %copy-start.9 = (s32[2,256]{1,0:T(2,128)S(1)}, s32[2,256]{1,0:T(2,128)}, u32[]{:S(2)}) copy-start(s32[2,256]{1,0:T(2,128)} %anchor.7) | copy-start | bytes 6148
  31.3 10.4 %collective-permute-start.1 = (bf16[8,32,128]{2,1,0:T(8,128)(2,1)S(1)}, bf16[8,32,128]{2,1,0:T(8,128)(2,1)S(1)}, u32[]{:S(2)}, u32[]{:S(2)}) collective-permute-start(bf16[8,32,128]{2,1,0:T(8,128)(2,1)S(1)} %get-tuple-element.46), channel_id=1, source_target_pairs={{0,4},{1,5},{2,6},{3,7},{4,0},{5,1},{6,2},{7,3},{8,12},{9,13},{10,... | collective-permute-start | bytes 196616 | tf_op jit(solution)/shard_map/ppermute | solution.py:433
  38.1 9.1 %copy-start.8 = (s32[2,16]{1,0:T(2,128)S(1)}, s32[2,16]{1,0:T(2,128)}, u32[]{:S(2)}) copy-start(s32[2,16]{1,0:T(2,128)} %pairs.11) | copy-start | bytes 388
  38.1 6.8 %collective-permute-start.2 = (bf16[8,32,128]{2,1,0:T(8,128)(2,1)S(1)}, bf16[8,32,128]{2,1,0:T(8,128)(2,1)S(1)}, u32[]{:S(2)}, u32[]{:S(2)}) collective-permute-start(bf16[8,32,128]{2,1,0:T(8,128)(2,1)S(1)} %get-tuple-element.47), channel_id=1, source_target_pairs={{0,2},{1,3},{2,4},{3,5},{4,6},{5,7},{6,0},{7,1},{8,10},{9,11},{10,... | collective-permute-start | bytes 196616 | tf_op jit(solution)/shard_map/ppermute | solution.py:433
  39.3 5.6 %collective-permute-start.3 = (bf16[8,32,128]{2,1,0:T(8,128)(2,1)S(1)}, bf16[8,32,128]{2,1,0:T(8,128)(2,1)S(1)}, u32[]{:S(2)}, u32[]{:S(2)}) collective-permute-start(bf16[8,32,128]{2,1,0:T(8,128)(2,1)S(1)} %get-tuple-element.48), channel_id=1, source_target_pairs={{0,6},{1,7},{2,0},{3,1},{4,2},{5,3},{6,4},{7,5},{8,14},{9,15},{10,... | collective-permute-start | bytes 196616 | tf_op jit(solution)/shard_map/ppermute | solution.py:433
  44.9 0.6 copy-start.6
  49.1 3.6 %copy-start.7 = (bf16[8,32,128]{2,1,0:T(8,128)(2,1)S(1)}, bf16[8,32,128]{2,1,0:T(8,128)(2,1)}, u32[]{:S(2)}) copy-start(bf16[8,32,128]{2,1,0:T(8,128)(2,1)} %copy-done.6) | copy-start | bytes 196612
  49.1 5.1 %collective-permute-start.8 = (bf16[512,128]{1,0:T(8,128)(2,1)S(1)}, bf16[512,128]{1,0:T(8,128)(2,1)S(1)}, u32[]{:S(2)}, u32[]{:S(2)}) collective-permute-start(bf16[512,128]{1,0:T(8,128)(2,1)S(1)} %get-tuple-element.62), channel_id=1, source_target_pairs={{0,1},{1,0},{2,3},{3,2},{4,5},{5,4},{6,7},{7,6},{8,9},{9,8},{10,11... | collective-permute-start | bytes 393224 | tf_op jit(solution)/shard_map/ppermute | solution.py:427
  52.5 12.1 %collective-permute-start.4 = (bf16[512,128]{1,0:T(8,128)(2,1)S(1)}, bf16[512,128]{1,0:T(8,128)(2,1)S(1)}, u32[]{:S(2)}, u32[]{:S(2)}) collective-permute-start(bf16[512,128]{1,0:T(8,128)(2,1)S(1)} %get-tuple-element.50), channel_id=1, source_target_pairs={{0,1},{1,0},{2,3},{3,2},{4,5},{5,4},{6,7},{7,6},{8,9},{9,8},{10,11... | collective-permute-start | bytes 393224 | tf_op jit(solution)/shard_map/ppermute | solution.py:427
  54.2 12.6 %collective-permute-start.9 = (bf16[8,32,128]{2,1,0:T(8,128)(2,1)S(1)}, bf16[8,32,128]{2,1,0:T(8,128)(2,1)S(1)}, u32[]{:S(2)}, u32[]{:S(2)}) collective-permute-start(bf16[8,32,128]{2,1,0:T(8,128)(2,1)S(1)} %get-tuple-element.65), channel_id=1, source_target_pairs={{0,4},{1,5},{2,6},{3,7},{4,0},{5,1},{6,2},{7,3},{8,12},{9,13},{10,... | collective-permute-start | bytes 196616 | tf_op jit(solution)/shard_map/ppermute | solution.py:433
  61.0 8.2 %collective-permute-start.10 = (bf16[8,32,128]{2,1,0:T(8,128)(2,1)S(1)}, bf16[8,32,128]{2,1,0:T(8,128)(2,1)S(1)}, u32[]{:S(2)}, u32[]{:S(2)}) collective-permute-start(bf16[8,32,128]{2,1,0:T(8,128)(2,1)S(1)} %get-tuple-element.66), channel_id=1, source_target_pairs={{0,2},{1,3},{2,4},{3,5},{4,6},{5,7},{6,0},{7,1},{8,10},{9,11},{10,... | collective-permute-start | bytes 196616 | tf_op jit(solution)/shard_map/ppermute | solution.py:433
  62.2 7.0 %collective-permute-start.11 = (bf16[8,32,128]{2,1,0:T(8,128)(2,1)S(1)}, bf16[8,32,128]{2,1,0:T(8,128)(2,1)S(1)}, u32[]{:S(2)}, u32[]{:S(2)}) collective-permute-start(bf16[8,32,128]{2,1,0:T(8,128)(2,1)S(1)} %get-tuple-element.67), channel_id=1, source_target_pairs={{0,6},{1,7},{2,0},{3,1},{4,2},{5,3},{6,4},{7,5},{8,14},{9,15},{10,... | collective-permute-start | bytes 196616 | tf_op jit(solution)/shard_map/ppermute | solution.py:433
  64.7 8.0 %collective-permute-start.5 = (bf16[8,32,128]{2,1,0:T(8,128)(2,1)S(1)}, bf16[8,32,128]{2,1,0:T(8,128)(2,1)S(1)}, u32[]{:S(2)}, u32[]{:S(2)}) collective-permute-start(bf16[8,32,128]{2,1,0:T(8,128)(2,1)S(1)} %get-tuple-element.52), channel_id=1, source_target_pairs={{0,4},{1,5},{2,6},{3,7},{4,0},{5,1},{6,2},{7,3},{8,12},{9,13},{10,... | collective-permute-start | bytes 196616 | tf_op jit(solution)/shard_map/ppermute | solution.py:433
  65.7 7.0 %collective-permute-start.6 = (bf16[8,32,128]{2,1,0:T(8,128)(2,1)S(1)}, bf16[8,32,128]{2,1,0:T(8,128)(2,1)S(1)}, u32[]{:S(2)}, u32[]{:S(2)}) collective-permute-start(bf16[8,32,128]{2,1,0:T(8,128)(2,1)S(1)} %get-tuple-element.53), channel_id=1, source_target_pairs={{0,2},{1,3},{2,4},{3,5},{4,6},{5,7},{6,0},{7,1},{8,10},{9,11},{10,... | collective-permute-start | bytes 196616 | tf_op jit(solution)/shard_map/ppermute | solution.py:433
  66.9 7.1 %collective-permute-start.7 = (bf16[8,32,128]{2,1,0:T(8,128)(2,1)S(1)}, bf16[8,32,128]{2,1,0:T(8,128)(2,1)S(1)}, u32[]{:S(2)}, u32[]{:S(2)}) collective-permute-start(bf16[8,32,128]{2,1,0:T(8,128)(2,1)S(1)} %get-tuple-element.54), channel_id=1, source_target_pairs={{0,6},{1,7},{2,0},{3,1},{4,2},{5,3},{6,4},{7,5},{8,14},{9,15},{10,... | collective-permute-start | bytes 196616 | tf_op jit(solution)/shard_map/ppermute | solution.py:433
  76.3 1.0 copy-start.1
  77.3 23.3 %all-to-all-start.2 = ((bf16[32,128,128]{2,1,0:T(8,128)(2,1)}), bf16[32,128,128]{2,1,0:T(8,128)(2,1)S(1)}, u32[]{:S(2)}, u32[]{:S(2)}) async-start(bf16[32,128,128]{2,1,0:T(8,128)(2,1)} %copy-done.1), calls=%async_computation.2 | async-start | bytes 2097152 | tf_op jit(solution)/shard_map/all_to_all | solution.py:424

commit v5 on v4

--- a/solution.py
+++ b/solution.py
@@ -21,7 +21,7 @@
 ORB_DEV = 8
 ENTRIES = 16
 EXTRA = 8
-HALF = ENTRIES // 2
+PARTS = ((0, 8), (8, 8))
 PAD = 10
 MU2 = 0.02
 BF16 = jnp.bfloat16
@@ -202,7 +202,7 @@
 
 
 def pair_scalars(pairs, anchor, n):
-    owner = pairs[0, n]
+    owner = jnp.maximum(pairs[0, n], 0)
     mate = jnp.maximum(pairs[1, n], 0)
     step_x = anchor[0, owner] - anchor[0, mate]
     step_y = anchor[1, owner] - anchor[1, mate]
@@ -244,7 +244,7 @@
     def step(i, carry):
         for d in range(4):
             d += 4 * i
-            pieces = [every[jnp.maximum(partners[ENTRIES * d + n], 0)] for n in range(ENTRIES)]
+            pieces = [every[partners[ENTRIES * d + n]] for n in range(ENTRIES)]
             out[d] = jnp.concatenate(pieces, axis=0).astype(BF16)
         return carry
 
@@ -258,10 +258,11 @@
 
 
 def pair_forward_kernel(start, pairs, anchor, orb_rows, fetched, y_right, x_left, z_table, moved_out, coeffs, ends, message, *refs):
-    buffers, held = refs[:HALF], refs[HALF:]
-    for n in range(HALF):
+    count = moved_out.shape[0]
+    buffers, held = refs[:count], refs[count:]
+    for n in range(count):
         clear_margins(buffers[n])
-    for m in range(0, HALF, 2):
+    for m in range(0, count, 2):
         row = PLANES * (start + m)
         both = [fetched[t, row : row + 2 * PLANES, :].astype(F32) for t in range(TILES)]
         for n in (m, m + 1):
@@ -306,14 +307,15 @@
 def pair_inverse_kernel(start, grid, pairs, anchor, near, *refs):
     sums, refs = refs[: PAIRS - 1], refs[PAIRS - 1 :]
     coeffs, orb_rows, moved, y_right, x_left, z_table, total_in, out_in, total, out, energy, *refs = refs
-    buffers, held = refs[:HALF], refs[HALF:]
+    count = moved.shape[0]
+    buffers, held = refs[:count], refs[count:]
     tables = (y_right, x_left, z_table)
-    for n in range(HALF):
+    for n in range(count):
         clear_margins(buffers[n])
     total[...] = total_in[...]
     if start:
         out[:, : PLANES * start, :] = out_in[:, : PLANES * start, :]
-    for m in range(0, HALF, 2):
+    for m in range(0, count, 2):
         backs = []
         for n in (m, m + 1):
             _, owner, step_x, step_y = pair_scalars(pairs, anchor, start + n)
@@ -324,7 +326,7 @@
         for t in range(TILES):
             piece = jnp.concatenate([tile(back, t) for back in backs], axis=0)
             out[t, row : row + 2 * PLANES, :] = piece.astype(BF16)
-    for n in range(HALF):
+    for n in range(count):
         live, owner, _, _ = pair_scalars(pairs, anchor, start + n)
         total[owner] += jnp.where(live, moved[n].astype(F32) * held[n][...], 0.0)
 
@@ -340,9 +342,7 @@
             for m in range(0, ENTRIES, 2):
                 both = arrived[d, PLANES * m : PLANES * (m + 2), :].astype(F32)
                 for n in (m, m + 1):
-                    which = partners[ENTRIES * d + n]
-                    which = jnp.where(which >= 0, which, spare)
-                    every[n % len(every)][which] += tile(both, n - m)
+                    every[n % len(every)][partners[ENTRIES * d + n]] += tile(both, n - m)
         return carry
 
     lax.fori_loop(0, count // 2, step, 0)
@@ -450,7 +450,7 @@
         [pltpu.VMEM((devices * ORB_DEV, PLANES, LANES), F32)],
         "serve",
         2,
-    )(partners, pieces)
+    )(jnp.maximum(partners, 0), pieces)
     fetched = to_all(served)
     base_sums = from_pairs(base_ends, base_near)
     fetched, base_sums = lax.optimization_barrier((fetched, base_sums))
@@ -464,12 +464,12 @@
     )(grid, base_near, *base_sums, base_coeffs, orb_rows, *tables)
 
     parts = []
-    for start in range(0, ENTRIES, HALF):
+    for start, count in PARTS:
         moved, coeffs, ends, message = call(
             functools.partial(pair_forward_kernel, start),
-            [shape(HALF, ROWS, LANES)] + solve_shapes(HALF),
+            [shape(count, ROWS, LANES)] + solve_shapes(count),
             [SMEM] * 2 + [VMEM] * 5,
-            [SHIFT_BUFFER] * HALF + [HELD] * HALF,
+            [SHIFT_BUFFER] * count + [HELD] * count,
             "pair_forward",
             2,
         )(pair_list, box_anchor, orb_rows, fetched, *tables)
@@ -480,14 +480,15 @@
     parts = [(*part, from_pairs(part[3], part[4])) for part in parts]
     back, energy = served, [base_energy]
     for start, moved, coeffs, ends, near, sums in parts:
+        count = moved.shape[0]
         total, back, value = call(
             functools.partial(pair_inverse_kernel, start),
-            [totals, shape(devices, ENTRIES * PLANES, LANES), shape(HALF, LANES, dtype=F32)],
+            [totals, shape(devices, (start + count) * PLANES, LANES), shape(count, LANES, dtype=F32)],
             [SMEM] * 3 + [VMEM] * (PAIRS + 7) + [VMEM if start else ANY],
-            [SHIFT_BUFFER] * HALF + [HELD] * HALF,
+            [SHIFT_BUFFER] * count + [HELD] * count,
             "pair_inverse",
             3,
-            aliases={PAIRS + 9: 0, PAIRS + 10: 1} if start else {PAIRS + 9: 0},
+            aliases={PAIRS + 9: 0},
         )(grid, pair_list, box_anchor, near, *sums, coeffs, orb_rows, moved, *tables, total, back)
         energy.append(value)
 
@@ -501,7 +502,7 @@
         + [pltpu.VMEM((devices * ORB_DEV + 1, PLANES, LANES), F32)] * 4,
         "gather",
         4,
-    )(partners, pair_list, arrived, energy)
+    )(jnp.where(partners >= 0, partners, devices * ORB_DEV), pair_list, arrived, energy)
     return call(
         finish_kernel,
         [shape(*orbitals.shape), shape(ORB_DEV, dtype=F32)],

time: 123 us -> 123 us (level)
  transfers between devices with their start and end apart: 15 -> 15, of which waited for: 8 -> 8; matrix products, arithmetic and copies ran while one was open for 1% -> 1% of each run, Pallas kernels for 5% -> 6%
where the time goes in v5:
time: 123 us; the launch traced here: 122 us
  starting transfers between devices  47.9 us (39%)
  blocking collectives  32.9 us (27%)
  Pallas kernels  18 us (15%)
  waiting for transfers between devices  17.8 us (14%)
  local copies, waits for them, and re-layouts  3.82 us (3%)
    ppermute x9, starting transfers between devices, from_pairs(): lax.ppermute(sums[e - 1], 'grid', hop)  25.4 us
    all_to_all x3, starting transfers between devices, to_all(): lax.all_to_all(blocks, 'orb', split_axis=0, concat_axis=0, tiled=True)  19.2 us
    all_to_all x1, blocking collectives, to_all(): lax.all_to_all(blocks, 'orb', split_axis=0, concat_axis=0, tiled=True)  19 us
    psum x1, blocking collectives, local(): energy = lax.psum(jnp.sum(jnp.concatenate(energy), axis=1), 'grid')  13.9 us
    all_to_all x3, waiting for transfers between devices, to_all(): lax.all_to_all(blocks, 'orb', split_axis=0, concat_axis=0, tiled=True)  8.43 us
    ppermute x9, waiting for transfers between devices, from_pairs(): lax.ppermute(sums[e - 1], 'grid', hop)  5.45 us
    pallas_call x2, Pallas kernels, local(): call(functools.partial(pair_inverse_kernel, start), [totals, shape(device...  4.72 us
    ppermute x3, waiting for transfers between devices, to_near(): return lax.ppermute(message, 'grid', [(i, i ^ 1) for i in range(GRID)])  3.91 us
  transfers between devices with their start and end apart: 15, of which 8 were waited for; matrix products, arithmetic and copies ran while one was open for 1% of the time, Pallas kernels for 6%

profile of v5, /device:TPU:1, one launch (start us, length us, event | category | flops | bytes accessed | tf_op | source)
XLA Modules:
  0.0 122.4 jit_solution(8055551085801396570)
XLA Ops:
  0.6 1.9 %spread.1 = bf16[32,72,128]{2,1,0:T(8,128)(2,1)} custom-call(s32[2,16]{1,0:T(2,128)} %pairs.11, bf16[8,8,4096]{2,1,0:T(8,128)(2,1)} %orb.2), custom_call_target="tpu_custom_call" | custom-call | bytes 3000000 | tf_op jit(solution)/shard_map/spread/pallas_call | solution.py:435
  2.6 8.7 %all-to-all-start = ((bf16[32,72,128]{2,1,0:T(8,128)(2,1)}), bf16[32,72,128]{2,1,0:T(8,128)(2,1)S(1)}, u32[]{:S(2)}, u32[]{:S(2)}) async-start(bf16[32,72,128]{2,1,0:T(8,128)(2,1)} %spread.1), calls=%async_computation | async-start | bytes 1179648 | tf_op jit(solution)/shard_map/all_to_all | solution.py:424
  11.5 0.1 copy.9
  11.6 0.1 add.681
  12.1 0.1 divide_dynamic-update-slice_fusion.1
  12.2 0.1 divide_dynamic-update-slice_fusion
  12.3 0.1 multiply_dynamic-update-slice_fusion
  12.5 0.1 divide_dynamic-update-slice_fusion.2
  12.7 0.6 copy-done
  13.2 0.1 copy-done.2
  13.4 1.0 base_forward.1
  14.4 1.7 %collective-permute-start = (bf16[512,128]{1,0:T(8,128)(2,1)S(1)}, bf16[512,128]{1,0:T(8,128)(2,1)S(1)}, u32[]{:S(2)}, u32[]{:S(2)}) collective-permute-start(bf16[512,128]{1,0:T(8,128)(2,1)S(1)} %get-tuple-element.42), channel_id=1, source_target_pairs={{0,1},{1,0},{2,3},{3,2},{4,5},{5,4},{6,7},{7,6},{8,9},{9,8},{10,11... | collective-permute-start | bytes 393224 | tf_op jit(solution)/shard_map/ppermute | solution.py:427
  16.1 3.6 %collective-permute-done.near = bf16[512,128]{1,0:T(8,128)(2,1)S(1)} collective-permute-done((bf16[512,128]{1,0:T(8,128)(2,1)S(1)}, bf16[512,128]{1,0:T(8,128)(2,1)S(1)}, u32[]{:S(2)}, u32[]{:S(2)}) %collective-permute-start) | collective-permute-done | bytes 131104 | tf_op jit(solution)/shard_map/ppermute | solution.py:427
  19.7 3.9 %all-to-all-done.held = bf16[32,72,128]{2,1,0:T(8,128)(2,1)S(1)} async-done(((bf16[32,72,128]{2,1,0:T(8,128)(2,1)}), bf16[32,72,128]{2,1,0:T(8,128)(2,1)S(1)}, u32[]{:S(2)}, u32[]{:S(2)}) %all-to-all-start) | async-done | bytes 589856 | tf_op jit(solution)/shard_map/all_to_all | solution.py:424
  23.6 0.1 reshape.545
  23.8 2.2 %serve.1.refs_10_ = bf16[32,128,128]{2,1,0:T(8,128)(2,1)} custom-call(s32[512]{0:T(512)S(1)} %get-tuple-element.84.partners, bf16[32,72,128]{2,1,0:T(8,128)(2,1)S(1)} %all-to-all-done.held), custom_call_target="tpu_custom_call" | custom-call | bytes 6000000 | tf_op jit(solution)/shard_map/serve/pallas_call | solution.py:446
  25.9 4.0 %all-to-all-start.1 = ((bf16[32,128,128]{2,1,0:T(8,128)(2,1)}), bf16[32,128,128]{2,1,0:T(8,128)(2,1)S(1)}, u32[]{:S(2)}, u32[]{:S(2)}) async-start(bf16[32,128,128]{2,1,0:T(8,128)(2,1)} %serve.1.refs_10_), calls=%async_computation.1 | async-start | bytes 2097152 | tf_op jit(solution)/shard_map/all_to_all | solution.py:424
  30.0 0.9 copy-done.5
  31.0 6.8 %collective-permute-start.1 = (bf16[8,32,128]{2,1,0:T(8,128)(2,1)S(1)}, bf16[8,32,128]{2,1,0:T(8,128)(2,1)S(1)}, u32[]{:S(2)}, u32[]{:S(2)}) collective-permute-start(bf16[8,32,128]{2,1,0:T(8,128)(2,1)S(1)} %get-tuple-element.46), channel_id=1, source_target_pairs={{0,4},{1,5},{2,6},{3,7},{4,0},{5,1},{6,2},{7,3},{8,12},{9,13},{10,... | collective-permute-start | bytes 196616 | tf_op jit(solution)/shard_map/ppermute | solution.py:433
  37.8 1.2 collective-permute-start.2
  39.0 2.4 %collective-permute-start.3 = (bf16[8,32,128]{2,1,0:T(8,128)(2,1)S(1)}, bf16[8,32,128]{2,1,0:T(8,128)(2,1)S(1)}, u32[]{:S(2)}, u32[]{:S(2)}) collective-permute-start(bf16[8,32,128]{2,1,0:T(8,128)(2,1)S(1)} %get-tuple-element.48), channel_id=1, source_target_pairs={{0,6},{1,7},{2,0},{3,1},{4,2},{5,3},{6,4},{7,5},{8,14},{9,15},{10,... | collective-permute-start | bytes 196616 | tf_op jit(solution)/shard_map/ppermute | solution.py:433
  41.4 3.3 %collective-permute-done.2.refs_1_ = bf16[8,32,128]{2,1,0:T(8,128)(2,1)S(1)} collective-permute-done((bf16[8,32,128]{2,1,0:T(8,128)(2,1)S(1)}, bf16[8,32,128]{2,1,0:T(8,128)(2,1)S(1)}, u32[]{:S(2)}, u32[]{:S(2)}) %collective-permute-start.2) | collective-permute-done | bytes 65568 | tf_op jit(solution)/shard_map/ppermute | solution.py:433
  44.7 0.6 copy-done.6
  45.3 1.6 %all-to-all-done.1.fetched = bf16[32,128,128]{2,1,0:T(8,128)(2,1)S(1)} async-done(((bf16[32,128,128]{2,1,0:T(8,128)(2,1)}), bf16[32,128,128]{2,1,0:T(8,128)(2,1)S(1)}, u32[]{:S(2)}, u32[]{:S(2)}) %all-to-all-start.1) | async-done | bytes 1048608 | tf_op jit(solution)/shard_map/all_to_all | solution.py:424
  46.9 1.9 %pair_forward.3 = (bf16[8,256,128]{2,1,0:T(8,128)(2,1)S(1)}, f32[8,256,128]{2,1,0:T(8,128)S(1)}, f32[8,64,128]{2,1,0:T(8,128)S(1)}, bf16[512,128]{1,0:T(8,128)(2,1)S(1)}) custom-call(s32[2,16]{1,0:T(2,128)S(1)} %copy-done.8, s32[2,256]{1,0:T(2,128)S(1)} %copy-done.9, bf16[8,256,128]{2,1,0:T(8,128)(2,1)S(1)} %rows.1.orb_rows.refs_4_, ...), custom_call_target="tpu_custom_call" | custom-call | bytes 6000000 | tf_op jit(solution)/shard_map/pair_forward/pallas_call | solution.py:468
  48.8 1.5 %collective-permute-start.8 = (bf16[512,128]{1,0:T(8,128)(2,1)S(1)}, bf16[512,128]{1,0:T(8,128)(2,1)S(1)}, u32[]{:S(2)}, u32[]{:S(2)}) collective-permute-start(bf16[512,128]{1,0:T(8,128)(2,1)S(1)} %get-tuple-element.62), channel_id=1, source_target_pairs={{0,1},{1,0},{2,3},{3,2},{4,5},{5,4},{6,7},{7,6},{8,9},{9,8},{10,11... | collective-permute-start | bytes 393224 | tf_op jit(solution)/shard_map/ppermute | solution.py:427
  50.3 1.9 %pair_forward.2 = (bf16[8,256,128]{2,1,0:T(8,128)(2,1)S(1)}, f32[8,256,128]{2,1,0:T(8,128)S(1)}, f32[8,64,128]{2,1,0:T(8,128)S(1)}, bf16[512,128]{1,0:T(8,128)(2,1)S(1)}) custom-call(s32[2,16]{1,0:T(2,128)S(1)} %copy-done.8, s32[2,256]{1,0:T(2,128)S(1)} %copy-done.9, bf16[8,256,128]{2,1,0:T(8,128)(2,1)S(1)} %rows.1.orb_rows.refs_4_, ...), custom_call_target="tpu_custom_call" | custom-call | bytes 6000000 | tf_op jit(solution)/shard_map/pair_forward/pallas_call | solution.py:468
  52.2 0.1 collective-permute-start.4
  52.4 1.2 base_inverse.1
  53.5 0.3 collective-permute-done.8.near
  53.9 6.8 %collective-permute-start.9 = (bf16[8,32,128]{2,1,0:T(8,128)(2,1)S(1)}, bf16[8,32,128]{2,1,0:T(8,128)(2,1)S(1)}, u32[]{:S(2)}, u32[]{:S(2)}) collective-permute-start(bf16[8,32,128]{2,1,0:T(8,128)(2,1)S(1)} %get-tuple-element.65), channel_id=1, source_target_pairs={{0,4},{1,5},{2,6},{3,7},{4,0},{5,1},{6,2},{7,3},{8,12},{9,13},{10,... | collective-permute-start | bytes 196616 | tf_op jit(solution)/shard_map/ppermute | solution.py:433
  60.7 1.2 collective-permute-start.10
  61.9 2.4 %collective-permute-start.11 = (bf16[8,32,128]{2,1,0:T(8,128)(2,1)S(1)}, bf16[8,32,128]{2,1,0:T(8,128)(2,1)S(1)}, u32[]{:S(2)}, u32[]{:S(2)}) collective-permute-start(bf16[8,32,128]{2,1,0:T(8,128)(2,1)S(1)} %get-tuple-element.67), channel_id=1, source_target_pairs={{0,6},{1,7},{2,0},{3,1},{4,2},{5,3},{6,4},{7,5},{8,14},{9,15},{10,... | collective-permute-start | bytes 196616 | tf_op jit(solution)/shard_map/ppermute | solution.py:433
  64.4 1.0 collective-permute-start.5
  65.4 1.2 collective-permute-start.6
  66.6 2.4 %collective-permute-start.7 = (bf16[8,32,128]{2,1,0:T(8,128)(2,1)S(1)}, bf16[8,32,128]{2,1,0:T(8,128)(2,1)S(1)}, u32[]{:S(2)}, u32[]{:S(2)}) collective-permute-start(bf16[8,32,128]{2,1,0:T(8,128)(2,1)S(1)} %get-tuple-element.54), channel_id=1, source_target_pairs={{0,6},{1,7},{2,0},{3,1},{4,2},{5,3},{6,4},{7,5},{8,14},{9,15},{10,... | collective-permute-start | bytes 196616 | tf_op jit(solution)/shard_map/ppermute | solution.py:433
  69.0 2.3 %pair_inverse.2 = (f32[8,256,128]{2,1,0:T(8,128)S(1)}, bf16[32,64,128]{2,1,0:T(8,128)(2,1)S(1)}, f32[8,128]{1,0:T(8,128)S(1)}) custom-call(s32[1]{0:T(128)} %bitcast.grid, s32[2,16]{1,0:T(2,128)S(1)} %copy-done.8, s32[2,256]{1,0:T(2,128)S(1)} %copy-done.9, bf16[512,128]{1,0:T(8,128)(2,1)S(1)} %collective-permute-done.8.near, ...), custom_call_target="tpu_custom_call", output_to_operand_aliasing={{0}: (13, {})} | custom-call | bytes 9000000 | tf_op jit(solution)/shard_map/pair_inverse/pallas_call | solution.py:484
  71.3 1.0 collective-permute-done.5.refs_0_
  72.4 1.1 collective-permute-done.7.refs_2_
  73.5 2.4 %pair_inverse.3 = (f32[8,256,128]{2,1,0:T(8,128)S(1)}, bf16[32,128,128]{2,1,0:T(8,128)(2,1)S(1)}, f32[8,128]{1,0:T(8,128)S(1)}) custom-call(s32[1]{0:T(128)} %bitcast.grid, s32[2,16]{1,0:T(2,128)S(1)} %copy-done.8, s32[2,256]{1,0:T(2,128)S(1)} %copy-done.9, bf16[512,128]{1,0:T(8,128)(2,1)S(1)} %collective-permute-done.4.near, ...), custom_call_target="tpu_custom_call", output_to_operand_aliasing={{0}: (13, {})} | custom-call | bytes 9000000 | tf_op jit(solution)/shard_map/pair_inverse/pallas_call | solution.py:484
  75.9 1.0 copy-done.3
  76.9 6.5 %all-to-all-start.2 = ((bf16[32,128,128]{2,1,0:T(8,128)(2,1)}), bf16[32,128,128]{2,1,0:T(8,128)(2,1)S(1)}, u32[]{:S(2)}, u32[]{:S(2)}) async-start(bf16[32,128,128]{2,1,0:T(8,128)(2,1)} %copy-done.3), calls=%async_computation.2 | async-start | bytes 2097152 | tf_op jit(solution)/shard_map/all_to_all | solution.py:424
  83.3 0.1 maximum_reduce_fusion
  83.4 13.9 %psum.7.energy = f32[24]{0:T(128)S(1)} all-reduce(f32[24]{0:T(128)S(1)} %maximum_reduce_fusion), channel_id=1, replica_groups=mesh['orb'=32,'grid'=8] {'grid'}, use_global_device_ids=true, to_apply=%region_1.2 | all-reduce | flops 24 | bytes 192 | tf_op jit(solution)/shard_map/psum | solution.py:496
  97.3 3.0 %all-to-all-done.2.arrived = bf16[32,128,128]{2,1,0:T(8,128)(2,1)S(1)} async-done(((bf16[32,128,128]{2,1,0:T(8,128)(2,1)}), bf16[32,128,128]{2,1,0:T(8,128)(2,1)S(1)}, u32[]{:S(2)}, u32[]{:S(2)}) %all-to-all-start.2) | async-done | bytes 1048608 | tf_op jit(solution)/shard_map/all_to_all | solution.py:424
  100.3 1.9 %gather.1 = (bf16[32,72,128]{2,1,0:T(8,128)(2,1)S(1)}, f32[8,128]{1,0:T(8,128)S(1)}) custom-call(s32[512]{0:T(512)S(1)} %get-tuple-element.85.partners, s32[2,16]{1,0:T(2,128)S(1)} %copy-done.8, bf16[32,128,128]{2,1,0:T(8,128)(2,1)S(1)} %all-to-all-done.2.arrived, f32[24]{0:T(128)S(1)} %psum.7.energy), custom_call_target="tpu_custom_call" | custom-call | bytes 12000000 | tf_op jit(solution)/shard_map/gather/pallas_call | solution.py:497
  102.2 19.0 %all_to_all.20.arrived = bf16[32,72,128]{2,1,0:T(8,128)(2,1)S(1)} all-to-all(bf16[32,72,128]{2,1,0:T(8,128)(2,1)S(1)} %get-tuple-element.77), channel_id=1, replica_groups=mesh['orb'=32,'grid'=8] {'orb'}, dimensions={0} | all-to-all | bytes 1179648 | tf_op jit(solution)/shard_map/all_to_all | solution.py:424
  121.2 1.0 finish.1
  (41 shorter events, 0.9 us)
Async XLA Ops:
  2.6 9.4 %copy-start.1 = (bf16[8,8,4096]{2,1,0:T(8,128)(2,1)S(1)}, bf16[8,8,4096]{2,1,0:T(8,128)(2,1)}, u32[]{:S(2)}) copy-start(bf16[8,8,4096]{2,1,0:T(8,128)(2,1)} %orb.2) | copy-start | bytes 1572868
  2.6 21.0 %all-to-all-start = ((bf16[32,72,128]{2,1,0:T(8,128)(2,1)}), bf16[32,72,128]{2,1,0:T(8,128)(2,1)S(1)}, u32[]{:S(2)}, u32[]{:S(2)}) async-start(bf16[32,72,128]{2,1,0:T(8,128)(2,1)} %spread.1), calls=%async_computation | async-start | bytes 1179648 | tf_op jit(solution)/shard_map/all_to_all | solution.py:424
  12.3 0.9 copy-start
  12.6 0.8 copy-start.2
  14.4 11.6 %copy-start.4 = (f32[8,64,128]{2,1,0:T(8,128)}, f32[8,64,128]{2,1,0:T(8,128)S(1)}, u32[]{:S(2)}) copy-start(f32[8,64,128]{2,1,0:T(8,128)S(1)} %get-tuple-element.44.ends) | copy-start | bytes 786436
  14.4 5.3 %collective-permute-start = (bf16[512,128]{1,0:T(8,128)(2,1)S(1)}, bf16[512,128]{1,0:T(8,128)(2,1)S(1)}, u32[]{:S(2)}, u32[]{:S(2)}) collective-permute-start(bf16[512,128]{1,0:T(8,128)(2,1)S(1)} %get-tuple-element.42), channel_id=1, source_target_pairs={{0,1},{1,0},{2,3},{3,2},{4,5},{5,4},{6,7},{7,6},{8,9},{9,8},{10,11... | collective-permute-start | bytes 393224 | tf_op jit(solution)/shard_map/ppermute | solution.py:427
  25.9 20.9 %all-to-all-start.1 = ((bf16[32,128,128]{2,1,0:T(8,128)(2,1)}), bf16[32,128,128]{2,1,0:T(8,128)(2,1)S(1)}, u32[]{:S(2)}, u32[]{:S(2)}) async-start(bf16[32,128,128]{2,1,0:T(8,128)(2,1)} %serve.1.refs_10_), calls=%async_computation.1 | async-start | bytes 2097152 | tf_op jit(solution)/shard_map/all_to_all | solution.py:424
  30.0 1.0 copy-start.5
  31.0 15.9 %copy-start.9 = (s32[2,256]{1,0:T(2,128)S(1)}, s32[2,256]{1,0:T(2,128)}, u32[]{:S(2)}) copy-start(s32[2,256]{1,0:T(2,128)} %anchor.7) | copy-start | bytes 6148
  31.0 10.4 %collective-permute-start.1 = (bf16[8,32,128]{2,1,0:T(8,128)(2,1)S(1)}, bf16[8,32,128]{2,1,0:T(8,128)(2,1)S(1)}, u32[]{:S(2)}, u32[]{:S(2)}) collective-permute-start(bf16[8,32,128]{2,1,0:T(8,128)(2,1)S(1)} %get-tuple-element.46), channel_id=1, source_target_pairs={{0,4},{1,5},{2,6},{3,7},{4,0},{5,1},{6,2},{7,3},{8,12},{9,13},{10,... | collective-permute-start | bytes 196616 | tf_op jit(solution)/shard_map/ppermute | solution.py:433
  37.8 9.1 %copy-start.8 = (s32[2,16]{1,0:T(2,128)S(1)}, s32[2,16]{1,0:T(2,128)}, u32[]{:S(2)}) copy-start(s32[2,16]{1,0:T(2,128)} %pairs.11) | copy-start | bytes 388
  37.8 6.8 %collective-permute-start.2 = (bf16[8,32,128]{2,1,0:T(8,128)(2,1)S(1)}, bf16[8,32,128]{2,1,0:T(8,128)(2,1)S(1)}, u32[]{:S(2)}, u32[]{:S(2)}) collective-permute-start(bf16[8,32,128]{2,1,0:T(8,128)(2,1)S(1)} %get-tuple-element.47), channel_id=1, source_target_pairs={{0,2},{1,3},{2,4},{3,5},{4,6},{5,7},{6,0},{7,1},{8,10},{9,11},{10,... | collective-permute-start | bytes 196616 | tf_op jit(solution)/shard_map/ppermute | solution.py:433
  39.0 5.7 %collective-permute-start.3 = (bf16[8,32,128]{2,1,0:T(8,128)(2,1)S(1)}, bf16[8,32,128]{2,1,0:T(8,128)(2,1)S(1)}, u32[]{:S(2)}, u32[]{:S(2)}) collective-permute-start(bf16[8,32,128]{2,1,0:T(8,128)(2,1)S(1)} %get-tuple-element.48), channel_id=1, source_target_pairs={{0,6},{1,7},{2,0},{3,1},{4,2},{5,3},{6,4},{7,5},{8,14},{9,15},{10,... | collective-permute-start | bytes 196616 | tf_op jit(solution)/shard_map/ppermute | solution.py:433
  44.7 0.6 copy-start.6
  48.8 3.6 %copy-start.7 = (bf16[8,32,128]{2,1,0:T(8,128)(2,1)S(1)}, bf16[8,32,128]{2,1,0:T(8,128)(2,1)}, u32[]{:S(2)}) copy-start(bf16[8,32,128]{2,1,0:T(8,128)(2,1)} %copy-done.6) | copy-start | bytes 196612
  48.8 5.1 %collective-permute-start.8 = (bf16[512,128]{1,0:T(8,128)(2,1)S(1)}, bf16[512,128]{1,0:T(8,128)(2,1)S(1)}, u32[]{:S(2)}, u32[]{:S(2)}) collective-permute-start(bf16[512,128]{1,0:T(8,128)(2,1)S(1)} %get-tuple-element.62), channel_id=1, source_target_pairs={{0,1},{1,0},{2,3},{3,2},{4,5},{5,4},{6,7},{7,6},{8,9},{9,8},{10,11... | collective-permute-start | bytes 393224 | tf_op jit(solution)/shard_map/ppermute | solution.py:427
  52.2 12.1 %collective-permute-start.4 = (bf16[512,128]{1,0:T(8,128)(2,1)S(1)}, bf16[512,128]{1,0:T(8,128)(2,1)S(1)}, u32[]{:S(2)}, u32[]{:S(2)}) collective-permute-start(bf16[512,128]{1,0:T(8,128)(2,1)S(1)} %get-tuple-element.50), channel_id=1, source_target_pairs={{0,1},{1,0},{2,3},{3,2},{4,5},{5,4},{6,7},{7,6},{8,9},{9,8},{10,11... | collective-permute-start | bytes 393224 | tf_op jit(solution)/shard_map/ppermute | solution.py:427
  53.9 12.7 %collective-permute-start.9 = (bf16[8,32,128]{2,1,0:T(8,128)(2,1)S(1)}, bf16[8,32,128]{2,1,0:T(8,128)(2,1)S(1)}, u32[]{:S(2)}, u32[]{:S(2)}) collective-permute-start(bf16[8,32,128]{2,1,0:T(8,128)(2,1)S(1)} %get-tuple-element.65), channel_id=1, source_target_pairs={{0,4},{1,5},{2,6},{3,7},{4,0},{5,1},{6,2},{7,3},{8,12},{9,13},{10,... | collective-permute-start | bytes 196616 | tf_op jit(solution)/shard_map/ppermute | solution.py:433
  60.7 8.2 %collective-permute-start.10 = (bf16[8,32,128]{2,1,0:T(8,128)(2,1)S(1)}, bf16[8,32,128]{2,1,0:T(8,128)(2,1)S(1)}, u32[]{:S(2)}, u32[]{:S(2)}) collective-permute-start(bf16[8,32,128]{2,1,0:T(8,128)(2,1)S(1)} %get-tuple-element.66), channel_id=1, source_target_pairs={{0,2},{1,3},{2,4},{3,5},{4,6},{5,7},{6,0},{7,1},{8,10},{9,11},{10,... | collective-permute-start | bytes 196616 | tf_op jit(solution)/shard_map/ppermute | solution.py:433
  61.9 7.1 %collective-permute-start.11 = (bf16[8,32,128]{2,1,0:T(8,128)(2,1)S(1)}, bf16[8,32,128]{2,1,0:T(8,128)(2,1)S(1)}, u32[]{:S(2)}, u32[]{:S(2)}) collective-permute-start(bf16[8,32,128]{2,1,0:T(8,128)(2,1)S(1)} %get-tuple-element.67), channel_id=1, source_target_pairs={{0,6},{1,7},{2,0},{3,1},{4,2},{5,3},{6,4},{7,5},{8,14},{9,15},{10,... | collective-permute-start | bytes 196616 | tf_op jit(solution)/shard_map/ppermute | solution.py:433
  64.4 8.0 %collective-permute-start.5 = (bf16[8,32,128]{2,1,0:T(8,128)(2,1)S(1)}, bf16[8,32,128]{2,1,0:T(8,128)(2,1)S(1)}, u32[]{:S(2)}, u32[]{:S(2)}) collective-permute-start(bf16[8,32,128]{2,1,0:T(8,128)(2,1)S(1)} %get-tuple-element.52), channel_id=1, source_target_pairs={{0,4},{1,5},{2,6},{3,7},{4,0},{5,1},{6,2},{7,3},{8,12},{9,13},{10,... | collective-permute-start | bytes 196616 | tf_op jit(solution)/shard_map/ppermute | solution.py:433
  65.4 7.0 %collective-permute-start.6 = (bf16[8,32,128]{2,1,0:T(8,128)(2,1)S(1)}, bf16[8,32,128]{2,1,0:T(8,128)(2,1)S(1)}, u32[]{:S(2)}, u32[]{:S(2)}) collective-permute-start(bf16[8,32,128]{2,1,0:T(8,128)(2,1)S(1)} %get-tuple-element.53), channel_id=1, source_target_pairs={{0,2},{1,3},{2,4},{3,5},{4,6},{5,7},{6,0},{7,1},{8,10},{9,11},{10,... | collective-permute-start | bytes 196616 | tf_op jit(solution)/shard_map/ppermute | solution.py:433
  66.6 6.9 %collective-permute-start.7 = (bf16[8,32,128]{2,1,0:T(8,128)(2,1)S(1)}, bf16[8,32,128]{2,1,0:T(8,128)(2,1)S(1)}, u32[]{:S(2)}, u32[]{:S(2)}) collective-permute-start(bf16[8,32,128]{2,1,0:T(8,128)(2,1)S(1)} %get-tuple-element.54), channel_id=1, source_target_pairs={{0,6},{1,7},{2,0},{3,1},{4,2},{5,3},{6,4},{7,5},{8,14},{9,15},{10,... | collective-permute-start | bytes 196616 | tf_op jit(solution)/shard_map/ppermute | solution.py:433
  75.9 1.0 copy-start.3
  76.9 23.5 %all-to-all-start.2 = ((bf16[32,128,128]{2,1,0:T(8,128)(2,1)}), bf16[32,128,128]{2,1,0:T(8,128)(2,1)S(1)}, u32[]{:S(2)}, u32[]{:S(2)}) async-start(bf16[32,128,128]{2,1,0:T(8,128)(2,1)} %copy-done.3), calls=%async_computation.2 | async-start | bytes 2097152 | tf_op jit(solution)/shard_map/all_to_all | solution.py:424

commit v6 on v5

--- a/solution.py
+++ b/solution.py
@@ -241,14 +241,9 @@
         for n in range(ORB_DEV):
             every[ORB_DEV * d + n] = tile(pieces, n)
 
-    def step(i, carry):
-        for d in range(4):
-            d += 4 * i
-            pieces = [every[partners[ENTRIES * d + n]] for n in range(ENTRIES)]
-            out[d] = jnp.concatenate(pieces, axis=0).astype(BF16)
-        return carry
-
-    lax.fori_loop(0, count // 4, step, 0)
+    for d in range(count):
+        pieces = [every[partners[ENTRIES * d + n]] for n in range(ENTRIES)]
+        out[d] = jnp.concatenate(pieces, axis=0).astype(BF16)
 
 
 def base_forward_kernel(orb_rows, y_right, x_left, z_table, coeffs, ends, message, *held):
@@ -338,14 +333,14 @@
         part[...] = jnp.zeros_like(part)
 
     def step(i, carry):
-        for d in (2 * i, 2 * i + 1):
+        for d in [8 * i + j for j in range(8)]:
             for m in range(0, ENTRIES, 2):
                 both = arrived[d, PLANES * m : PLANES * (m + 2), :].astype(F32)
                 for n in (m, m + 1):
                     every[n % len(every)][partners[ENTRIES * d + n]] += tile(both, n - m)
         return carry
 
-    lax.fori_loop(0, count // 2, step, 0)
+    lax.fori_loop(0, count // 8, step, 0)
     every_energy[...] = jnp.zeros_like(every_energy)
     first = lane_iota(1) == 0
     for n in range(ORB_DEV):

time: 123 us -> 123 us (level)
  no operation moved by 1% of the time
where the time goes in v6:
time: 123 us; the launch traced here: 122 us
  starting transfers between devices  47.9 us (39%)
  blocking collectives  33 us (27%)
  Pallas kernels  17.8 us (14%)
  waiting for transfers between devices  17.8 us (14%)
  local copies, waits for them, and re-layouts  3.82 us (3%)
    ppermute x9, starting transfers between devices, from_pairs(): lax.ppermute(sums[e - 1], 'grid', hop)  25.4 us
    all_to_all x3, starting transfers between devices, to_all(): lax.all_to_all(blocks, 'orb', split_axis=0, concat_axis=0, tiled=True)  19.2 us
    all_to_all x1, blocking collectives, to_all(): lax.all_to_all(blocks, 'orb', split_axis=0, concat_axis=0, tiled=True)  19.1 us
    psum x1, blocking collectives, local(): energy = lax.psum(jnp.sum(jnp.concatenate(energy), axis=1), 'grid')  13.9 us
    all_to_all x3, waiting for transfers between devices, to_all(): lax.all_to_all(blocks, 'orb', split_axis=0, concat_axis=0, tiled=True)  8.4 us
    ppermute x9, waiting for transfers between devices, from_pairs(): lax.ppermute(sums[e - 1], 'grid', hop)  5.47 us
    pallas_call x2, Pallas kernels, local(): call(functools.partial(pair_inverse_kernel, start), [totals, shape(device...  4.72 us
    ppermute x3, waiting for transfers between devices, to_near(): return lax.ppermute(message, 'grid', [(i, i ^ 1) for i in range(GRID)])  3.92 us
  transfers between devices with their start and end apart: 15, of which 8 were waited for; matrix products, arithmetic and copies ran while one was open for 1% of the time, Pallas kernels for 6%

profile of v6, /device:TPU:1, one launch (start us, length us, event | category | flops | bytes accessed | tf_op | source)
XLA Modules:
  0.0 122.2 jit_solution(1621236214026798403)
XLA Ops:
  0.6 1.9 %spread.1 = bf16[32,72,128]{2,1,0:T(8,128)(2,1)} custom-call(s32[2,16]{1,0:T(2,128)} %pairs.11, bf16[8,8,4096]{2,1,0:T(8,128)(2,1)} %orb.2), custom_call_target="tpu_custom_call" | custom-call | bytes 3000000 | tf_op jit(solution)/shard_map/spread/pallas_call | solution.py:430
  2.6 8.7 %all-to-all-start = ((bf16[32,72,128]{2,1,0:T(8,128)(2,1)}), bf16[32,72,128]{2,1,0:T(8,128)(2,1)S(1)}, u32[]{:S(2)}, u32[]{:S(2)}) async-start(bf16[32,72,128]{2,1,0:T(8,128)(2,1)} %spread.1), calls=%async_computation | async-start | bytes 1179648 | tf_op jit(solution)/shard_map/all_to_all | solution.py:419
  11.5 0.1 copy.9
  11.6 0.1 add.681
  12.1 0.1 divide_dynamic-update-slice_fusion.1
  12.2 0.1 divide_dynamic-update-slice_fusion
  12.3 0.1 multiply_dynamic-update-slice_fusion
  12.5 0.1 divide_dynamic-update-slice_fusion.2
  12.7 0.6 copy-done
  13.2 0.1 copy-done.2
  13.4 1.0 base_forward.1
  14.4 1.7 %collective-permute-start = (bf16[512,128]{1,0:T(8,128)(2,1)S(1)}, bf16[512,128]{1,0:T(8,128)(2,1)S(1)}, u32[]{:S(2)}, u32[]{:S(2)}) collective-permute-start(bf16[512,128]{1,0:T(8,128)(2,1)S(1)} %get-tuple-element.42), channel_id=1, source_target_pairs={{0,1},{1,0},{2,3},{3,2},{4,5},{5,4},{6,7},{7,6},{8,9},{9,8},{10,11... | collective-permute-start | bytes 393224 | tf_op jit(solution)/shard_map/ppermute | solution.py:422
  16.1 3.6 %collective-permute-done.near = bf16[512,128]{1,0:T(8,128)(2,1)S(1)} collective-permute-done((bf16[512,128]{1,0:T(8,128)(2,1)S(1)}, bf16[512,128]{1,0:T(8,128)(2,1)S(1)}, u32[]{:S(2)}, u32[]{:S(2)}) %collective-permute-start) | collective-permute-done | bytes 131104 | tf_op jit(solution)/shard_map/ppermute | solution.py:422
  19.7 3.9 %all-to-all-done.held = bf16[32,72,128]{2,1,0:T(8,128)(2,1)S(1)} async-done(((bf16[32,72,128]{2,1,0:T(8,128)(2,1)}), bf16[32,72,128]{2,1,0:T(8,128)(2,1)S(1)}, u32[]{:S(2)}, u32[]{:S(2)}) %all-to-all-start) | async-done | bytes 589856 | tf_op jit(solution)/shard_map/all_to_all | solution.py:419
  23.6 0.1 reshape.545
  23.8 2.0 %serve.1.refs_10_ = bf16[32,128,128]{2,1,0:T(8,128)(2,1)} custom-call(s32[512]{0:T(512)S(1)} %get-tuple-element.84.partners, bf16[32,72,128]{2,1,0:T(8,128)(2,1)S(1)} %all-to-all-done.held), custom_call_target="tpu_custom_call" | custom-call | bytes 6000000 | tf_op jit(solution)/shard_map/serve/pallas_call | solution.py:441
  25.8 4.0 %all-to-all-start.1 = ((bf16[32,128,128]{2,1,0:T(8,128)(2,1)}), bf16[32,128,128]{2,1,0:T(8,128)(2,1)S(1)}, u32[]{:S(2)}, u32[]{:S(2)}) async-start(bf16[32,128,128]{2,1,0:T(8,128)(2,1)} %serve.1.refs_10_), calls=%async_computation.1 | async-start | bytes 2097152 | tf_op jit(solution)/shard_map/all_to_all | solution.py:419
  29.8 0.9 copy-done.5
  30.8 6.8 %collective-permute-start.1 = (bf16[8,32,128]{2,1,0:T(8,128)(2,1)S(1)}, bf16[8,32,128]{2,1,0:T(8,128)(2,1)S(1)}, u32[]{:S(2)}, u32[]{:S(2)}) collective-permute-start(bf16[8,32,128]{2,1,0:T(8,128)(2,1)S(1)} %get-tuple-element.46), channel_id=1, source_target_pairs={{0,4},{1,5},{2,6},{3,7},{4,0},{5,1},{6,2},{7,3},{8,12},{9,13},{10,... | collective-permute-start | bytes 196616 | tf_op jit(solution)/shard_map/ppermute | solution.py:428
  37.6 1.2 collective-permute-start.2
  38.8 2.4 %collective-permute-start.3 = (bf16[8,32,128]{2,1,0:T(8,128)(2,1)S(1)}, bf16[8,32,128]{2,1,0:T(8,128)(2,1)S(1)}, u32[]{:S(2)}, u32[]{:S(2)}) collective-permute-start(bf16[8,32,128]{2,1,0:T(8,128)(2,1)S(1)} %get-tuple-element.48), channel_id=1, source_target_pairs={{0,6},{1,7},{2,0},{3,1},{4,2},{5,3},{6,4},{7,5},{8,14},{9,15},{10,... | collective-permute-start | bytes 196616 | tf_op jit(solution)/shard_map/ppermute | solution.py:428
  41.2 3.3 %collective-permute-done.2.refs_1_ = bf16[8,32,128]{2,1,0:T(8,128)(2,1)S(1)} collective-permute-done((bf16[8,32,128]{2,1,0:T(8,128)(2,1)S(1)}, bf16[8,32,128]{2,1,0:T(8,128)(2,1)S(1)}, u32[]{:S(2)}, u32[]{:S(2)}) %collective-permute-start.2) | collective-permute-done | bytes 65568 | tf_op jit(solution)/shard_map/ppermute | solution.py:428
  44.5 0.6 copy-done.6
  45.1 1.6 %all-to-all-done.1.fetched = bf16[32,128,128]{2,1,0:T(8,128)(2,1)S(1)} async-done(((bf16[32,128,128]{2,1,0:T(8,128)(2,1)}), bf16[32,128,128]{2,1,0:T(8,128)(2,1)S(1)}, u32[]{:S(2)}, u32[]{:S(2)}) %all-to-all-start.1) | async-done | bytes 1048608 | tf_op jit(solution)/shard_map/all_to_all | solution.py:419
  46.7 1.9 %pair_forward.3 = (bf16[8,256,128]{2,1,0:T(8,128)(2,1)S(1)}, f32[8,256,128]{2,1,0:T(8,128)S(1)}, f32[8,64,128]{2,1,0:T(8,128)S(1)}, bf16[512,128]{1,0:T(8,128)(2,1)S(1)}) custom-call(s32[2,16]{1,0:T(2,128)S(1)} %copy-done.8, s32[2,256]{1,0:T(2,128)S(1)} %copy-done.9, bf16[8,256,128]{2,1,0:T(8,128)(2,1)S(1)} %rows.1.orb_rows.refs_4_, ...), custom_call_target="tpu_custom_call" | custom-call | bytes 6000000 | tf_op jit(solution)/shard_map/pair_forward/pallas_call | solution.py:463
  48.6 1.5 %collective-permute-start.8 = (bf16[512,128]{1,0:T(8,128)(2,1)S(1)}, bf16[512,128]{1,0:T(8,128)(2,1)S(1)}, u32[]{:S(2)}, u32[]{:S(2)}) collective-permute-start(bf16[512,128]{1,0:T(8,128)(2,1)S(1)} %get-tuple-element.62), channel_id=1, source_target_pairs={{0,1},{1,0},{2,3},{3,2},{4,5},{5,4},{6,7},{7,6},{8,9},{9,8},{10,11... | collective-permute-start | bytes 393224 | tf_op jit(solution)/shard_map/ppermute | solution.py:422
  50.2 1.9 %pair_forward.2 = (bf16[8,256,128]{2,1,0:T(8,128)(2,1)S(1)}, f32[8,256,128]{2,1,0:T(8,128)S(1)}, f32[8,64,128]{2,1,0:T(8,128)S(1)}, bf16[512,128]{1,0:T(8,128)(2,1)S(1)}) custom-call(s32[2,16]{1,0:T(2,128)S(1)} %copy-done.8, s32[2,256]{1,0:T(2,128)S(1)} %copy-done.9, bf16[8,256,128]{2,1,0:T(8,128)(2,1)S(1)} %rows.1.orb_rows.refs_4_, ...), custom_call_target="tpu_custom_call" | custom-call | bytes 6000000 | tf_op jit(solution)/shard_map/pair_forward/pallas_call | solution.py:463
  52.0 0.1 collective-permute-start.4
  52.2 1.2 base_inverse.1
  53.4 0.3 collective-permute-done.8.near
  53.7 6.8 %collective-permute-start.9 = (bf16[8,32,128]{2,1,0:T(8,128)(2,1)S(1)}, bf16[8,32,128]{2,1,0:T(8,128)(2,1)S(1)}, u32[]{:S(2)}, u32[]{:S(2)}) collective-permute-start(bf16[8,32,128]{2,1,0:T(8,128)(2,1)S(1)} %get-tuple-element.65), channel_id=1, source_target_pairs={{0,4},{1,5},{2,6},{3,7},{4,0},{5,1},{6,2},{7,3},{8,12},{9,13},{10,... | collective-permute-start | bytes 196616 | tf_op jit(solution)/shard_map/ppermute | solution.py:428
  60.6 1.2 collective-permute-start.10
  61.7 2.4 %collective-permute-start.11 = (bf16[8,32,128]{2,1,0:T(8,128)(2,1)S(1)}, bf16[8,32,128]{2,1,0:T(8,128)(2,1)S(1)}, u32[]{:S(2)}, u32[]{:S(2)}) collective-permute-start(bf16[8,32,128]{2,1,0:T(8,128)(2,1)S(1)} %get-tuple-element.67), channel_id=1, source_target_pairs={{0,6},{1,7},{2,0},{3,1},{4,2},{5,3},{6,4},{7,5},{8,14},{9,15},{10,... | collective-permute-start | bytes 196616 | tf_op jit(solution)/shard_map/ppermute | solution.py:428
  64.2 1.0 collective-permute-start.5
  65.2 1.2 collective-permute-start.6
  66.4 2.4 %collective-permute-start.7 = (bf16[8,32,128]{2,1,0:T(8,128)(2,1)S(1)}, bf16[8,32,128]{2,1,0:T(8,128)(2,1)S(1)}, u32[]{:S(2)}, u32[]{:S(2)}) collective-permute-start(bf16[8,32,128]{2,1,0:T(8,128)(2,1)S(1)} %get-tuple-element.54), channel_id=1, source_target_pairs={{0,6},{1,7},{2,0},{3,1},{4,2},{5,3},{6,4},{7,5},{8,14},{9,15},{10,... | collective-permute-start | bytes 196616 | tf_op jit(solution)/shard_map/ppermute | solution.py:428
  68.8 2.3 %pair_inverse.2 = (f32[8,256,128]{2,1,0:T(8,128)S(1)}, bf16[32,64,128]{2,1,0:T(8,128)(2,1)S(1)}, f32[8,128]{1,0:T(8,128)S(1)}) custom-call(s32[1]{0:T(128)} %bitcast.grid, s32[2,16]{1,0:T(2,128)S(1)} %copy-done.8, s32[2,256]{1,0:T(2,128)S(1)} %copy-done.9, bf16[512,128]{1,0:T(8,128)(2,1)S(1)} %collective-permute-done.8.near, ...), custom_call_target="tpu_custom_call", output_to_operand_aliasing={{0}: (13, {})} | custom-call | bytes 9000000 | tf_op jit(solution)/shard_map/pair_inverse/pallas_call | solution.py:479
  71.2 1.1 collective-permute-done.5.refs_0_
  72.2 1.1 collective-permute-done.7.refs_2_
  73.3 2.4 %pair_inverse.3 = (f32[8,256,128]{2,1,0:T(8,128)S(1)}, bf16[32,128,128]{2,1,0:T(8,128)(2,1)S(1)}, f32[8,128]{1,0:T(8,128)S(1)}) custom-call(s32[1]{0:T(128)} %bitcast.grid, s32[2,16]{1,0:T(2,128)S(1)} %copy-done.8, s32[2,256]{1,0:T(2,128)S(1)} %copy-done.9, bf16[512,128]{1,0:T(8,128)(2,1)S(1)} %collective-permute-done.4.near, ...), custom_call_target="tpu_custom_call", output_to_operand_aliasing={{0}: (13, {})} | custom-call | bytes 9000000 | tf_op jit(solution)/shard_map/pair_inverse/pallas_call | solution.py:479
  75.7 1.0 copy-done.3
  76.7 6.4 %all-to-all-start.2 = ((bf16[32,128,128]{2,1,0:T(8,128)(2,1)}), bf16[32,128,128]{2,1,0:T(8,128)(2,1)S(1)}, u32[]{:S(2)}, u32[]{:S(2)}) async-start(bf16[32,128,128]{2,1,0:T(8,128)(2,1)} %copy-done.3), calls=%async_computation.2 | async-start | bytes 2097152 | tf_op jit(solution)/shard_map/all_to_all | solution.py:419
  83.1 0.1 maximum_reduce_fusion
  83.3 13.9 %psum.7.energy = f32[24]{0:T(128)S(1)} all-reduce(f32[24]{0:T(128)S(1)} %maximum_reduce_fusion), channel_id=1, replica_groups=mesh['orb'=32,'grid'=8] {'grid'}, use_global_device_ids=true, to_apply=%region_1.2 | all-reduce | flops 24 | bytes 192 | tf_op jit(solution)/shard_map/psum | solution.py:491
  97.2 3.0 %all-to-all-done.2.arrived = bf16[32,128,128]{2,1,0:T(8,128)(2,1)S(1)} async-done(((bf16[32,128,128]{2,1,0:T(8,128)(2,1)}), bf16[32,128,128]{2,1,0:T(8,128)(2,1)S(1)}, u32[]{:S(2)}, u32[]{:S(2)}) %all-to-all-start.2) | async-done | bytes 1048608 | tf_op jit(solution)/shard_map/all_to_all | solution.py:419
  100.1 1.8 %gather.1 = (bf16[32,72,128]{2,1,0:T(8,128)(2,1)S(1)}, f32[8,128]{1,0:T(8,128)S(1)}) custom-call(s32[512]{0:T(512)S(1)} %get-tuple-element.85.partners, s32[2,16]{1,0:T(2,128)S(1)} %copy-done.8, bf16[32,128,128]{2,1,0:T(8,128)(2,1)S(1)} %all-to-all-done.2.arrived, f32[24]{0:T(128)S(1)} %psum.7.energy), custom_call_target="tpu_custom_call" | custom-call | bytes 12000000 | tf_op jit(solution)/shard_map/gather/pallas_call | solution.py:492
  102.0 19.1 %all_to_all.20.arrived = bf16[32,72,128]{2,1,0:T(8,128)(2,1)S(1)} all-to-all(bf16[32,72,128]{2,1,0:T(8,128)(2,1)S(1)} %get-tuple-element.77), channel_id=1, replica_groups=mesh['orb'=32,'grid'=8] {'orb'}, dimensions={0} | all-to-all | bytes 1179648 | tf_op jit(solution)/shard_map/all_to_all | solution.py:419
  121.0 1.0 finish.1
  (41 shorter events, 0.9 us)
Async XLA Ops:
  2.6 9.4 %copy-start.1 = (bf16[8,8,4096]{2,1,0:T(8,128)(2,1)S(1)}, bf16[8,8,4096]{2,1,0:T(8,128)(2,1)}, u32[]{:S(2)}) copy-start(bf16[8,8,4096]{2,1,0:T(8,128)(2,1)} %orb.2) | copy-start | bytes 1572868
  2.6 21.0 %all-to-all-start = ((bf16[32,72,128]{2,1,0:T(8,128)(2,1)}), bf16[32,72,128]{2,1,0:T(8,128)(2,1)S(1)}, u32[]{:S(2)}, u32[]{:S(2)}) async-start(bf16[32,72,128]{2,1,0:T(8,128)(2,1)} %spread.1), calls=%async_computation | async-start | bytes 1179648 | tf_op jit(solution)/shard_map/all_to_all | solution.py:419
  12.3 0.9 copy-start
  12.6 0.8 copy-start.2
  14.4 11.4 %copy-start.4 = (f32[8,64,128]{2,1,0:T(8,128)}, f32[8,64,128]{2,1,0:T(8,128)S(1)}, u32[]{:S(2)}) copy-start(f32[8,64,128]{2,1,0:T(8,128)S(1)} %get-tuple-element.44.ends) | copy-start | bytes 786436
  14.4 5.3 %collective-permute-start = (bf16[512,128]{1,0:T(8,128)(2,1)S(1)}, bf16[512,128]{1,0:T(8,128)(2,1)S(1)}, u32[]{:S(2)}, u32[]{:S(2)}) collective-permute-start(bf16[512,128]{1,0:T(8,128)(2,1)S(1)} %get-tuple-element.42), channel_id=1, source_target_pairs={{0,1},{1,0},{2,3},{3,2},{4,5},{5,4},{6,7},{7,6},{8,9},{9,8},{10,11... | collective-permute-start | bytes 393224 | tf_op jit(solution)/shard_map/ppermute | solution.py:422
  25.8 20.9 %all-to-all-start.1 = ((bf16[32,128,128]{2,1,0:T(8,128)(2,1)}), bf16[32,128,128]{2,1,0:T(8,128)(2,1)S(1)}, u32[]{:S(2)}, u32[]{:S(2)}) async-start(bf16[32,128,128]{2,1,0:T(8,128)(2,1)} %serve.1.refs_10_), calls=%async_computation.1 | async-start | bytes 2097152 | tf_op jit(solution)/shard_map/all_to_all | solution.py:419
  29.8 1.0 copy-start.5
  30.8 15.9 %copy-start.9 = (s32[2,256]{1,0:T(2,128)S(1)}, s32[2,256]{1,0:T(2,128)}, u32[]{:S(2)}) copy-start(s32[2,256]{1,0:T(2,128)} %anchor.7) | copy-start | bytes 6148
  30.8 10.4 %collective-permute-start.1 = (bf16[8,32,128]{2,1,0:T(8,128)(2,1)S(1)}, bf16[8,32,128]{2,1,0:T(8,128)(2,1)S(1)}, u32[]{:S(2)}, u32[]{:S(2)}) collective-permute-start(bf16[8,32,128]{2,1,0:T(8,128)(2,1)S(1)} %get-tuple-element.46), channel_id=1, source_target_pairs={{0,4},{1,5},{2,6},{3,7},{4,0},{5,1},{6,2},{7,3},{8,12},{9,13},{10,... | collective-permute-start | bytes 196616 | tf_op jit(solution)/shard_map/ppermute | solution.py:428
  37.6 9.1 %copy-start.8 = (s32[2,16]{1,0:T(2,128)S(1)}, s32[2,16]{1,0:T(2,128)}, u32[]{:S(2)}) copy-start(s32[2,16]{1,0:T(2,128)} %pairs.11) | copy-start | bytes 388
  37.6 6.8 %collective-permute-start.2 = (bf16[8,32,128]{2,1,0:T(8,128)(2,1)S(1)}, bf16[8,32,128]{2,1,0:T(8,128)(2,1)S(1)}, u32[]{:S(2)}, u32[]{:S(2)}) collective-permute-start(bf16[8,32,128]{2,1,0:T(8,128)(2,1)S(1)} %get-tuple-element.47), channel_id=1, source_target_pairs={{0,2},{1,3},{2,4},{3,5},{4,6},{5,7},{6,0},{7,1},{8,10},{9,11},{10,... | collective-permute-start | bytes 196616 | tf_op jit(solution)/shard_map/ppermute | solution.py:428
  38.8 5.7 %collective-permute-start.3 = (bf16[8,32,128]{2,1,0:T(8,128)(2,1)S(1)}, bf16[8,32,128]{2,1,0:T(8,128)(2,1)S(1)}, u32[]{:S(2)}, u32[]{:S(2)}) collective-permute-start(bf16[8,32,128]{2,1,0:T(8,128)(2,1)S(1)} %get-tuple-element.48), channel_id=1, source_target_pairs={{0,6},{1,7},{2,0},{3,1},{4,2},{5,3},{6,4},{7,5},{8,14},{9,15},{10,... | collective-permute-start | bytes 196616 | tf_op jit(solution)/shard_map/ppermute | solution.py:428
  44.5 0.6 copy-start.6
  48.6 3.6 %copy-start.7 = (bf16[8,32,128]{2,1,0:T(8,128)(2,1)S(1)}, bf16[8,32,128]{2,1,0:T(8,128)(2,1)}, u32[]{:S(2)}) copy-start(bf16[8,32,128]{2,1,0:T(8,128)(2,1)} %copy-done.6) | copy-start | bytes 196612
  48.6 5.1 %collective-permute-start.8 = (bf16[512,128]{1,0:T(8,128)(2,1)S(1)}, bf16[512,128]{1,0:T(8,128)(2,1)S(1)}, u32[]{:S(2)}, u32[]{:S(2)}) collective-permute-start(bf16[512,128]{1,0:T(8,128)(2,1)S(1)} %get-tuple-element.62), channel_id=1, source_target_pairs={{0,1},{1,0},{2,3},{3,2},{4,5},{5,4},{6,7},{7,6},{8,9},{9,8},{10,11... | collective-permute-start | bytes 393224 | tf_op jit(solution)/shard_map/ppermute | solution.py:422
  52.0 12.1 %collective-permute-start.4 = (bf16[512,128]{1,0:T(8,128)(2,1)S(1)}, bf16[512,128]{1,0:T(8,128)(2,1)S(1)}, u32[]{:S(2)}, u32[]{:S(2)}) collective-permute-start(bf16[512,128]{1,0:T(8,128)(2,1)S(1)} %get-tuple-element.50), channel_id=1, source_target_pairs={{0,1},{1,0},{2,3},{3,2},{4,5},{5,4},{6,7},{7,6},{8,9},{9,8},{10,11... | collective-permute-start | bytes 393224 | tf_op jit(solution)/shard_map/ppermute | solution.py:422
  53.7 12.6 %collective-permute-start.9 = (bf16[8,32,128]{2,1,0:T(8,128)(2,1)S(1)}, bf16[8,32,128]{2,1,0:T(8,128)(2,1)S(1)}, u32[]{:S(2)}, u32[]{:S(2)}) collective-permute-start(bf16[8,32,128]{2,1,0:T(8,128)(2,1)S(1)} %get-tuple-element.65), channel_id=1, source_target_pairs={{0,4},{1,5},{2,6},{3,7},{4,0},{5,1},{6,2},{7,3},{8,12},{9,13},{10,... | collective-permute-start | bytes 196616 | tf_op jit(solution)/shard_map/ppermute | solution.py:428
  60.6 8.2 %collective-permute-start.10 = (bf16[8,32,128]{2,1,0:T(8,128)(2,1)S(1)}, bf16[8,32,128]{2,1,0:T(8,128)(2,1)S(1)}, u32[]{:S(2)}, u32[]{:S(2)}) collective-permute-start(bf16[8,32,128]{2,1,0:T(8,128)(2,1)S(1)} %get-tuple-element.66), channel_id=1, source_target_pairs={{0,2},{1,3},{2,4},{3,5},{4,6},{5,7},{6,0},{7,1},{8,10},{9,11},{10,... | collective-permute-start | bytes 196616 | tf_op jit(solution)/shard_map/ppermute | solution.py:428
  61.7 7.1 %collective-permute-start.11 = (bf16[8,32,128]{2,1,0:T(8,128)(2,1)S(1)}, bf16[8,32,128]{2,1,0:T(8,128)(2,1)S(1)}, u32[]{:S(2)}, u32[]{:S(2)}) collective-permute-start(bf16[8,32,128]{2,1,0:T(8,128)(2,1)S(1)} %get-tuple-element.67), channel_id=1, source_target_pairs={{0,6},{1,7},{2,0},{3,1},{4,2},{5,3},{6,4},{7,5},{8,14},{9,15},{10,... | collective-permute-start | bytes 196616 | tf_op jit(solution)/shard_map/ppermute | solution.py:428
  64.2 8.0 %collective-permute-start.5 = (bf16[8,32,128]{2,1,0:T(8,128)(2,1)S(1)}, bf16[8,32,128]{2,1,0:T(8,128)(2,1)S(1)}, u32[]{:S(2)}, u32[]{:S(2)}) collective-permute-start(bf16[8,32,128]{2,1,0:T(8,128)(2,1)S(1)} %get-tuple-element.52), channel_id=1, source_target_pairs={{0,4},{1,5},{2,6},{3,7},{4,0},{5,1},{6,2},{7,3},{8,12},{9,13},{10,... | collective-permute-start | bytes 196616 | tf_op jit(solution)/shard_map/ppermute | solution.py:428
  65.2 7.0 %collective-permute-start.6 = (bf16[8,32,128]{2,1,0:T(8,128)(2,1)S(1)}, bf16[8,32,128]{2,1,0:T(8,128)(2,1)S(1)}, u32[]{:S(2)}, u32[]{:S(2)}) collective-permute-start(bf16[8,32,128]{2,1,0:T(8,128)(2,1)S(1)} %get-tuple-element.53), channel_id=1, source_target_pairs={{0,2},{1,3},{2,4},{3,5},{4,6},{5,7},{6,0},{7,1},{8,10},{9,11},{10,... | collective-permute-start | bytes 196616 | tf_op jit(solution)/shard_map/ppermute | solution.py:428
  66.4 7.0 %collective-permute-start.7 = (bf16[8,32,128]{2,1,0:T(8,128)(2,1)S(1)}, bf16[8,32,128]{2,1,0:T(8,128)(2,1)S(1)}, u32[]{:S(2)}, u32[]{:S(2)}) collective-permute-start(bf16[8,32,128]{2,1,0:T(8,128)(2,1)S(1)} %get-tuple-element.54), channel_id=1, source_target_pairs={{0,6},{1,7},{2,0},{3,1},{4,2},{5,3},{6,4},{7,5},{8,14},{9,15},{10,... | collective-permute-start | bytes 196616 | tf_op jit(solution)/shard_map/ppermute | solution.py:428
  75.7 1.0 copy-start.3
  76.7 23.4 %all-to-all-start.2 = ((bf16[32,128,128]{2,1,0:T(8,128)(2,1)}), bf16[32,128,128]{2,1,0:T(8,128)(2,1)S(1)}, u32[]{:S(2)}, u32[]{:S(2)}) async-start(bf16[32,128,128]{2,1,0:T(8,128)(2,1)} %copy-done.3), calls=%async_computation.2 | async-start | bytes 2097152 | tf_op jit(solution)/shard_map/all_to_all | solution.py:419

commit v7 on v5

--- a/solution.py
+++ b/solution.py
@@ -426,9 +426,15 @@
     def to_near(message):
         return lax.ppermute(message, "grid", [(i, i ^ 1) for i in range(GRID)])
 
-    def from_pairs(ends, near):
+    def from_pairs(ends, near, back=False):
         outs = [shape(ends.shape[0], TILES, LANES)] * (PAIRS - 1)
         sums = call(pair_up_kernel, outs, [SMEM] + [VMEM] * 3, [], "pair_up", 1)(grid, ends, near, z_table)
+        if back:
+            hop = [(i, (i + 6) % GRID) for i in range(GRID)]
+            got = lax.ppermute(jnp.concatenate([sums[2], sums[1]]), "grid", hop)
+            count = ends.shape[0]
+            ahead = lax.ppermute(sums[0], "grid", [(i, (i + 2) % GRID) for i in range(GRID)])
+            return [lax.ppermute(got[count:], "grid", hop), ahead, got[:count]]
         hops = [[(i, (i + 2 * e) % GRID) for i in range(GRID)] for e in ORDER]
         return [lax.ppermute(sums[e - 1], "grid", hop) for e, hop in zip(ORDER, hops)]
 
@@ -477,7 +483,7 @@
     start, moved, coeffs, ends, near = parts[0]
     total, near = lax.optimization_barrier((total, near))
     parts[0] = (start, moved, coeffs, ends, near)
-    parts = [(*part, from_pairs(part[3], part[4])) for part in parts]
+    parts = [(*part, from_pairs(part[3], part[4], part[0] > 0)) for part in parts]
     back, energy = served, [base_energy]
     for start, moved, coeffs, ends, near, sums in parts:
         count = moved.shape[0]

time: 123 us -> 125 us (1.016)
  starting transfers between devices: 47.9 us -> 51.7 us
    ppermute x0 -> x3, starting transfers between devices: none -> 11.1 us  [the longest x1 5.92 us: from_pairs(): got = lax.ppermute(jnp.concatenate([sums[2], sums[1]]), 'grid', hop)]
    ppermute x9 -> x6, starting transfers between devices: 25.4 us -> 16.1 us  [from_pairs(): lax.ppermute(sums[e - 1], 'grid', hop)]
    ppermute x9 -> x6, waiting for transfers between devices: 5.45 us -> 3.27 us  [from_pairs(): lax.ppermute(sums[e - 1], 'grid', hop)]
    all_to_all x3, starting transfers between devices: 19.2 us -> 21.1 us  [to_all(): lax.all_to_all(blocks, 'orb', split_axis=0, concat_axis=0, tiled=True)]
  transfers between devices with their start and end apart: 15 -> 15, of which waited for: 8 -> 6; matrix products, arithmetic and copies ran while one was open for 1% -> 1% of each run, Pallas kernels for 6% -> 5%
where the time goes in v7:
time: 125 us
  starting transfers between devices  51.7 us (41%)
  blocking collectives  32.4 us (26%)
  Pallas kernels  18 us (14%)
  waiting for transfers between devices  17.1 us (14%)
  local copies, waits for them, and re-layouts  3.82 us (3%)
    all_to_all x3, starting transfers between devices, to_all(): lax.all_to_all(blocks, 'orb', split_axis=0, concat_axis=0, tiled=True)  21.1 us
    all_to_all x1, blocking collectives, to_all(): lax.all_to_all(blocks, 'orb', split_axis=0, concat_axis=0, tiled=True)  18.8 us
    ppermute x6, starting transfers between devices, from_pairs(): lax.ppermute(sums[e - 1], 'grid', hop)  16.1 us
    psum x1, blocking collectives, local(): energy = lax.psum(jnp.sum(jnp.concatenate(energy), axis=1), 'grid')  13.6 us
    all_to_all x3, waiting for transfers between devices, to_all(): lax.all_to_all(blocks, 'orb', split_axis=0, concat_axis=0, tiled=True)  8.67 us
    ppermute x1, starting transfers between devices, from_pairs(): got = lax.ppermute(jnp.concatenate([sums[2], sums[1]]), 'grid', hop)  5.92 us
    ppermute x1, starting transfers between devices, from_pairs(): return [lax.ppermute(got[count:], 'grid', hop), ahead, got[:count]]  5.16 us
    ppermute x3, waiting for transfers between devices, to_near(): return lax.ppermute(message, 'grid', [(i, i ^ 1) for i in range(GRID)])  5.11 us
  transfers between devices with their start and end apart: 15, of which 6 were waited for; matrix products, arithmetic and copies ran while one was open for 1% of the time, Pallas kernels for 5%

profile of v7, /device:TPU:1, one launch (start us, length us, event | category | flops | bytes accessed | tf_op | source)
XLA Modules:
  0.0 124.9 jit_solution(7390421810272198198)
XLA Ops:
  0.6 1.9 %spread.1 = bf16[32,72,128]{2,1,0:T(8,128)(2,1)} custom-call(s32[2,16]{1,0:T(2,128)} %pairs.11, bf16[8,8,4096]{2,1,0:T(8,128)(2,1)} %orb.2), custom_call_target="tpu_custom_call" | custom-call | bytes 3000000 | tf_op jit(solution)/shard_map/spread/pallas_call | solution.py:441
  2.6 8.7 %all-to-all-start = ((bf16[32,72,128]{2,1,0:T(8,128)(2,1)}), bf16[32,72,128]{2,1,0:T(8,128)(2,1)S(1)}, u32[]{:S(2)}, u32[]{:S(2)}) async-start(bf16[32,72,128]{2,1,0:T(8,128)(2,1)} %spread.1), calls=%async_computation | async-start | bytes 1179648 | tf_op jit(solution)/shard_map/all_to_all | solution.py:424
  11.5 0.1 copy.9
  11.5 0.1 add.662
  11.6 0.1 add.681
  11.7 0.1 add.663
  11.8 0.1 add.667
  12.1 0.1 divide_dynamic-update-slice_fusion.1
  12.2 0.1 divide_dynamic-update-slice_fusion
  12.3 0.1 multiply_dynamic-update-slice_fusion
  12.5 0.1 divide_dynamic-update-slice_fusion.2
  12.7 0.6 copy-done
  13.2 0.1 copy-done.2
  13.3 1.0 base_forward.1
  14.4 1.7 %collective-permute-start = (bf16[512,128]{1,0:T(8,128)(2,1)S(1)}, bf16[512,128]{1,0:T(8,128)(2,1)S(1)}, u32[]{:S(2)}, u32[]{:S(2)}) collective-permute-start(bf16[512,128]{1,0:T(8,128)(2,1)S(1)} %get-tuple-element.42), channel_id=1, source_target_pairs={{0,1},{1,0},{2,3},{3,2},{4,5},{5,4},{6,7},{7,6},{8,9},{9,8},{10,11... | collective-permute-start | bytes 393224 | tf_op jit(solution)/shard_map/ppermute | solution.py:427
  16.1 3.6 %collective-permute-done.near = bf16[512,128]{1,0:T(8,128)(2,1)S(1)} collective-permute-done((bf16[512,128]{1,0:T(8,128)(2,1)S(1)}, bf16[512,128]{1,0:T(8,128)(2,1)S(1)}, u32[]{:S(2)}, u32[]{:S(2)}) %collective-permute-start) | collective-permute-done | bytes 131104 | tf_op jit(solution)/shard_map/ppermute | solution.py:427
  19.7 3.9 %all-to-all-done.held = bf16[32,72,128]{2,1,0:T(8,128)(2,1)S(1)} async-done(((bf16[32,72,128]{2,1,0:T(8,128)(2,1)}), bf16[32,72,128]{2,1,0:T(8,128)(2,1)S(1)}, u32[]{:S(2)}, u32[]{:S(2)}) %all-to-all-start) | async-done | bytes 589856 | tf_op jit(solution)/shard_map/all_to_all | solution.py:424
  23.6 0.1 reshape.545
  23.7 2.2 %serve.1.refs_10_ = bf16[32,128,128]{2,1,0:T(8,128)(2,1)} custom-call(s32[512]{0:T(512)S(1)} %get-tuple-element.86.partners, bf16[32,72,128]{2,1,0:T(8,128)(2,1)S(1)} %all-to-all-done.held), custom_call_target="tpu_custom_call" | custom-call | bytes 6000000 | tf_op jit(solution)/shard_map/serve/pallas_call | solution.py:452
  25.9 4.0 %all-to-all-start.1 = ((bf16[32,128,128]{2,1,0:T(8,128)(2,1)}), bf16[32,128,128]{2,1,0:T(8,128)(2,1)S(1)}, u32[]{:S(2)}, u32[]{:S(2)}) async-start(bf16[32,128,128]{2,1,0:T(8,128)(2,1)} %serve.1.refs_10_), calls=%async_computation.1 | async-start | bytes 2097152 | tf_op jit(solution)/shard_map/all_to_all | solution.py:424
  30.0 0.9 copy-done.5
  31.0 6.8 %collective-permute-start.1 = (bf16[8,32,128]{2,1,0:T(8,128)(2,1)S(1)}, bf16[8,32,128]{2,1,0:T(8,128)(2,1)S(1)}, u32[]{:S(2)}, u32[]{:S(2)}) collective-permute-start(bf16[8,32,128]{2,1,0:T(8,128)(2,1)S(1)} %get-tuple-element.46), channel_id=1, source_target_pairs={{0,4},{1,5},{2,6},{3,7},{4,0},{5,1},{6,2},{7,3},{8,12},{9,13},{10,... | collective-permute-start | bytes 196616 | tf_op jit(solution)/shard_map/ppermute | solution.py:439
  37.8 1.2 collective-permute-start.2
  39.0 2.4 %collective-permute-start.3 = (bf16[8,32,128]{2,1,0:T(8,128)(2,1)S(1)}, bf16[8,32,128]{2,1,0:T(8,128)(2,1)S(1)}, u32[]{:S(2)}, u32[]{:S(2)}) collective-permute-start(bf16[8,32,128]{2,1,0:T(8,128)(2,1)S(1)} %get-tuple-element.48), channel_id=1, source_target_pairs={{0,6},{1,7},{2,0},{3,1},{4,2},{5,3},{6,4},{7,5},{8,14},{9,15},{10,... | collective-permute-start | bytes 196616 | tf_op jit(solution)/shard_map/ppermute | solution.py:439
  41.4 3.3 %collective-permute-done.2.refs_1_ = bf16[8,32,128]{2,1,0:T(8,128)(2,1)S(1)} collective-permute-done((bf16[8,32,128]{2,1,0:T(8,128)(2,1)S(1)}, bf16[8,32,128]{2,1,0:T(8,128)(2,1)S(1)}, u32[]{:S(2)}, u32[]{:S(2)}) %collective-permute-start.2) | collective-permute-done | bytes 65568 | tf_op jit(solution)/shard_map/ppermute | solution.py:439
  44.7 0.6 copy-done.6
  45.3 1.6 %all-to-all-done.1.fetched = bf16[32,128,128]{2,1,0:T(8,128)(2,1)S(1)} async-done(((bf16[32,128,128]{2,1,0:T(8,128)(2,1)}), bf16[32,128,128]{2,1,0:T(8,128)(2,1)S(1)}, u32[]{:S(2)}, u32[]{:S(2)}) %all-to-all-start.1) | async-done | bytes 1048608 | tf_op jit(solution)/shard_map/all_to_all | solution.py:424
  46.9 1.9 %pair_forward.2 = (bf16[8,256,128]{2,1,0:T(8,128)(2,1)S(1)}, f32[8,256,128]{2,1,0:T(8,128)S(1)}, f32[8,64,128]{2,1,0:T(8,128)S(1)}, bf16[512,128]{1,0:T(8,128)(2,1)S(1)}) custom-call(s32[2,16]{1,0:T(2,128)S(1)} %copy-done.8, s32[2,256]{1,0:T(2,128)S(1)} %copy-done.9, bf16[8,256,128]{2,1,0:T(8,128)(2,1)S(1)} %rows.1.orb_rows.refs_4_, ...), custom_call_target="tpu_custom_call" | custom-call | bytes 6000000 | tf_op jit(solution)/shard_map/pair_forward/pallas_call | solution.py:474
  48.8 1.5 %collective-permute-start.4 = (bf16[512,128]{1,0:T(8,128)(2,1)S(1)}, bf16[512,128]{1,0:T(8,128)(2,1)S(1)}, u32[]{:S(2)}, u32[]{:S(2)}) collective-permute-start(bf16[512,128]{1,0:T(8,128)(2,1)S(1)} %get-tuple-element.50), channel_id=1, source_target_pairs={{0,1},{1,0},{2,3},{3,2},{4,5},{5,4},{6,7},{7,6},{8,9},{9,8},{10,11... | collective-permute-start | bytes 393224 | tf_op jit(solution)/shard_map/ppermute | solution.py:427
  50.3 1.9 %pair_forward.3 = (bf16[8,256,128]{2,1,0:T(8,128)(2,1)S(1)}, f32[8,256,128]{2,1,0:T(8,128)S(1)}, f32[8,64,128]{2,1,0:T(8,128)S(1)}, bf16[512,128]{1,0:T(8,128)(2,1)S(1)}) custom-call(s32[2,16]{1,0:T(2,128)S(1)} %copy-done.8, s32[2,256]{1,0:T(2,128)S(1)} %copy-done.9, bf16[8,256,128]{2,1,0:T(8,128)(2,1)S(1)} %rows.1.orb_rows.refs_4_, ...), custom_call_target="tpu_custom_call" | custom-call | bytes 6000000 | tf_op jit(solution)/shard_map/pair_forward/pallas_call | solution.py:474
  52.2 0.1 collective-permute-start.8
  52.3 1.5 %collective-permute-done.4.near = bf16[512,128]{1,0:T(8,128)(2,1)S(1)} collective-permute-done((bf16[512,128]{1,0:T(8,128)(2,1)S(1)}, bf16[512,128]{1,0:T(8,128)(2,1)S(1)}, u32[]{:S(2)}, u32[]{:S(2)}) %collective-permute-start.4) | collective-permute-done | bytes 131104 | tf_op jit(solution)/shard_map/ppermute | solution.py:427
  53.9 5.9 %collective-permute-start.5 = (bf16[16,32,128]{2,1,0:T(8,128)(2,1)S(1)}, bf16[16,32,128]{2,1,0:T(8,128)(2,1)S(1)}, u32[]{:S(2)}, u32[]{:S(2)}) collective-permute-start(bf16[16,32,128]{2,1,0:T(8,128)(2,1)S(1)} %pad_maximum_fusion), channel_id=1, source_target_pairs={{0,6},{1,7},{2,0},{3,1},{4,2},{5,3},{6,4},{7,5},{8,14},{9,15},{10,... | collective-permute-start | bytes 393224 | tf_op jit(solution)/shard_map/ppermute | solution.py:434
  59.8 1.2 base_inverse.1
  61.1 2.2 %collective-permute-start.9 = (bf16[8,32,128]{2,1,0:T(8,128)(2,1)S(1)}, bf16[8,32,128]{2,1,0:T(8,128)(2,1)S(1)}, u32[]{:S(2)}, u32[]{:S(2)}) collective-permute-start(bf16[8,32,128]{2,1,0:T(8,128)(2,1)S(1)} %get-tuple-element.65), channel_id=1, source_target_pairs={{0,4},{1,5},{2,6},{3,7},{4,0},{5,1},{6,2},{7,3},{8,12},{9,13},{10,... | collective-permute-start | bytes 196616 | tf_op jit(solution)/shard_map/ppermute | solution.py:439
  63.3 1.2 collective-permute-start.10
  64.5 2.4 %collective-permute-start.11 = (bf16[8,32,128]{2,1,0:T(8,128)(2,1)S(1)}, bf16[8,32,128]{2,1,0:T(8,128)(2,1)S(1)}, u32[]{:S(2)}, u32[]{:S(2)}) collective-permute-start(bf16[8,32,128]{2,1,0:T(8,128)(2,1)S(1)} %get-tuple-element.67), channel_id=1, source_target_pairs={{0,6},{1,7},{2,0},{3,1},{4,2},{5,3},{6,4},{7,5},{8,14},{9,15},{10,... | collective-permute-start | bytes 196616 | tf_op jit(solution)/shard_map/ppermute | solution.py:439
  66.9 5.2 %collective-permute-start.6 = (bf16[8,32,128]{2,1,0:T(8,128)(2,1)S(1)}, bf16[8,32,128]{2,1,0:T(8,128)(2,1)S(1)}, u32[]{:S(2)}, u32[]{:S(2)}) collective-permute-start(bf16[8,32,128]{2,1,0:T(8,128)(2,1)S(1)} %get-tuple-element.81), channel_id=1, source_target_pairs={{0,6},{1,7},{2,0},{3,1},{4,2},{5,3},{6,4},{7,5},{8,14},{9,15},{10,... | collective-permute-start | bytes 196616 | tf_op jit(solution)/shard_map/ppermute | solution.py:437
  72.1 2.4 %pair_inverse.2 = (f32[8,256,128]{2,1,0:T(8,128)S(1)}, bf16[32,64,128]{2,1,0:T(8,128)(2,1)S(1)}, f32[8,128]{1,0:T(8,128)S(1)}) custom-call(s32[1]{0:T(128)} %bitcast.grid, s32[2,16]{1,0:T(2,128)S(1)} %copy-done.8, s32[2,256]{1,0:T(2,128)S(1)} %copy-done.9, bf16[512,128]{1,0:T(8,128)(2,1)S(1)} %collective-permute-done.8.near, ...), custom_call_target="tpu_custom_call", output_to_operand_aliasing={{0}: (13, {})} | custom-call | bytes 9000000 | tf_op jit(solution)/shard_map/pair_inverse/pallas_call | solution.py:490
  74.5 2.4 %pair_inverse.3 = (f32[8,256,128]{2,1,0:T(8,128)S(1)}, bf16[32,128,128]{2,1,0:T(8,128)(2,1)S(1)}, f32[8,128]{1,0:T(8,128)S(1)}) custom-call(s32[1]{0:T(128)} %bitcast.grid, s32[2,16]{1,0:T(2,128)S(1)} %copy-done.8, s32[2,256]{1,0:T(2,128)S(1)} %copy-done.9, bf16[512,128]{1,0:T(8,128)(2,1)S(1)} %collective-permute-done.4.near, ...), custom_call_target="tpu_custom_call", output_to_operand_aliasing={{0}: (13, {})} | custom-call | bytes 9000000 | tf_op jit(solution)/shard_map/pair_inverse/pallas_call | solution.py:490
  76.9 1.0 copy-done.3
  77.8 8.3 %all-to-all-start.2 = ((bf16[32,128,128]{2,1,0:T(8,128)(2,1)}), bf16[32,128,128]{2,1,0:T(8,128)(2,1)S(1)}, u32[]{:S(2)}, u32[]{:S(2)}) async-start(bf16[32,128,128]{2,1,0:T(8,128)(2,1)} %copy-done.3), calls=%async_computation.2 | async-start | bytes 2097152 | tf_op jit(solution)/shard_map/all_to_all | solution.py:424
  86.2 0.1 maximum_reduce_fusion
  86.3 13.6 %psum.7.energy = f32[24]{0:T(128)S(1)} all-reduce(f32[24]{0:T(128)S(1)} %maximum_reduce_fusion), channel_id=1, replica_groups=mesh['orb'=32,'grid'=8] {'grid'}, use_global_device_ids=true, to_apply=%region_1.2 | all-reduce | flops 24 | bytes 192 | tf_op jit(solution)/shard_map/psum | solution.py:502
  99.8 3.2 %all-to-all-done.2.arrived = bf16[32,128,128]{2,1,0:T(8,128)(2,1)S(1)} async-done(((bf16[32,128,128]{2,1,0:T(8,128)(2,1)}), bf16[32,128,128]{2,1,0:T(8,128)(2,1)S(1)}, u32[]{:S(2)}, u32[]{:S(2)}) %all-to-all-start.2) | async-done | bytes 1048608 | tf_op jit(solution)/shard_map/all_to_all | solution.py:424
  103.1 1.9 %gather.1 = (bf16[32,72,128]{2,1,0:T(8,128)(2,1)S(1)}, f32[8,128]{1,0:T(8,128)S(1)}) custom-call(s32[512]{0:T(512)S(1)} %get-tuple-element.87.partners, s32[2,16]{1,0:T(2,128)S(1)} %copy-done.8, bf16[32,128,128]{2,1,0:T(8,128)(2,1)S(1)} %all-to-all-done.2.arrived, f32[24]{0:T(128)S(1)} %psum.7.energy), custom_call_target="tpu_custom_call" | custom-call | bytes 12000000 | tf_op jit(solution)/shard_map/gather/pallas_call | solution.py:503
  105.0 18.8 %all_to_all.20.arrived = bf16[32,72,128]{2,1,0:T(8,128)(2,1)S(1)} all-to-all(bf16[32,72,128]{2,1,0:T(8,128)(2,1)S(1)} %get-tuple-element.77), channel_id=1, replica_groups=mesh['orb'=32,'grid'=8] {'orb'}, dimensions={0} | all-to-all | bytes 1179648 | tf_op jit(solution)/shard_map/all_to_all | solution.py:424
  123.8 1.0 finish.1
  (43 shorter events, 0.7 us)
Async XLA Ops:
  2.6 9.4 %copy-start.1 = (bf16[8,8,4096]{2,1,0:T(8,128)(2,1)S(1)}, bf16[8,8,4096]{2,1,0:T(8,128)(2,1)}, u32[]{:S(2)}) copy-start(bf16[8,8,4096]{2,1,0:T(8,128)(2,1)} %orb.2) | copy-start | bytes 1572868
  2.6 21.0 %all-to-all-start = ((bf16[32,72,128]{2,1,0:T(8,128)(2,1)}), bf16[32,72,128]{2,1,0:T(8,128)(2,1)S(1)}, u32[]{:S(2)}, u32[]{:S(2)}) async-start(bf16[32,72,128]{2,1,0:T(8,128)(2,1)} %spread.1), calls=%async_computation | async-start | bytes 1179648 | tf_op jit(solution)/shard_map/all_to_all | solution.py:424
  12.3 0.9 copy-start
  12.6 0.8 copy-start.2
  14.4 11.6 %copy-start.4 = (f32[8,64,128]{2,1,0:T(8,128)}, f32[8,64,128]{2,1,0:T(8,128)S(1)}, u32[]{:S(2)}) copy-start(f32[8,64,128]{2,1,0:T(8,128)S(1)} %get-tuple-element.44.ends) | copy-start | bytes 786436
  14.4 5.3 %collective-permute-start = (bf16[512,128]{1,0:T(8,128)(2,1)S(1)}, bf16[512,128]{1,0:T(8,128)(2,1)S(1)}, u32[]{:S(2)}, u32[]{:S(2)}) collective-permute-start(bf16[512,128]{1,0:T(8,128)(2,1)S(1)} %get-tuple-element.42), channel_id=1, source_target_pairs={{0,1},{1,0},{2,3},{3,2},{4,5},{5,4},{6,7},{7,6},{8,9},{9,8},{10,11... | collective-permute-start | bytes 393224 | tf_op jit(solution)/shard_map/ppermute | solution.py:427
  25.9 20.9 %all-to-all-start.1 = ((bf16[32,128,128]{2,1,0:T(8,128)(2,1)}), bf16[32,128,128]{2,1,0:T(8,128)(2,1)S(1)}, u32[]{:S(2)}, u32[]{:S(2)}) async-start(bf16[32,128,128]{2,1,0:T(8,128)(2,1)} %serve.1.refs_10_), calls=%async_computation.1 | async-start | bytes 2097152 | tf_op jit(solution)/shard_map/all_to_all | solution.py:424
  30.0 1.0 copy-start.5
  31.0 15.9 %copy-start.9 = (s32[2,256]{1,0:T(2,128)S(1)}, s32[2,256]{1,0:T(2,128)}, u32[]{:S(2)}) copy-start(s32[2,256]{1,0:T(2,128)} %anchor.7) | copy-start | bytes 6148
  31.0 10.4 %collective-permute-start.1 = (bf16[8,32,128]{2,1,0:T(8,128)(2,1)S(1)}, bf16[8,32,128]{2,1,0:T(8,128)(2,1)S(1)}, u32[]{:S(2)}, u32[]{:S(2)}) collective-permute-start(bf16[8,32,128]{2,1,0:T(8,128)(2,1)S(1)} %get-tuple-element.46), channel_id=1, source_target_pairs={{0,4},{1,5},{2,6},{3,7},{4,0},{5,1},{6,2},{7,3},{8,12},{9,13},{10,... | collective-permute-start | bytes 196616 | tf_op jit(solution)/shard_map/ppermute | solution.py:439
  37.8 9.1 %copy-start.8 = (s32[2,16]{1,0:T(2,128)S(1)}, s32[2,16]{1,0:T(2,128)}, u32[]{:S(2)}) copy-start(s32[2,16]{1,0:T(2,128)} %pairs.11) | copy-start | bytes 388
  37.8 6.8 %collective-permute-start.2 = (bf16[8,32,128]{2,1,0:T(8,128)(2,1)S(1)}, bf16[8,32,128]{2,1,0:T(8,128)(2,1)S(1)}, u32[]{:S(2)}, u32[]{:S(2)}) collective-permute-start(bf16[8,32,128]{2,1,0:T(8,128)(2,1)S(1)} %get-tuple-element.47), channel_id=1, source_target_pairs={{0,2},{1,3},{2,4},{3,5},{4,6},{5,7},{6,0},{7,1},{8,10},{9,11},{10,... | collective-permute-start | bytes 196616 | tf_op jit(solution)/shard_map/ppermute | solution.py:439
  39.0 5.6 %collective-permute-start.3 = (bf16[8,32,128]{2,1,0:T(8,128)(2,1)S(1)}, bf16[8,32,128]{2,1,0:T(8,128)(2,1)S(1)}, u32[]{:S(2)}, u32[]{:S(2)}) collective-permute-start(bf16[8,32,128]{2,1,0:T(8,128)(2,1)S(1)} %get-tuple-element.48), channel_id=1, source_target_pairs={{0,6},{1,7},{2,0},{3,1},{4,2},{5,3},{6,4},{7,5},{8,14},{9,15},{10,... | collective-permute-start | bytes 196616 | tf_op jit(solution)/shard_map/ppermute | solution.py:439
  44.7 0.6 copy-start.6
  48.8 5.0 %collective-permute-start.4 = (bf16[512,128]{1,0:T(8,128)(2,1)S(1)}, bf16[512,128]{1,0:T(8,128)(2,1)S(1)}, u32[]{:S(2)}, u32[]{:S(2)}) collective-permute-start(bf16[512,128]{1,0:T(8,128)(2,1)S(1)} %get-tuple-element.50), channel_id=1, source_target_pairs={{0,1},{1,0},{2,3},{3,2},{4,5},{5,4},{6,7},{7,6},{8,9},{9,8},{10,11... | collective-permute-start | bytes 393224 | tf_op jit(solution)/shard_map/ppermute | solution.py:427
  52.2 8.8 %collective-permute-start.8 = (bf16[512,128]{1,0:T(8,128)(2,1)S(1)}, bf16[512,128]{1,0:T(8,128)(2,1)S(1)}, u32[]{:S(2)}, u32[]{:S(2)}) collective-permute-start(bf16[512,128]{1,0:T(8,128)(2,1)S(1)} %get-tuple-element.62), channel_id=1, source_target_pairs={{0,1},{1,0},{2,3},{3,2},{4,5},{5,4},{6,7},{7,6},{8,9},{9,8},{10,11... | collective-permute-start | bytes 393224 | tf_op jit(solution)/shard_map/ppermute | solution.py:427
  53.9 6.0 %copy-start.7 = (bf16[8,32,128]{2,1,0:T(8,128)(2,1)S(1)}, bf16[8,32,128]{2,1,0:T(8,128)(2,1)}, u32[]{:S(2)}) copy-start(bf16[8,32,128]{2,1,0:T(8,128)(2,1)} %copy-done.6) | copy-start | bytes 196612
  53.9 13.0 %collective-permute-start.5 = (bf16[16,32,128]{2,1,0:T(8,128)(2,1)S(1)}, bf16[16,32,128]{2,1,0:T(8,128)(2,1)S(1)}, u32[]{:S(2)}, u32[]{:S(2)}) collective-permute-start(bf16[16,32,128]{2,1,0:T(8,128)(2,1)S(1)} %pad_maximum_fusion), channel_id=1, source_target_pairs={{0,6},{1,7},{2,0},{3,1},{4,2},{5,3},{6,4},{7,5},{8,14},{9,15},{10,... | collective-permute-start | bytes 393224 | tf_op jit(solution)/shard_map/ppermute | solution.py:434
  61.1 10.9 %collective-permute-start.9 = (bf16[8,32,128]{2,1,0:T(8,128)(2,1)S(1)}, bf16[8,32,128]{2,1,0:T(8,128)(2,1)S(1)}, u32[]{:S(2)}, u32[]{:S(2)}) collective-permute-start(bf16[8,32,128]{2,1,0:T(8,128)(2,1)S(1)} %get-tuple-element.65), channel_id=1, source_target_pairs={{0,4},{1,5},{2,6},{3,7},{4,0},{5,1},{6,2},{7,3},{8,12},{9,13},{10,... | collective-permute-start | bytes 196616 | tf_op jit(solution)/shard_map/ppermute | solution.py:439
  63.3 8.8 %collective-permute-start.10 = (bf16[8,32,128]{2,1,0:T(8,128)(2,1)S(1)}, bf16[8,32,128]{2,1,0:T(8,128)(2,1)S(1)}, u32[]{:S(2)}, u32[]{:S(2)}) collective-permute-start(bf16[8,32,128]{2,1,0:T(8,128)(2,1)S(1)} %get-tuple-element.66), channel_id=1, source_target_pairs={{0,2},{1,3},{2,4},{3,5},{4,6},{5,7},{6,0},{7,1},{8,10},{9,11},{10,... | collective-permute-start | bytes 196616 | tf_op jit(solution)/shard_map/ppermute | solution.py:439
  64.5 7.6 %collective-permute-start.11 = (bf16[8,32,128]{2,1,0:T(8,128)(2,1)S(1)}, bf16[8,32,128]{2,1,0:T(8,128)(2,1)S(1)}, u32[]{:S(2)}, u32[]{:S(2)}) collective-permute-start(bf16[8,32,128]{2,1,0:T(8,128)(2,1)S(1)} %get-tuple-element.67), channel_id=1, source_target_pairs={{0,6},{1,7},{2,0},{3,1},{4,2},{5,3},{6,4},{7,5},{8,14},{9,15},{10,... | collective-permute-start | bytes 196616 | tf_op jit(solution)/shard_map/ppermute | solution.py:439
  66.9 7.6 %collective-permute-start.7 = (bf16[8,32,128]{2,1,0:T(8,128)(2,1)S(1)}, bf16[8,32,128]{2,1,0:T(8,128)(2,1)S(1)}, u32[]{:S(2)}, u32[]{:S(2)}) collective-permute-start(bf16[8,32,128]{2,1,0:T(8,128)(2,1)S(1)} %get-tuple-element.54), channel_id=1, source_target_pairs={{0,2},{1,3},{2,4},{3,5},{4,6},{5,7},{6,0},{7,1},{8,10},{9,11},{10,... | collective-permute-start | bytes 196616 | tf_op jit(solution)/shard_map/ppermute | solution.py:436
  66.9 7.6 %collective-permute-start.6 = (bf16[8,32,128]{2,1,0:T(8,128)(2,1)S(1)}, bf16[8,32,128]{2,1,0:T(8,128)(2,1)S(1)}, u32[]{:S(2)}, u32[]{:S(2)}) collective-permute-start(bf16[8,32,128]{2,1,0:T(8,128)(2,1)S(1)} %get-tuple-element.81), channel_id=1, source_target_pairs={{0,6},{1,7},{2,0},{3,1},{4,2},{5,3},{6,4},{7,5},{8,14},{9,15},{10,... | collective-permute-start | bytes 196616 | tf_op jit(solution)/shard_map/ppermute | solution.py:437
  76.8 1.0 copy-start.3
  77.8 25.3 %all-to-all-start.2 = ((bf16[32,128,128]{2,1,0:T(8,128)(2,1)}), bf16[32,128,128]{2,1,0:T(8,128)(2,1)S(1)}, u32[]{:S(2)}, u32[]{:S(2)}) async-start(bf16[32,128,128]{2,1,0:T(8,128)(2,1)} %copy-done.3), calls=%async_computation.2 | async-start | bytes 2097152 | tf_op jit(solution)/shard_map/all_to_all | solution.py:424
